TPU v7x, 256 devices: a whole 4x4x8 slice. The times are simulated.
256 devices in a mesh: ax: 128 (over z, x_lo, y, core), xs: 2 (over x_hi).
Axes of the slice: x: 4 (x_hi: 2, x_lo: 2; x = x_hi * 2 + x_lo), y: 4, z: 8, core: 2. Of those that a mesh axis runs over, the one named last changes fastest.
Arguments:
- displacement: float32 [3, 512, 16, 1536], P(None, 'ax', 'xs'), may hold values from -6 to 6
- previous: float32 [3, 512, 16, 1536], P(None, 'ax', 'xs'), may hold values from -6 to 6
- stiffness: float32 [512, 16, 1536], P('ax', 'xs'), may hold values from 0.5 to 2
- tissue_mask: int32 [512], P('ax'), may hold values 0 or 1
- compartment: int32 [16, 1536], P('xs'), may hold values from 0 to 3
- drive: float32 [3, 4], replicated, may hold values from -1 to 1
Outputs:
- fine_field: float32 [3, 512, 16, 1536], P(None, 'ax', 'xs')
- coarse_field: float32 [3, 256, 8, 768], P(None, 'ax', 'xs')
All inputs are finite; a program needn't handle non-finite values. No bound on the sum of `tissue_mask` on one device may be relied on, other than what follows from the above.
Results may differ from a plain program's by a relative error of at most 0.00011.
Values sent between devices are 32-bit elements; how exact they have to be, the bound alone decides.
No kernel may reach another device: no remote copies, remote signals or barrier semaphores. Data moves between devices by JAX's collectives and lax.ppermute only.
A program may use at most 192 MiB of HBM per device.

v0:
```python
import jax
import jax.numpy as jnp
from jax import lax
from jax.sharding import PartitionSpec as P

STEPS = 4


TIME_SQUARE = 0.12


def with_halo(cells, sides, width):
    for axis, dim in sides:
        count = lax.axis_size(axis)
        ends = count - 1
        head = lax.slice_in_dim(cells, 0, width, axis=dim)
        tail = lax.slice_in_dim(cells, cells.shape[dim] - width, cells.shape[dim], axis=dim)
        cells = jnp.concatenate(
            [
                lax.ppermute(tail, axis, [(i, (i + 1) % count) for i in range(ends)]),
                cells,
                lax.ppermute(head, axis, [((i + 1) % count, i) for i in range(ends)]),
            ],
            axis=dim,
        )
    return cells


def neighbour_windows():
    inner = slice(1, -1)
    return [
        (slice(2, None), inner, inner),
        (slice(0, -2), inner, inner),
        (inner, slice(2, None), inner),
        (inner, slice(0, -2), inner),
        (inner, inner, slice(2, None)),
        (inner, inner, slice(0, -2)),
    ]


def operate(padded, kpadded):
    inner = slice(1, -1)
    centre = padded[:, inner, inner, inner]
    stiff_mid = kpadded[inner, inner, inner]
    total = jnp.zeros_like(centre)
    for window in neighbour_windows():
        total = total + 0.5 * (stiff_mid + kpadded[window]) * (
            padded[(slice(None),) + window] - centre
        )
    return total


def make_force(tissue_mask, compartment, drive):
    groups = (
        compartment[None, :, :] == jnp.arange(drive.shape[1], dtype=jnp.int32)[:, None, None]
    ).astype(jnp.float32)
    per_cell = jnp.einsum("cg,gyx->cyx", drive, groups, precision=lax.Precision.HIGHEST)
    return per_cell[:, None, :, :] * tissue_mask.astype(jnp.float32)[None, :, None, None]


def restrict(field):
    shape = field.shape
    lead = shape[:-3]
    blocks = field.reshape(lead + (shape[-3] // 2, 2, shape[-2] // 2, 2, shape[-1] // 2, 2))
    return jnp.mean(blocks, axis=(-5, -3, -1))


def pad_field(field, depth_z, depth_y):
    return jnp.pad(field, ((0, 0), (depth_z, depth_z), (depth_y, depth_y), (1, 1)))


def pad_stiff(stiff, depth_z, depth_y):
    return jnp.pad(stiff, ((depth_z, depth_z), (depth_y, depth_y), (1, 1)))


def local(displacement, previous, stiffness, tissue_mask, compartment, drive):
    force = make_force(tissue_mask, compartment, drive)
    coarse_now = restrict(displacement)
    coarse_prev = restrict(previous)
    coarse_stiff = restrict(stiffness)
    coarse_force = restrict(force)
    kpadded = with_halo(coarse_stiff, (("ax", 0), ("xs", 1)), 1)
    kpadded = pad_stiff(kpadded, 0, 0)
    for repeat in range(STEPS):
        padded = with_halo(coarse_now, (("ax", 1), ("xs", 2)), 1)
        padded = pad_field(padded, 0, 0)
        fresh = (
            2.0 * coarse_now
            - coarse_prev
            + TIME_SQUARE * (0.25 * operate(padded, kpadded) + coarse_force)
        )
        coarse_prev = coarse_now
        coarse_now = fresh
    current = displacement
    earlier = previous
    kpadded = with_halo(stiffness, (("ax", 0), ("xs", 1)), 1)
    kpadded = pad_stiff(kpadded, 0, 0)
    for repeat in range(STEPS):
        padded = with_halo(current, (("ax", 1), ("xs", 2)), 1)
        padded = pad_field(padded, 0, 0)
        fresh = 2.0 * current - earlier + TIME_SQUARE * (operate(padded, kpadded) + force)
        earlier = current
        current = fresh
    return (current, coarse_now)


def solution(mesh):
    placed = (
        P(None, "ax", "xs", None),
        P(None, "ax", "xs", None),
        P("ax", "xs", None),
        P("ax"),
        P("xs", None),
        P(),
    )
    return jax.shard_map(
        local,
        mesh=mesh,
        in_specs=placed,
        out_specs=(P(None, "ax", "xs", None), P(None, "ax", "xs", None)),
        check_vma=False,
    )
```

profile of v0, /device:TPU:128, one launch (start us, length us, event | category | flops | bytes accessed | tf_op | source)
XLA Modules:
  0.0 343.6 jit_solution(9148185095521551545)
XLA Ops:
  11.2 15.3 %reshape.33 = f32[2,2,4,2,768,2]{5,4,3,2,1,0:T(8,128)} reshape(f32[4,8,1536]{2,1,0:T(8,128)} %param.8) | data formatting | bytes 393216 | tf_op jit(solution)/shard_map/reshape | solution.py:64
  26.4 5.6 %reduce_sum.38 = f32[2,4,768]{2,1,0:T(4,128)S(1)} reduce(f32[2,2,4,2,768,2]{5,4,3,2,1,0:T(8,128)} %reshape.33, f32[]{:T(128)} %constant.8.clone.1), dimensions={1,3,5}, to_apply=%region_2.0 | reduce | flops 43008 | bytes 221188 | tf_op jit(solution)/shard_map/reduce_sum | solution.py:65
  34.0 7.9 %collective-permute-start.20 = (f32[1,4,768]{2,1,0:T(4,128)S(1)}, f32[1,4,768]{2,1,0:T(4,128)S(1)}, u32[]{:S(2)}, u32[]{:S(2)}) collective-permute-start(f32[1,4,768]{2,1,0:T(4,128)S(1)} %get-tuple-element.61), channel_id=1, source_target_pairs={{2,0},{4,2},{6,4},{8,6},{10,8},{12,10},{14,12},{16,14},{18,16},{20... | collective-permute-start | bytes 36872 | tf_op jit(solution)/shard_map/ppermute | solution.py:22
  41.8 39.9 %reshape.31 = f32[3,2,2,4,2,768,2]{6,5,4,3,2,1,0:T(8,128)} reshape(f32[3,4,8,1536]{3,2,1,0:T(8,128)S(1)} %copy-done.2) | data formatting | bytes 1179648 | tf_op jit(solution)/shard_map/reshape | solution.py:64
  81.7 13.8 %reduce_sum.36 = f32[3,2,4,768]{3,2,1,0:T(4,128)S(1)} reduce(f32[3,2,2,4,2,768,2]{6,5,4,3,2,1,0:T(8,128)} %reshape.31, f32[]{:T(128)} %constant.8.clone.1), dimensions={2,4,6}, to_apply=%region_0.0 | reduce | flops 129024 | bytes 663556 | tf_op jit(solution)/shard_map/reduce_sum | solution.py:65
  95.9 11.1 %reshape.35 = f32[3,4,2,768,2]{4,3,0,2,1:T(8,128)} reshape(f32[3,8,1536]{2,0,1:T(4,128)S(1)} %convolution_bitcast_fusion) | data formatting | bytes 294912 | tf_op jit(solution)/shard_map/mul | solution.py:58
  107.1 5.6 %copy.120 = f32[3,4,2,768,2]{3,1,4,2,0:T(4,128)S(1)} copy(f32[3,4,2,768,2]{4,3,0,2,1:T(8,128)} %reshape.35) | data formatting | bytes 294912 | tf_op jit(solution)/shard_map/mul | solution.py:58
  119.5 39.9 %reshape.32 = f32[3,2,2,4,2,768,2]{6,5,4,3,2,1,0:T(8,128)} reshape(f32[3,4,8,1536]{3,2,1,0:T(8,128)S(1)} %copy-done.4) | data formatting | bytes 1179648 | tf_op jit(solution)/shard_map/reshape | solution.py:64
  159.3 13.8 %reduce_sum.37 = f32[3,2,4,768]{3,2,1,0:T(4,128)S(1)} reduce(f32[3,2,2,4,2,768,2]{6,5,4,3,2,1,0:T(8,128)} %reshape.32, f32[]{:T(128)} %constant.8.clone.1), dimensions={2,4,6}, to_apply=%region_1.0 | reduce | flops 129024 | bytes 663556 | tf_op jit(solution)/shard_map/reduce_sum | solution.py:65
  175.0 7.9 %collective-permute-start.21 = (f32[3,1,4,768]{3,2,1,0:T(4,128)S(1)}, f32[3,1,4,768]{3,2,1,0:T(4,128)S(1)}, u32[]{:S(2)}, u32[]{:S(2)}) collective-permute-start(f32[3,1,4,768]{3,2,1,0:T(4,128)S(1)} %get-tuple-element.53), channel_id=1, source_target_pairs={{2,0},{4,2},{6,4},{8,6},{10,8},{12,10},{14,12},{16,14},{18,16},{20... | collective-permute-start | bytes 110600 | tf_op jit(solution)/shard_map/ppermute | solution.py:22
  185.2 6.0 %collective-permute-start.27 = (f32[3,4,1,768]{3,2,1,0:T(1,128)S(1)}, f32[3,4,1,768]{3,2,1,0:T(1,128)S(1)}, u32[]{:S(2)}, u32[]{:S(2)}) collective-permute-start(f32[3,4,1,768]{3,2,1,0:T(1,128)S(1)} %get-tuple-element.42), channel_id=1, source_target_pairs={{0,1},{2,3},{4,5},{6,7},{8,9},{10,11},{12,13},{14,15},{16,17},{18,... | collective-permute-start | bytes 110600 | tf_op jit(solution)/shard_map/ppermute | solution.py:20
  192.7 6.1 %collective-permute-start.6 = (f32[6,1,1536]{2,1,0:T(1,128)S(1)}, f32[6,1,1536]{2,1,0:T(1,128)S(1)}, u32[]{:S(2)}, u32[]{:S(2)}) collective-permute-start(f32[6,1,1536]{2,1,0:T(1,128)S(1)} %get-tuple-element.28), channel_id=1, source_target_pairs={{0,1},{2,3},{4,5},{6,7},{8,9},{10,11},{12,13},{14,15},{16,17},{18,... | collective-permute-start | bytes 110600 | tf_op jit(solution)/shard_map/ppermute | solution.py:20
  202.6 7.9 %collective-permute-start.28 = (f32[3,1,4,768]{3,2,1,0:T(4,128)S(1)}, f32[3,1,4,768]{3,2,1,0:T(4,128)S(1)}, u32[]{:S(2)}, u32[]{:S(2)}) collective-permute-start(f32[3,1,4,768]{3,2,1,0:T(4,128)S(1)} %get-tuple-element.51), channel_id=1, source_target_pairs={{2,0},{4,2},{6,4},{8,6},{10,8},{12,10},{14,12},{16,14},{18,16},{20... | collective-permute-start | bytes 110600 | tf_op jit(solution)/shard_map/ppermute | solution.py:22
  212.2 6.1 %collective-permute-start.31 = (f32[3,4,1,768]{3,2,1,0:T(1,128)S(1)}, f32[3,4,1,768]{3,2,1,0:T(1,128)S(1)}, u32[]{:S(2)}, u32[]{:S(2)}) collective-permute-start(f32[3,4,1,768]{3,2,1,0:T(1,128)S(1)} %get-tuple-element.40), channel_id=1, source_target_pairs={{0,1},{2,3},{4,5},{6,7},{8,9},{10,11},{12,13},{14,15},{16,17},{18,... | collective-permute-start | bytes 110600 | tf_op jit(solution)/shard_map/ppermute | solution.py:20
  228.1 7.9 %collective-permute-start.32 = (f32[3,1,4,768]{3,2,1,0:T(4,128)S(1)}, f32[3,1,4,768]{3,2,1,0:T(4,128)S(1)}, u32[]{:S(2)}, u32[]{:S(2)}) collective-permute-start(f32[3,1,4,768]{3,2,1,0:T(4,128)S(1)} %get-tuple-element.49), channel_id=1, source_target_pairs={{2,0},{4,2},{6,4},{8,6},{10,8},{12,10},{14,12},{16,14},{18,16},{20... | collective-permute-start | bytes 110600 | tf_op jit(solution)/shard_map/ppermute | solution.py:22
  239.4 6.1 %collective-permute-start.35 = (f32[3,4,1,768]{3,2,1,0:T(1,128)S(1)}, f32[3,4,1,768]{3,2,1,0:T(1,128)S(1)}, u32[]{:S(2)}, u32[]{:S(2)}) collective-permute-start(f32[3,4,1,768]{3,2,1,0:T(1,128)S(1)} %get-tuple-element.38), channel_id=1, source_target_pairs={{0,1},{2,3},{4,5},{6,7},{8,9},{10,11},{12,13},{14,15},{16,17},{18,... | collective-permute-start | bytes 110600 | tf_op jit(solution)/shard_map/ppermute | solution.py:20
  255.9 7.8 %collective-permute-done.9 = f32[3,1,8,1536]{3,2,1,0:T(8,128)S(1)} collective-permute-done((f32[3,1,8,1536]{3,2,1,0:T(8,128)S(1)}, f32[3,1,8,1536]{3,2,1,0:T(8,128)S(1)}, u32[]{:S(2)}, u32[]{:S(2)}) %collective-permute-start.9) | collective-permute-done | bytes 147488 | tf_op jit(solution)/shard_map/ppermute | solution.py:20
  264.0 5.8 %collective-permute-start.11 = (f32[3,6,1,1536]{3,1,2,0:T(8,128)S(1)}, f32[3,6,1,1536]{3,1,2,0:T(8,128)S(1)}, u32[]{:S(2)}, u32[]{:S(2)}) collective-permute-start(f32[3,6,1,1536]{3,1,2,0:T(8,128)S(1)} %get-tuple-element.12), channel_id=1, source_target_pairs={{0,1},{2,3},{4,5},{6,7},{8,9},{10,11},{12,13},{14,15},{16,17},{18,... | collective-permute-start | bytes 331784 | tf_op jit(solution)/shard_map/ppermute | solution.py:20
  272.5 5.9 %collective-permute-done.10 = f32[3,6,1,1536]{3,1,2,0:T(8,128)S(1)} collective-permute-done((f32[3,6,1,1536]{3,1,2,0:T(8,128)S(1)}, f32[3,6,1,1536]{3,1,2,0:T(8,128)S(1)}, u32[]{:S(2)}, u32[]{:S(2)}) %collective-permute-start.10) | collective-permute-done | bytes 110624 | tf_op jit(solution)/shard_map/ppermute | solution.py:22
  288.7 7.9 %collective-permute-start.36 = (f32[3,1,4,768]{3,2,1,0:T(4,128)S(1)}, f32[3,1,4,768]{3,2,1,0:T(4,128)S(1)}, u32[]{:S(2)}, u32[]{:S(2)}) collective-permute-start(f32[3,1,4,768]{3,2,1,0:T(4,128)S(1)} %get-tuple-element.47), channel_id=1, source_target_pairs={{2,0},{4,2},{6,4},{8,6},{10,8},{12,10},{14,12},{16,14},{18,16},{20... | collective-permute-start | bytes 110600 | tf_op jit(solution)/shard_map/ppermute | solution.py:22
  299.9 6.1 %collective-permute-start.39 = (f32[3,4,1,768]{3,2,1,0:T(1,128)S(1)}, f32[3,4,1,768]{3,2,1,0:T(1,128)S(1)}, u32[]{:S(2)}, u32[]{:S(2)}) collective-permute-start(f32[3,4,1,768]{3,2,1,0:T(1,128)S(1)} %get-tuple-element.36), channel_id=1, source_target_pairs={{0,1},{2,3},{4,5},{6,7},{8,9},{10,11},{12,13},{14,15},{16,17},{18,... | collective-permute-start | bytes 110600 | tf_op jit(solution)/shard_map/ppermute | solution.py:20
  316.3 7.8 %collective-permute-done.17 = f32[3,1,8,1536]{3,2,1,0:T(8,128)S(1)} collective-permute-done((f32[3,1,8,1536]{3,2,1,0:T(8,128)S(1)}, f32[3,1,8,1536]{3,2,1,0:T(8,128)S(1)}, u32[]{:S(2)}, u32[]{:S(2)}) %collective-permute-start.17) | collective-permute-done | bytes 147488 | tf_op jit(solution)/shard_map/ppermute | solution.py:20
  324.4 6.1 %collective-permute-start.19 = (f32[3,6,1,1536]{3,1,2,0:T(8,128)S(1)}, f32[3,6,1,1536]{3,1,2,0:T(8,128)S(1)}, u32[]{:S(2)}, u32[]{:S(2)}) collective-permute-start(f32[3,6,1,1536]{3,1,2,0:T(8,128)S(1)} %get-tuple-element.8), channel_id=1, source_target_pairs={{0,1},{2,3},{4,5},{6,7},{8,9},{10,11},{12,13},{14,15},{16,17},{18,... | collective-permute-start | bytes 331784 | tf_op jit(solution)/shard_map/ppermute | solution.py:20
  333.1 5.9 %collective-permute-done.18 = f32[3,6,1,1536]{3,1,2,0:T(8,128)S(1)} collective-permute-done((f32[3,6,1,1536]{3,1,2,0:T(8,128)S(1)}, f32[3,6,1,1536]{3,1,2,0:T(8,128)S(1)}, u32[]{:S(2)}, u32[]{:S(2)}) %collective-permute-start.18) | collective-permute-done | bytes 110624 | tf_op jit(solution)/shard_map/ppermute | solution.py:22
  (150 shorter events, 88.2 us)
Async XLA Ops:
  1.5 191.2 %collective-permute-start = (f32[1,8,1536]{2,1,0:T(8,128)S(1)}, f32[1,8,1536]{2,1,0:T(8,128)S(1)}, u32[]{:S(2)}, u32[]{:S(2)}) collective-permute-start(f32[1,8,1536]{2,1,0:T(8,128)S(1)} %get-tuple-element.34), channel_id=1, source_target_pairs={{2,0},{4,2},{6,4},{8,6},{10,8},{12,10},{14,12},{16,14},{18,16},{20... | collective-permute-start | bytes 147464 | tf_op jit(solution)/shard_map/ppermute | solution.py:22
  6.3 185.0 %collective-permute-start.2 = (f32[1,8,1536]{2,1,0:T(8,128)S(1)}, f32[1,8,1536]{2,1,0:T(8,128)S(1)}, u32[]{:S(2)}, u32[]{:S(2)}) collective-permute-start(f32[1,8,1536]{2,1,0:T(8,128)S(1)} %get-tuple-element.35), channel_id=1, source_target_pairs={{0,2},{2,4},{4,6},{6,8},{8,10},{10,12},{12,14},{14,16},{16,18},{18... | collective-permute-start | bytes 147464 | tf_op jit(solution)/shard_map/ppermute | solution.py:20
  9.3 226.7 %collective-permute-start.3 = (f32[3,1,8,1536]{3,2,1,0:T(8,128)S(1)}, f32[3,1,8,1536]{3,2,1,0:T(8,128)S(1)}, u32[]{:S(2)}, u32[]{:S(2)}) collective-permute-start(f32[3,1,8,1536]{3,2,1,0:T(8,128)S(1)} %get-tuple-element.24), channel_id=1, source_target_pairs={{0,2},{2,4},{4,6},{6,8},{8,10},{10,12},{12,14},{14,16},{16,18},{18... | collective-permute-start | bytes 442376 | tf_op jit(solution)/shard_map/ppermute | solution.py:20
  32.0 80.6 %collective-permute-start.22 = (f32[1,4,768]{2,1,0:T(4,128)S(1)}, f32[1,4,768]{2,1,0:T(4,128)S(1)}, u32[]{:S(2)}, u32[]{:S(2)}) collective-permute-start(f32[1,4,768]{2,1,0:T(4,128)S(1)} %get-tuple-element.60), channel_id=1, source_target_pairs={{0,2},{2,4},{4,6},{6,8},{8,10},{10,12},{12,14},{14,16},{16,18},{18... | collective-permute-start | bytes 36872 | tf_op jit(solution)/shard_map/ppermute | solution.py:20
  34.0 78.7 %collective-permute-start.20 = (f32[1,4,768]{2,1,0:T(4,128)S(1)}, f32[1,4,768]{2,1,0:T(4,128)S(1)}, u32[]{:S(2)}, u32[]{:S(2)}) collective-permute-start(f32[1,4,768]{2,1,0:T(4,128)S(1)} %get-tuple-element.61), channel_id=1, source_target_pairs={{2,0},{4,2},{6,4},{8,6},{10,8},{12,10},{14,12},{16,14},{18,16},{20... | collective-permute-start | bytes 36872 | tf_op jit(solution)/shard_map/ppermute | solution.py:22
  112.7 60.4 %collective-permute-start.26 = (f32[4,1,768]{2,1,0:T(1,128)S(1)}, f32[4,1,768]{2,1,0:T(1,128)S(1)}, u32[]{:S(2)}, u32[]{:S(2)}) collective-permute-start(f32[4,1,768]{2,1,0:T(1,128)S(1)} %get-tuple-element.56), channel_id=1, source_target_pairs={{0,1},{2,3},{4,5},{6,7},{8,9},{10,11},{12,13},{14,15},{16,17},{18,... | collective-permute-start | bytes 36872 | tf_op jit(solution)/shard_map/ppermute | solution.py:20
  117.5 57.5 %collective-permute-start.24 = (f32[4,1,768]{2,1,0:T(1,128)S(1)}, f32[4,1,768]{2,1,0:T(1,128)S(1)}, u32[]{:S(2)}, u32[]{:S(2)}) collective-permute-start(f32[4,1,768]{2,1,0:T(1,128)S(1)} %get-tuple-element.57), channel_id=1, source_target_pairs={{1,0},{3,2},{5,4},{7,6},{9,8},{11,10},{13,12},{15,14},{17,16},{19,... | collective-permute-start | bytes 36872 | tf_op jit(solution)/shard_map/ppermute | solution.py:22
  173.1 10.1 %collective-permute-start.23 = (f32[3,1,4,768]{3,2,1,0:T(4,128)S(1)}, f32[3,1,4,768]{3,2,1,0:T(4,128)S(1)}, u32[]{:S(2)}, u32[]{:S(2)}) collective-permute-start(f32[3,1,4,768]{3,2,1,0:T(4,128)S(1)} %get-tuple-element.52), channel_id=1, source_target_pairs={{0,2},{2,4},{4,6},{6,8},{8,10},{10,12},{12,14},{14,16},{16,18},{18... | collective-permute-start | bytes 110600 | tf_op jit(solution)/shard_map/ppermute | solution.py:20
  183.2 52.9 %collective-permute-start.1 = (f32[3,1,8,1536]{3,2,1,0:T(8,128)S(1)}, f32[3,1,8,1536]{3,2,1,0:T(8,128)S(1)}, u32[]{:S(2)}, u32[]{:S(2)}) collective-permute-start(f32[3,1,8,1536]{3,2,1,0:T(8,128)S(1)} %get-tuple-element.25), channel_id=1, source_target_pairs={{2,0},{4,2},{6,4},{8,6},{10,8},{12,10},{14,12},{16,14},{18,16},{20... | collective-permute-start | bytes 442376 | tf_op jit(solution)/shard_map/ppermute | solution.py:22
  185.2 13.6 %collective-permute-start.27 = (f32[3,4,1,768]{3,2,1,0:T(1,128)S(1)}, f32[3,4,1,768]{3,2,1,0:T(1,128)S(1)}, u32[]{:S(2)}, u32[]{:S(2)}) collective-permute-start(f32[3,4,1,768]{3,2,1,0:T(1,128)S(1)} %get-tuple-element.42), channel_id=1, source_target_pairs={{0,1},{2,3},{4,5},{6,7},{8,9},{10,11},{12,13},{14,15},{16,17},{18,... | collective-permute-start | bytes 110600 | tf_op jit(solution)/shard_map/ppermute | solution.py:20
  198.8 11.7 %collective-permute-start.4 = (f32[6,1,1536]{2,1,0:T(1,128)S(1)}, f32[6,1,1536]{2,1,0:T(1,128)S(1)}, u32[]{:S(2)}, u32[]{:S(2)}) collective-permute-start(f32[6,1,1536]{2,1,0:T(1,128)S(1)} %get-tuple-element.29), channel_id=1, source_target_pairs={{1,0},{3,2},{5,4},{7,6},{9,8},{11,10},{13,12},{15,14},{17,16},{19,... | collective-permute-start | bytes 110600 | tf_op jit(solution)/shard_map/ppermute | solution.py:22
  200.7 10.2 %collective-permute-start.29 = (f32[3,1,4,768]{3,2,1,0:T(4,128)S(1)}, f32[3,1,4,768]{3,2,1,0:T(4,128)S(1)}, u32[]{:S(2)}, u32[]{:S(2)}) collective-permute-start(f32[3,1,4,768]{3,2,1,0:T(4,128)S(1)} %get-tuple-element.50), channel_id=1, source_target_pairs={{0,2},{2,4},{4,6},{6,8},{8,10},{10,12},{12,14},{14,16},{16,18},{18... | collective-permute-start | bytes 110600 | tf_op jit(solution)/shard_map/ppermute | solution.py:20
  226.2 13.2 %collective-permute-start.33 = (f32[3,1,4,768]{3,2,1,0:T(4,128)S(1)}, f32[3,1,4,768]{3,2,1,0:T(4,128)S(1)}, u32[]{:S(2)}, u32[]{:S(2)}) collective-permute-start(f32[3,1,4,768]{3,2,1,0:T(4,128)S(1)} %get-tuple-element.48), channel_id=1, source_target_pairs={{0,2},{2,4},{4,6},{6,8},{8,10},{10,12},{12,14},{14,16},{16,18},{18... | collective-permute-start | bytes 110600 | tf_op jit(solution)/shard_map/ppermute | solution.py:20
  228.1 11.3 %collective-permute-start.32 = (f32[3,1,4,768]{3,2,1,0:T(4,128)S(1)}, f32[3,1,4,768]{3,2,1,0:T(4,128)S(1)}, u32[]{:S(2)}, u32[]{:S(2)}) collective-permute-start(f32[3,1,4,768]{3,2,1,0:T(4,128)S(1)} %get-tuple-element.49), channel_id=1, source_target_pairs={{2,0},{4,2},{6,4},{8,6},{10,8},{12,10},{14,12},{16,14},{18,16},{20... | collective-permute-start | bytes 110600 | tf_op jit(solution)/shard_map/ppermute | solution.py:22
  236.4 10.4 %collective-permute-start.7 = (f32[3,6,1,1536]{3,1,2,0:T(8,128)S(1)}, f32[3,6,1,1536]{3,1,2,0:T(8,128)S(1)}, u32[]{:S(2)}, u32[]{:S(2)}) collective-permute-start(f32[3,6,1,1536]{3,1,2,0:T(8,128)S(1)} %get-tuple-element.14), channel_id=1, source_target_pairs={{0,1},{2,3},{4,5},{6,7},{8,9},{10,11},{12,13},{14,15},{16,17},{18,... | collective-permute-start | bytes 331784 | tf_op jit(solution)/shard_map/ppermute | solution.py:20
  239.4 15.9 %collective-permute-start.35 = (f32[3,4,1,768]{3,2,1,0:T(1,128)S(1)}, f32[3,4,1,768]{3,2,1,0:T(1,128)S(1)}, u32[]{:S(2)}, u32[]{:S(2)}) collective-permute-start(f32[3,4,1,768]{3,2,1,0:T(1,128)S(1)} %get-tuple-element.38), channel_id=1, source_target_pairs={{0,1},{2,3},{4,5},{6,7},{8,9},{10,11},{12,13},{14,15},{16,17},{18,... | collective-permute-start | bytes 110600 | tf_op jit(solution)/shard_map/ppermute | solution.py:20
  253.0 10.8 %collective-permute-start.9 = (f32[3,1,8,1536]{3,2,1,0:T(8,128)S(1)}, f32[3,1,8,1536]{3,2,1,0:T(8,128)S(1)}, u32[]{:S(2)}, u32[]{:S(2)}) collective-permute-start(f32[3,1,8,1536]{3,2,1,0:T(8,128)S(1)} %copy.103), channel_id=1, source_target_pairs={{0,2},{2,4},{4,6},{6,8},{8,10},{10,12},{12,14},{14,16},{16,18},{18... | collective-permute-start | bytes 442376 | tf_op jit(solution)/shard_map/ppermute | solution.py:20
  282.4 14.2 %collective-permute-start.12 = (f32[3,1,8,1536]{3,2,1,0:T(8,128)S(1)}, f32[3,1,8,1536]{3,2,1,0:T(8,128)S(1)}, u32[]{:S(2)}, u32[]{:S(2)}) collective-permute-start(f32[3,1,8,1536]{3,2,1,0:T(8,128)S(1)} %copy.107), channel_id=1, source_target_pairs={{2,0},{4,2},{6,4},{8,6},{10,8},{12,10},{14,12},{16,14},{18,16},{20... | collective-permute-start | bytes 442376 | tf_op jit(solution)/shard_map/ppermute | solution.py:22
  284.3 12.4 %collective-permute-start.13 = (f32[3,1,8,1536]{3,2,1,0:T(8,128)S(1)}, f32[3,1,8,1536]{3,2,1,0:T(8,128)S(1)}, u32[]{:S(2)}, u32[]{:S(2)}) collective-permute-start(f32[3,1,8,1536]{3,2,1,0:T(8,128)S(1)} %copy.109), channel_id=1, source_target_pairs={{0,2},{2,4},{4,6},{6,8},{8,10},{10,12},{12,14},{14,16},{16,18},{18... | collective-permute-start | bytes 442376 | tf_op jit(solution)/shard_map/ppermute | solution.py:20
  286.8 13.0 %collective-permute-start.37 = (f32[3,1,4,768]{3,2,1,0:T(4,128)S(1)}, f32[3,1,4,768]{3,2,1,0:T(4,128)S(1)}, u32[]{:S(2)}, u32[]{:S(2)}) collective-permute-start(f32[3,1,4,768]{3,2,1,0:T(4,128)S(1)} %get-tuple-element.46), channel_id=1, source_target_pairs={{0,2},{2,4},{4,6},{6,8},{8,10},{10,12},{12,14},{14,16},{16,18},{18... | collective-permute-start | bytes 110600 | tf_op jit(solution)/shard_map/ppermute | solution.py:20
  288.7 11.1 %collective-permute-start.36 = (f32[3,1,4,768]{3,2,1,0:T(4,128)S(1)}, f32[3,1,4,768]{3,2,1,0:T(4,128)S(1)}, u32[]{:S(2)}, u32[]{:S(2)}) collective-permute-start(f32[3,1,4,768]{3,2,1,0:T(4,128)S(1)} %get-tuple-element.47), channel_id=1, source_target_pairs={{2,0},{4,2},{6,4},{8,6},{10,8},{12,10},{14,12},{16,14},{18,16},{20... | collective-permute-start | bytes 110600 | tf_op jit(solution)/shard_map/ppermute | solution.py:22
  297.0 10.5 %collective-permute-start.15 = (f32[3,6,1,1536]{3,1,2,0:T(8,128)S(1)}, f32[3,6,1,1536]{3,1,2,0:T(8,128)S(1)}, u32[]{:S(2)}, u32[]{:S(2)}) collective-permute-start(f32[3,6,1,1536]{3,1,2,0:T(8,128)S(1)} %get-tuple-element.10), channel_id=1, source_target_pairs={{0,1},{2,3},{4,5},{6,7},{8,9},{10,11},{12,13},{14,15},{16,17},{18,... | collective-permute-start | bytes 331784 | tf_op jit(solution)/shard_map/ppermute | solution.py:20
  299.9 15.9 %collective-permute-start.39 = (f32[3,4,1,768]{3,2,1,0:T(1,128)S(1)}, f32[3,4,1,768]{3,2,1,0:T(1,128)S(1)}, u32[]{:S(2)}, u32[]{:S(2)}) collective-permute-start(f32[3,4,1,768]{3,2,1,0:T(1,128)S(1)} %get-tuple-element.36), channel_id=1, source_target_pairs={{0,1},{2,3},{4,5},{6,7},{8,9},{10,11},{12,13},{14,15},{16,17},{18,... | collective-permute-start | bytes 110600 | tf_op jit(solution)/shard_map/ppermute | solution.py:20
  313.3 10.8 %collective-permute-start.17 = (f32[3,1,8,1536]{3,2,1,0:T(8,128)S(1)}, f32[3,1,8,1536]{3,2,1,0:T(8,128)S(1)}, u32[]{:S(2)}, u32[]{:S(2)}) collective-permute-start(f32[3,1,8,1536]{3,2,1,0:T(8,128)S(1)} %copy.115), channel_id=1, source_target_pairs={{0,2},{2,4},{4,6},{6,8},{8,10},{10,12},{12,14},{14,16},{16,18},{18... | collective-permute-start | bytes 442376 | tf_op jit(solution)/shard_map/ppermute | solution.py:20
  (23 other events, 317.0 us)
where the time goes:
time: 345 us; the launch traced here: 344 us
  starting transfers between devices  136 us (39%)
  local copies, waits for them, and re-layouts  118 us (34%)
  other arithmetic  52.5 us (15%)
  waiting for transfers between devices  35.5 us (10%)
    reshape x3, local copies, waits for them, and re-layouts, restrict(): field.reshape(lead + (shape[-3] // 2, 2, shape[-2] // 2, 2, shape[-1] //...  95 us
    ppermute x20, starting transfers between devices, with_halo(): lax.ppermute(tail, axis, [(i, (i + 1) % count) for i in range(ends)])  70.6 us
    ppermute x20, starting transfers between devices, with_halo(): lax.ppermute(head, axis, [((i + 1) % count, i) for i in range(ends)])  65 us
    reduce_sum x4, other arithmetic, restrict(): return jnp.mean(blocks, axis=(-5, -3, -1))  33.3 us
    ppermute x20, waiting for transfers between devices, with_halo(): lax.ppermute(head, axis, [((i + 1) % count, i) for i in range(ends)])  18.2 us
    ppermute x20, waiting for transfers between devices, with_halo(): lax.ppermute(tail, axis, [(i, (i + 1) % count) for i in range(ends)])  17.3 us
    mul x3, local copies, waits for them, and re-layouts, make_force(): per_cell[:, None, :, :]  16.8 us
    add x4, other arithmetic, local(): 2.0 * current - earlier + TIME_SQUARE * (operate(padded, kpadded) + force)  9.77 us
  transfers between devices with their start and end apart: 40, of which 9 were waited for; matrix products, arithmetic and copies ran while one was open for 47% of the time, Pallas kernels for 0%

commit v1 on v0

v1 whole, which is shorter than its diff:
```python
import functools

import jax
import jax.numpy as jnp
from jax import lax
from jax.experimental import pallas as pl
from jax.experimental.pallas import tpu as pltpu
from jax.sharding import PartitionSpec as P

TIME_SQUARE = 0.12
FINE_FACE = 0.5 * TIME_SQUARE
COARSE_FACE = 0.25 * 0.5 * TIME_SQUARE
PLANES = 4
ROWS = 8
FIELDS = 3
F32 = jnp.float32


def roll(x, shift, axis):
    return pltpu.roll(x, shift % x.shape[axis], axis)


def place():
    i = lax.axis_index("ax")
    s = lax.axis_index("xs")
    return (lax.rem(i, 2) == 1), (s == 0), (i > 0), (i < lax.axis_size("ax") - 1)


def iota(shape, dim):
    return lax.broadcasted_iota(jnp.int32, shape, dim)


def stiff_coefs(k, face, low_y, high_y, outer_row):
    width = k.shape[1]
    lane = iota(k.shape, 1)
    last = lane == width - 1
    start = lane == 0
    kp = jnp.where(last, 0.0, roll(k, -1, 1))
    km = jnp.where(start, 0.0, roll(k, 1, 1))
    full_p = face * (k + kp)
    full_m = face * (k + km)
    cyp = jnp.where(high_y, face * (k + roll(k, -1, 0)), 0.0)
    cym = jnp.where(low_y, face * (k + roll(k, 1, 0)), 0.0)
    edge = jnp.where(outer_row, face * k, 0.0)
    centre = 2.0 - (full_p + full_m + cyp + cym + edge)
    return jnp.where(last, 0.0, full_p), jnp.where(start, 0.0, full_m), cyp, cym, centre


def fine_coefs(k_ref, first, coef):
    shape = k_ref.shape[1:]
    row = iota(shape, 0)
    for z in range(PLANES - 1):
        coef[5, z] = FINE_FACE * (k_ref[z] + k_ref[z + 1])
    for z in range(PLANES):
        cxp, cxm, cyp, cym, centre = stiff_coefs(
            k_ref[z], FINE_FACE, row > 0, row < ROWS - 1, row == jnp.where(first, 0, ROWS - 1)
        )
        if z > 0:
            centre = centre - coef[5, z - 1]
        if z < PLANES - 1:
            centre = centre - coef[5, z]
        coef[0, z] = cxp
        coef[1, z] = cxm
        coef[2, z] = cyp
        coef[3, z] = cym
        coef[4, z] = centre


def fine_free(u_ref, before, c, z, coef, drive_term):
    u = u_ref[c, z]
    acc = coef[4, z] * u - before
    acc = acc + coef[0, z] * roll(u, -1, 1) + coef[1, z] * roll(u, 1, 1)
    acc = acc + coef[2, z] * roll(u, -1, 0) + coef[3, z] * roll(u, 1, 0)
    if z > 0:
        acc = acc + coef[5, z - 1] * u_ref[c, z - 1]
    if z < PLANES - 1:
        acc = acc + coef[5, z] * u_ref[c, z + 1]
    return acc + drive_term


def coarse_coefs(k, first):
    row = iota(k.shape, 0)
    inner = lax.rem(row, 4)
    cxp, cxm, cyp, cym, centre = stiff_coefs(
        k, COARSE_FACE, inner > 0, inner < 3, inner == jnp.where(first, 0, 3)
    )
    cz = COARSE_FACE * (k + roll(k, 4, 0))
    return cxp, cxm, cyp, cym, centre - cz, cz


def coarse_free(u, before, coefs, force):
    cxp, cxm, cyp, cym, centre, cz = coefs
    return (
        centre * u
        - before
        + cxp * roll(u, -1, 1)
        + cxm * roll(u, 1, 1)
        + cyp * roll(u, -1, 0)
        + cym * roll(u, 1, 0)
        + cz * roll(u, 4, 0)
        + force
    )


def group_drive(compartment, drive_ref, c):
    value = jnp.full(compartment.shape, drive_ref[c, 0], F32)
    for g in range(1, drive_ref.shape[1]):
        value = jnp.where(compartment == g, drive_ref[c, g], value)
    return value


def fine_row(r, width):
    if r < 24:
        return [(r % 8, (r // 8) * width, width)]
    half = width // 2
    return [(2 * (r - 24) + h, 3 * width, half) for h in range(2)]


def coarse_row(q, width, base):
    half = width // 2
    return [(q % 8, base + (q // 8) * half, half)]


def corner_fine(f, width):
    half = width // 2
    return [(2 * f + h, 0, half) for h in range(2)]


def corner_coarse(f, width):
    quarter = width // 4
    return [(2 * f + h, width // 2, quarter) for h in range(2)]


def put(buf, pieces, line):
    at = 0
    for row, lane, lanes in pieces:
        buf[row : row + 1, lane : lane + lanes] = line[:, at : at + lanes]
        at += lanes


def take(buf, pieces):
    parts = [buf[row : row + 1, lane : lane + lanes] for row, lane, lanes in pieces]
    return parts[0] if len(parts) == 1 else jnp.concatenate(parts, axis=1)


def spread(line, rows=ROWS):
    return jnp.broadcast_to(line, (rows, line.shape[1]))


def edge_line(tile, top_half, base=0, rows=ROWS):
    return jnp.where(top_half, tile[base + rows - 1 : base + rows], tile[base : base + 1])


def pack(odd, top_half, fine, coarse, stiff, coarse_stiff, a_buf, b_buf, y_buf, da_buf, db_buf, width):
    half = width // 2
    quarter = width // 4
    with_k = stiff is not None
    fields = 7 if with_k else 6
    zero = jnp.zeros((2, half), F32)
    upper = iota((ROWS, half), 0) < 4

    def tile(f, z):
        return fine(f, z) if f < 6 else stiff(z)

    base = 3 * width + (half if with_k else 0)
    for f in range(fields):
        for z in range(PLANES):
            t = tile(f, z)
            line = edge_line(t, top_half)
            put(y_buf, fine_row(f * PLANES + z, width), line)
            if z == 0:
                low, low_line = t, line
        a_buf[:, f * width : (f + 1) * width] = jnp.where(odd, low, t)
        b_buf[:, f * width : (f + 1) * width] = jnp.where(odd, t, low)
        g = f if f < 3 else (3 if f == 6 else None)
        if g is not None:
            put(da_buf, corner_fine(g, width), jnp.where(odd, low_line, line))
            put(db_buf, corner_fine(g, width), jnp.where(odd, line, low_line))

    for f in range(fields):
        t = coarse(f) if f < 6 else coarse_stiff
        lines = [edge_line(t, top_half, 4 * zc, 4) for zc in range(2)]
        for zc in range(2):
            put(y_buf, coarse_row(2 * f + zc, width, base), lines[zc])
        g = f if f < 3 else (3 if f == 6 else None)
        if g is not None:
            put(da_buf, corner_coarse(g, width), jnp.where(odd, lines[0], lines[1]))
            put(db_buf, corner_coarse(g, width), jnp.where(odd, lines[1], lines[0]))
    if with_k:
        y_buf[6:8, base + half : base + 2 * half] = zero
    else:
        y_buf[4:8, base + half : base + 2 * half] = jnp.zeros((4, half), F32)
        da_buf[6:8, :] = jnp.zeros((2, da_buf.shape[1]), F32)
        db_buf[6:8, :] = jnp.zeros((2, db_buf.shape[1]), F32)

    at = fields * width
    for c in range(FIELDS):
        first, second = coarse(c), coarse(c + 3)
        low = jnp.where(upper, first, roll(second, 4, 0))
        high = jnp.where(upper, roll(first, 4, 0), second)
        a_buf[:, at : at + half] = jnp.where(odd, low, high)
        b_buf[:, at : at + half] = jnp.where(odd, high, low)
        at += half
    if with_k:
        some = iota((ROWS, quarter), 0) < 4
        low, high = coarse_stiff, roll(coarse_stiff, 4, 0)
        low = jnp.where(some, low[:, :quarter], roll(low[:, quarter:], 4, 0))
        high = jnp.where(some, high[:, :quarter], roll(high[:, quarter:], 4, 0))
        a_buf[:, at : at + quarter] = jnp.where(odd, low, high)
        b_buf[:, at : at + quarter] = jnp.where(odd, high, low)


def begin_kernel(
    mask, drive, comp, stiff, now, before,
    w_out, cu_out, cw_out, ck_out, cf_out, a_buf, b_buf, y_buf, da_buf, db_buf,
    coef, group, wide,
):
    odd, top_half, _, _ = place()
    width = stiff.shape[2]
    half = width // 2
    row = iota((ROWS, width), 0)
    even_row = lax.rem(row, 2) == 0

    for c in range(FIELDS):
        group[c] = group_drive(comp[...], drive, c)

    def pooled(first, second):
        first = first + roll(first, -1, 0)
        second = second + roll(second, -1, 0)
        return jnp.where(even_row, first, roll(second, 1, 0))

    tiles = []
    for c in range(FIELDS):
        tiles.append(pooled(now[c, 0] + now[c, 1], now[c, 2] + now[c, 3]))
    for c in range(FIELDS):
        tiles.append(pooled(before[c, 0] + before[c, 1], before[c, 2] + before[c, 3]))
    tiles.append(pooled(stiff[0] + stiff[1], stiff[2] + stiff[3]))
    for c in range(FIELDS):
        tiles.append(pooled(group[c], group[c]))
    stacked = jnp.concatenate(tiles, axis=0)
    pool = jnp.where(iota((256, 128), 0) // 2 == iota((256, 128), 1), 0.125, 0.0)
    for q in range(width // 256):
        wide[q] = lax.dot_general(
            stacked[:, q * 256 : (q + 1) * 256], pool, (((1,), (0,)), ((), ())),
            precision=lax.Precision.HIGHEST, preferred_element_type=F32,
        )

    def coarse_tile(f):
        planes = [
            jnp.concatenate([wide[q, pl.ds(8 * f + zc, 4, stride=2), :] for q in range(half // 128)], axis=1)
            for zc in range(2)
        ]
        return jnp.concatenate(planes, axis=0)

    on = [mask[z].astype(F32) for z in range(PLANES)]
    upper = iota((ROWS, half), 0) < 4
    weight = jnp.where(upper, on[0] + on[1], on[2] + on[3]) * TIME_SQUARE
    ck_out[...] = coarse_tile(6)
    coefs = coarse_coefs(ck_out[...], top_half)
    for c in range(FIELDS):
        cu_out[c] = coarse_tile(c)
        cf_out[c] = coarse_tile(7 + c) * weight
        cw_out[c] = coarse_free(cu_out[c], coarse_tile(3 + c), coefs, cf_out[c])

    fine_coefs(stiff, top_half, coef)
    for c in range(FIELDS):
        for z in range(PLANES):
            w_out[c, z] = fine_free(
                now, before[c, z], c, z, coef, group[c] * (TIME_SQUARE * on[z])
            )
    pack(
        odd, top_half,
        lambda f, z: now[f, z] if f < 3 else w_out[f - 3, z],
        lambda f: cu_out[f] if f < 3 else cw_out[f - 3],
        lambda z: stiff[z], ck_out[...],
        a_buf, b_buf, y_buf, da_buf, db_buf, width,
    )


def join(
    round_one, round_two, mask, drive, comp, stiff, now, free, cu_now, cu_free, ck, cf,
    mid, mid_y, mid_low, mid_high, coef, halo, group, emit, emit_coarse, coarse_mid,
):
    odd, top_half, has_low, has_high = place()
    width = stiff.shape[2]
    half = width // 2
    quarter = width // 4
    a_one, b_one, y_one, da_one, db_one = round_one
    a_two, b_two, y_two, da_two, db_two = round_two
    row = iota((ROWS, width), 0)
    edge_row = row == jnp.where(top_half, ROWS - 1, 0)

    def low_of(a, b, at, lanes=width):
        return jnp.where(odd, a[:, at : at + lanes], b[:, at : at + lanes])

    def high_of(a, b, at, lanes=width):
        return jnp.where(odd, b[:, at : at + lanes], a[:, at : at + lanes])

    def corner(a, b, pieces):
        first, second = take(a, pieces), take(b, pieces)
        return spread(jnp.where(odd, first, second)), spread(jnp.where(odd, second, first))

    def y_tile(buf, f, z):
        return spread(take(buf, fine_row(f * PLANES + z, width)))

    for z in range(PLANES):
        halo[z] = jnp.where(edge_row, FINE_FACE * (stiff[z] + y_tile(y_one, 6, z)), 0.0)
    k_low = low_of(a_one, b_one, 6 * width)
    k_high = high_of(a_one, b_one, 6 * width)
    halo[4] = FINE_FACE * (stiff[0] + k_low)
    halo[5] = FINE_FACE * (stiff[PLANES - 1] + k_high)
    kd_low, kd_high = corner(da_one, db_one, corner_fine(3, width))
    halo[6] = jnp.where(edge_row, FINE_FACE * (k_low + kd_low), 0.0)
    halo[7] = jnp.where(edge_row, FINE_FACE * (k_high + kd_high), 0.0)
    halo[8] = FINE_FACE * (y_tile(y_one, 6, 0) + kd_low)
    halo[9] = FINE_FACE * (y_tile(y_one, 6, PLANES - 1) + kd_high)
    fine_coefs(stiff, top_half, coef)
    for c in range(FIELDS):
        group[c] = group_drive(comp[...], drive, c)
    on = [mask[z].astype(F32) * TIME_SQUARE for z in range(PLANES)]

    for c in range(FIELDS):
        d_low, d_high = corner(da_two, db_two, corner_fine(c, width))
        for z in range(PLANES):
            u = now[c, z]
            u_y = y_tile(y_two, c, z)
            flux = halo[z] * (u_y - u)
            new = free[c, z] + flux
            new_y = y_tile(y_two, 3 + c, z) - flux
            if z == 0:
                other = low_of(a_two, b_two, c * width)
                flux = halo[4] * (other - u)
                new = new + flux
                out = low_of(a_two, b_two, (3 + c) * width) - flux + halo[6] * (d_low - other)
                mid_low[c] = jnp.where(has_low, out, 0.0)
                new_y = new_y + halo[8] * (d_low - u_y)
            if z == PLANES - 1:
                other = high_of(a_two, b_two, c * width)
                flux = halo[5] * (other - u)
                new = new + flux
                out = high_of(a_two, b_two, (3 + c) * width) - flux + halo[7] * (d_high - other)
                mid_high[c] = jnp.where(has_high, out, 0.0)
                new_y = new_y + halo[9] * (d_high - u_y)
            mid[c, z] = new
            mid_y[c, z] = new_y
    for c in range(FIELDS):
        for z in range(PLANES):
            u = mid[c, z]
            new = fine_free(mid, now[c, z], c, z, coef, group[c] * on[z])
            new = new + halo[z] * (mid_y[c, z] - u)
            if z == 0:
                new = new + halo[4] * (mid_low[c] - u)
            if z == PLANES - 1:
                new = new + halo[5] * (mid_high[c] - u)
            emit(c, z, new)

    crow = iota((ROWS, half), 0)
    upper = crow < 4
    c_edge = lax.rem(crow, 4) == jnp.where(top_half, 3, 0)
    fields_one, fields_two = 7, 7 if round_two is round_one else 6
    base_one = 3 * width + half
    base_two = base_one if round_two is round_one else 3 * width

    def cy_tile(buf, f, base):
        lines = [take(buf, coarse_row(2 * f + zc, width, base)) for zc in range(2)]
        return jnp.where(upper, spread(lines[0]), spread(lines[1]))

    def c_corner(a, b, g):
        first, second = take(a, corner_coarse(g, width)), take(b, corner_coarse(g, width))
        low, high = jnp.where(odd, first, second), jnp.where(odd, second, first)
        return jnp.where(upper, spread(low), spread(high))

    def plane_pair(a, b, c):
        at = fields_two * width + c * half
        low, high = low_of(a, b, at, half), high_of(a, b, at, half)
        return (
            jnp.where(upper, low, roll(high, 4, 0)),
            jnp.where(upper, roll(low, 4, 0), high),
        )

    at = fields_one * width + 3 * half
    low, high = low_of(a_one, b_one, at, quarter), high_of(a_one, b_one, at, quarter)
    kz = jnp.where(
        upper,
        jnp.concatenate([low, roll(low, 4, 0)], axis=1),
        jnp.concatenate([roll(high, 4, 0), high], axis=1),
    )
    k = ck[...]
    kd = c_corner(da_one, db_one, 3)
    ky = cy_tile(y_one, 6, base_one)
    face_z = COARSE_FACE * (k + kz)
    face_y = jnp.where(c_edge, COARSE_FACE * (k + ky), 0.0)
    face_zd = jnp.where(c_edge, COARSE_FACE * (kz + kd), 0.0)
    face_yd = COARSE_FACE * (ky + kd)
    inside = jnp.where(upper, jnp.where(has_low, 1.0, 0.0), jnp.where(has_high, 1.0, 0.0))
    coefs = coarse_coefs(k, top_half)
    for c in range(FIELDS):
        u = cu_now[c]
        u_z, w_z = plane_pair(a_two, b_two, c)
        u_y = cy_tile(y_two, c, base_two)
        u_d = c_corner(da_two, db_two, c)
        flux_z = face_z * (u_z - u)
        flux_y = face_y * (u_y - u)
        new = cu_free[c] + flux_z + flux_y
        new_z = inside * (w_z - flux_z + face_zd * (u_d - u_z))
        new_y = cy_tile(y_two, 3 + c, base_two) - flux_y + face_yd * (u_d - u_y)
        coarse_mid[c] = new
        after = coarse_free(new, u, coefs, cf[c])
        emit_coarse(c, after + face_z * (new_z - new) + face_y * (new_y - new))
    return odd, top_half, on, coefs


def middle_kernel(
    mask, drive, comp, stiff, now, free, cu_now, cu_free, ck, cf,
    a_one, b_one, y_one, da_one, db_one,
    u_out, w_out, cu_out, cw_out, a_buf, b_buf, y_buf, da_buf, db_buf,
    mid, mid_y, mid_low, mid_high, coef, halo, group, coarse_mid,
):
    one = (a_one, b_one, y_one, da_one, db_one)

    def emit(c, z, value):
        u_out[c, z] = value

    def emit_coarse(c, value):
        cu_out[c] = value

    odd, top_half, on, coefs = join(
        one, one, mask, drive, comp, stiff, now, free, cu_now, cu_free, ck, cf,
        mid, mid_y, mid_low, mid_high, coef, halo, group, emit, emit_coarse, coarse_mid,
    )
    for c in range(FIELDS):
        cw_out[c] = coarse_free(cu_out[c], coarse_mid[c], coefs, cf[c])
        for z in range(PLANES):
            w_out[c, z] = fine_free(u_out, mid[c, z], c, z, coef, group[c] * on[z])
    pack(
        odd, top_half,
        lambda f, z: u_out[f, z] if f < 3 else w_out[f - 3, z],
        lambda f: cu_out[f] if f < 3 else cw_out[f - 3],
        None, None, a_buf, b_buf, y_buf, da_buf, db_buf, stiff.shape[2],
    )


def end_kernel(
    mask, drive, comp, stiff, now, free, cu_now, cu_free, ck, cf,
    a_one, b_one, y_one, da_one, db_one,
    a_two, b_two, y_two, da_two, db_two,
    u_out, cu_out,
    mid, mid_y, mid_low, mid_high, coef, halo, group, coarse_mid,
):
    def emit(c, z, value):
        u_out[c, z] = value

    def emit_coarse(c, value):
        for zc in range(2):
            cu_out[c, zc] = value[4 * zc : 4 * zc + 4]

    join(
        (a_one, b_one, y_one, da_one, db_one), (a_two, b_two, y_two, da_two, db_two),
        mask, drive, comp, stiff, now, free, cu_now, cu_free, ck, cf,
        mid, mid_y, mid_low, mid_high, coef, halo, group, emit, emit_coarse, coarse_mid,
    )


def struct(*shape):
    return jax.ShapeDtypeStruct(shape, F32)


def call(kernel, name, outs, scratch, operands):
    smem = pl.BlockSpec(memory_space=pltpu.SMEM)
    vmem = pl.BlockSpec(memory_space=pltpu.VMEM)
    return pl.pallas_call(
        kernel,
        name=name,
        out_shape=outs,
        in_specs=[smem, smem] + [vmem] * (len(operands) - 2),
        out_specs=[vmem] * len(outs),
        scratch_shapes=scratch,
        compiler_params=pltpu.CompilerParams(vmem_limit_bytes=32 * 1024 * 1024),
    )(*operands)


def exchange(bufs):
    count = lax.axis_size("ax")
    pair_a = [(i, i ^ 1) for i in range(count)]
    pair_b = [(i, i + 1 if i % 2 else i - 1) for i in range(1, count - 1)]

    def across(pairs):
        return [(2 * i + s, 2 * j + 1 - s) for i, j in pairs for s in (0, 1)]

    a, b, y, da, db = bufs
    b = lax.ppermute(b, "ax", pair_b)
    y = lax.ppermute(y, "xs", [(0, 1), (1, 0)])
    a = lax.ppermute(a, "ax", pair_a)
    db = lax.ppermute(db, ("ax", "xs"), across(pair_b))
    da = lax.ppermute(da, ("ax", "xs"), across(pair_a))
    return a, b, y, da, db


def local(displacement, previous, stiffness, tissue_mask, compartment, drive):
    width = displacement.shape[3]
    half = width // 2
    quarter = width // 4
    field = struct(FIELDS, PLANES, ROWS, width)
    coarse = struct(FIELDS, ROWS, half)

    def buffers(fields, with_k):
        plane = fields * width + 3 * half + (quarter if with_k else 0)
        rows = 3 * width + (3 * half if with_k else 2 * half)
        corner = struct(ROWS, half + quarter)
        return [struct(ROWS, plane), struct(ROWS, plane), struct(ROWS, rows), corner, corner]

    coef = pltpu.VMEM((6, PLANES, ROWS, width), F32)
    group = pltpu.VMEM((FIELDS, ROWS, width), F32)
    steps = [
        pltpu.VMEM((FIELDS, PLANES, ROWS, width), F32),
        pltpu.VMEM((FIELDS, PLANES, ROWS, width), F32),
        pltpu.VMEM((FIELDS, ROWS, width), F32),
        pltpu.VMEM((FIELDS, ROWS, width), F32),
        coef,
        pltpu.VMEM((10, ROWS, width), F32),
        group,
        pltpu.VMEM((FIELDS, ROWS, half), F32),
    ]
    fixed = (tissue_mask, drive, compartment, stiffness)
    w, cu, cw, ck, cf, *bufs = call(
        begin_kernel,
        "restrict_and_first_step",
        [field, coarse, coarse, struct(ROWS, half), coarse] + buffers(7, True),
        [coef, group, pltpu.VMEM((half // 128, 10 * ROWS, 128), F32)],
        fixed + (displacement, previous),
    )
    one = exchange(bufs)
    u, w, cu, cw, *bufs = call(
        middle_kernel,
        "two_steps",
        [field, field, coarse, coarse] + buffers(6, False),
        steps,
        fixed + (displacement, w, cu, cw, ck, cf) + one,
    )
    two = exchange(bufs)
    return call(
        end_kernel,
        "last_steps",
        [field, struct(FIELDS, 2, 4, half)],
        steps,
        fixed + (u, w, cu, cw, ck, cf) + one + two,
    )


def solution(mesh):
    placed = (
        P(None, "ax", "xs", None),
        P(None, "ax", "xs", None),
        P("ax", "xs", None),
        P("ax"),
        P("xs", None),
        P(),
    )

    def run(*args):
        return tuple(local(*args))

    return jax.shard_map(
        run,
        mesh=mesh,
        in_specs=placed,
        out_specs=(P(None, "ax", "xs", None), P(None, "ax", "xs", None)),
        check_vma=False,
    )
```

time: 345 us -> 52.3 us (0.15)
  the two profiles are of different devices: /device:TPU:128 before, /device:TPU:130 now
where the time goes in v1:
time: 52.3 us; the launch traced here: 51.9 us
  starting transfers between devices  21.4 us (41%)
  waiting for transfers between devices  16.4 us (31%)
  Pallas kernels  8.14 us (16%)
  local copies, waits for them, and re-layouts  5.18 us (10%)
  between operations  0.72 us (1%)
    ppermute x2, waiting for transfers between devices, exchange(): da = lax.ppermute(da, ('ax', 'xs'), across(pair_a))  9 us
    ppermute x2, starting transfers between devices, exchange(): db = lax.ppermute(db, ('ax', 'xs'), across(pair_b))  8.36 us
    pallas_call x3, Pallas kernels, call(): pl.pallas_call(kernel, name=name, out_shape=outs, in_specs=[smem, smem] +...  8.14 us
    ppermute x2, starting transfers between devices, exchange(): b = lax.ppermute(b, 'ax', pair_b)  7.65 us
    ppermute x2, waiting for transfers between devices, exchange(): db = lax.ppermute(db, ('ax', 'xs'), across(pair_b))  7.42 us
    unnamed x12, local copies, waits for them, and re-layouts  5.18 us
    ppermute x2, starting transfers between devices, exchange(): y = lax.ppermute(y, 'xs', [(0, 1), (1, 0)])  5.05 us
  transfers between devices with their start and end apart: 10, of which 4 were waited for; matrix products, arithmetic and copies ran while one was open for 0% of the time, Pallas kernels for 0%

profile of v1, /device:TPU:130, one launch (start us, length us, event | category | flops | bytes accessed | tf_op | source)
XLA Modules:
  0.0 51.9 jit_solution(13209822777660800983)
XLA Ops:
  0.6 1.1 %copy-done = f32[3,4,8,1536]{3,2,1,0:T(8,128)S(1)} copy-done((f32[3,4,8,1536]{3,2,1,0:T(8,128)S(1)}, f32[3,4,8,1536]{3,2,1,0:T(8,128)}, u32[]{:S(2)}) %copy-start) | copy-done | bytes 589848
  1.7 0.9 %copy-done.1 = f32[4,8,1536]{2,1,0:T(8,128)S(1)} copy-done((f32[4,8,1536]{2,1,0:T(8,128)S(1)}, f32[4,8,1536]{2,1,0:T(8,128)}, u32[]{:S(2)}) %copy-start.1) | copy-done | bytes 196632
  2.6 1.1 %copy-done.2 = f32[3,4,8,1536]{3,2,1,0:T(8,128)S(1)} copy-done((f32[3,4,8,1536]{3,2,1,0:T(8,128)S(1)}, f32[3,4,8,1536]{3,2,1,0:T(8,128)}, u32[]{:S(2)}) %copy-start.2) | copy-done | bytes 589848
  3.7 0.8 %copy-done.3 = s32[8,1536]{1,0:T(8,128)S(1)} copy-done((s32[8,1536]{1,0:T(8,128)S(1)}, s32[8,1536]{1,0:T(8,128)}, u32[]{:S(2)}) %copy-start.3) | copy-done | bytes 49176
  4.5 0.7 %copy-done.4 = f32[3,4]{1,0:T(4,128)S(1)} copy-done((f32[3,4]{1,0:T(4,128)S(1)}, f32[3,4]{1,0:T(4,128)}, u32[]{:S(2)}) %copy-start.4) | copy-done | bytes 72
  5.2 0.7 %copy-done.5 = s32[4]{0:T(128)S(1)} copy-done((s32[4]{0:T(128)S(1)}, s32[4]{0:T(128)}, u32[]{:S(2)}) %copy-start.5) | copy-done | bytes 40
  5.8 2.3 %restrict_and_first_step.1 = (f32[3,4,8,1536]{3,2,1,0:T(8,128)S(1)}, f32[3,8,768]{2,1,0:T(8,128)S(1)}, f32[3,8,768]{2,1,0:T(8,128)S(1)}, f32[8,768]{1,0:T(8,128)...) custom-call(s32[4]{0:T(128)S(1)} %copy-done.5, ...), custom_call_target="tpu_custom_call" | custom-call | tf_op jit(solution)/shard_map/restrict_and_first_step/pallas_call | solution.py:471
  8.2 0.1 collective-permute-start
  8.3 5.0 %collective-permute-start.1 = (f32[8,13440]{1,0:T(8,128)S(1)}, f32[8,13440]{1,0:T(8,128)S(1)}, u32[]{:S(2)}, u32[]{:S(2)}) collective-permute-start(f32[8,13440]{1,0:T(8,128)S(1)} %get-tuple-element.27), channel_id=1, source_target_pairs={{2,4},{4,2},{6,8},{8,6},{10,12},{12,10},{14,16},{16,14},{18,20},{2... | collective-permute-start | bytes 1290248 | tf_op jit(solution)/shard_map/ppermute | solution.py:491
  13.2 2.5 %collective-permute-start.2 = (f32[8,6912]{1,0:T(8,128)S(1)}, f32[8,6912]{1,0:T(8,128)S(1)}, u32[]{:S(2)}, u32[]{:S(2)}) collective-permute-start(f32[8,6912]{1,0:T(8,128)S(1)} %get-tuple-element.28), channel_id=1, source_target_pairs={{0,1},{1,0},{2,3},{3,2},{4,5},{5,4},{6,7},{7,6},{8,9},{9,8},{10,11... | collective-permute-start | bytes 663560 | tf_op jit(solution)/shard_map/ppermute | solution.py:492
  15.8 4.4 %collective-permute-start.4 = (f32[8,1152]{1,0:T(8,128)S(1)}, f32[8,1152]{1,0:T(8,128)S(1)}, u32[]{:S(2)}, u32[]{:S(2)}) collective-permute-start(f32[8,1152]{1,0:T(8,128)S(1)} %get-tuple-element.30), channel_id=1, source_target_pairs={{2,5},{3,4},{4,3},{5,2},{6,9},{7,8},{8,7},{9,6},{10,13},{11,12},{1... | collective-permute-start | bytes 110600 | tf_op jit(solution)/shard_map/ppermute | solution.py:494
  20.2 4.9 %collective-permute-done.3.da_one = f32[8,1152]{1,0:T(8,128)S(1)} collective-permute-done((f32[8,1152]{1,0:T(8,128)S(1)}, f32[8,1152]{1,0:T(8,128)S(1)}, u32[]{:S(2)}, u32[]{:S(2)}) %collective-permute-start.3) | collective-permute-done | bytes 36896 | tf_op jit(solution)/shard_map/ppermute | solution.py:495
  25.1 3.2 %collective-permute-done.4.db_one = f32[8,1152]{1,0:T(8,128)S(1)} collective-permute-done((f32[8,1152]{1,0:T(8,128)S(1)}, f32[8,1152]{1,0:T(8,128)S(1)}, u32[]{:S(2)}, u32[]{:S(2)}) %collective-permute-start.4) | collective-permute-done | bytes 36896 | tf_op jit(solution)/shard_map/ppermute | solution.py:494
  28.2 0.0 collective-permute-done.2.y_one
  28.3 2.9 %two_steps.1 = (f32[3,4,8,1536]{3,2,1,0:T(8,128)S(1)}, f32[3,4,8,1536]{3,2,1,0:T(8,128)S(1)}, f32[3,8,768]{2,1,0:T(8,128)S(1)}, f32[3,8,768]{2,1,0:T(8,128)S(1)}...) custom-call(s32[4]{0:T(128)S(1)} %copy-done.5, ...), custom_call_target="tpu_custom_call" | custom-call | tf_op jit(solution)/shard_map/two_steps/pallas_call | solution.py:471
  31.2 0.1 collective-permute-start.5
  31.3 2.7 %collective-permute-start.6 = (f32[8,11520]{1,0:T(8,128)S(1)}, f32[8,11520]{1,0:T(8,128)S(1)}, u32[]{:S(2)}, u32[]{:S(2)}) collective-permute-start(f32[8,11520]{1,0:T(8,128)S(1)} %get-tuple-element.36), channel_id=1, source_target_pairs={{2,4},{4,2},{6,8},{8,6},{10,12},{12,10},{14,16},{16,14},{18,20},{2... | collective-permute-start | bytes 1105928 | tf_op jit(solution)/shard_map/ppermute | solution.py:491
  34.0 2.5 %collective-permute-start.7 = (f32[8,6144]{1,0:T(8,128)S(1)}, f32[8,6144]{1,0:T(8,128)S(1)}, u32[]{:S(2)}, u32[]{:S(2)}) collective-permute-start(f32[8,6144]{1,0:T(8,128)S(1)} %get-tuple-element.37), channel_id=1, source_target_pairs={{0,1},{1,0},{2,3},{3,2},{4,5},{5,4},{6,7},{7,6},{8,9},{9,8},{10,11... | collective-permute-start | bytes 589832 | tf_op jit(solution)/shard_map/ppermute | solution.py:492
  36.5 0.1 collective-permute-start.8
  36.7 3.9 %collective-permute-start.9 = (f32[8,1152]{1,0:T(8,128)S(1)}, f32[8,1152]{1,0:T(8,128)S(1)}, u32[]{:S(2)}, u32[]{:S(2)}) collective-permute-start(f32[8,1152]{1,0:T(8,128)S(1)} %get-tuple-element.39), channel_id=1, source_target_pairs={{2,5},{3,4},{4,3},{5,2},{6,9},{7,8},{8,7},{9,6},{10,13},{11,12},{1... | collective-permute-start | bytes 110600 | tf_op jit(solution)/shard_map/ppermute | solution.py:494
  40.6 4.1 %collective-permute-done.8.da_two = f32[8,1152]{1,0:T(8,128)S(1)} collective-permute-done((f32[8,1152]{1,0:T(8,128)S(1)}, f32[8,1152]{1,0:T(8,128)S(1)}, u32[]{:S(2)}, u32[]{:S(2)}) %collective-permute-start.8) | collective-permute-done | bytes 36896 | tf_op jit(solution)/shard_map/ppermute | solution.py:495
  44.7 4.2 %collective-permute-done.9.db_two = f32[8,1152]{1,0:T(8,128)S(1)} collective-permute-done((f32[8,1152]{1,0:T(8,128)S(1)}, f32[8,1152]{1,0:T(8,128)S(1)}, u32[]{:S(2)}, u32[]{:S(2)}) %collective-permute-start.9) | collective-permute-done | bytes 36896 | tf_op jit(solution)/shard_map/ppermute | solution.py:494
  49.0 0.0 collective-permute-done.7.y_two
  49.0 2.9 %last_steps.1 = (f32[3,4,8,1536]{3,2,1,0:T(8,128)}, f32[3,2,4,768]{3,2,1,0:T(4,128)}) custom-call(s32[4]{0:T(128)S(1)} %copy-done.5, f32[3,4]{1,0:T(4,128)S(1)} %copy-done.4, s32[8,1536]{1,0:T(8,128)S(1)} %copy-done.3, f32[4,8,1536]{2,1,0:T(8,128)S(1)} %copy-done.1, f32[3,4,8,1536]{3,2,1,0:T(8,128)S(1)} %get-tuple-element.31.now, ...), custom_call_target="tpu_custom_call" | custom-call | tf_op jit(solution)/shard_map/last_steps/pallas_call | solution.py:471
  (11 shorter events, 0.0 us)
Async XLA Ops:
  0.6 1.1 %copy-start = (f32[3,4,8,1536]{3,2,1,0:T(8,128)S(1)}, f32[3,4,8,1536]{3,2,1,0:T(8,128)}, u32[]{:S(2)}) copy-start(f32[3,4,8,1536]{3,2,1,0:T(8,128)} %now.3) | copy-start | bytes 1769476
  1.7 0.9 %copy-start.1 = (f32[4,8,1536]{2,1,0:T(8,128)S(1)}, f32[4,8,1536]{2,1,0:T(8,128)}, u32[]{:S(2)}) copy-start(f32[4,8,1536]{2,1,0:T(8,128)} %stiff.5) | copy-start | bytes 589828
  2.6 1.1 %copy-start.2 = (f32[3,4,8,1536]{3,2,1,0:T(8,128)S(1)}, f32[3,4,8,1536]{3,2,1,0:T(8,128)}, u32[]{:S(2)}) copy-start(f32[3,4,8,1536]{3,2,1,0:T(8,128)} %before.1) | copy-start | bytes 1769476
  3.7 0.8 %copy-start.3 = (s32[8,1536]{1,0:T(8,128)S(1)}, s32[8,1536]{1,0:T(8,128)}, u32[]{:S(2)}) copy-start(s32[8,1536]{1,0:T(8,128)} %comp.5) | copy-start | bytes 147460
  4.5 0.7 %copy-start.4 = (f32[3,4]{1,0:T(4,128)S(1)}, f32[3,4]{1,0:T(4,128)}, u32[]{:S(2)}) copy-start(f32[3,4]{1,0:T(4,128)} %drive.5) | copy-start | bytes 148
  5.2 0.7 %copy-start.5 = (s32[4]{0:T(128)S(1)}, s32[4]{0:T(128)}, u32[]{:S(2)}) copy-start(s32[4]{0:T(128)} %mask.5) | copy-start | bytes 52
  8.2 20.1 %collective-permute-start = (f32[8,13440]{1,0:T(8,128)S(1)}, f32[8,13440]{1,0:T(8,128)S(1)}, u32[]{:S(2)}, u32[]{:S(2)}) collective-permute-start(f32[8,13440]{1,0:T(8,128)S(1)} %get-tuple-element.26), channel_id=1, source_target_pairs={{0,2},{2,0},{4,6},{6,4},{8,10},{10,8},{12,14},{14,12},{16,18},{18,... | collective-permute-start | bytes 1290248 | tf_op jit(solution)/shard_map/ppermute | solution.py:493
  8.3 20.0 %collective-permute-start.1 = (f32[8,13440]{1,0:T(8,128)S(1)}, f32[8,13440]{1,0:T(8,128)S(1)}, u32[]{:S(2)}, u32[]{:S(2)}) collective-permute-start(f32[8,13440]{1,0:T(8,128)S(1)} %get-tuple-element.27), channel_id=1, source_target_pairs={{2,4},{4,2},{6,8},{8,6},{10,12},{12,10},{14,16},{16,14},{18,20},{2... | collective-permute-start | bytes 1290248 | tf_op jit(solution)/shard_map/ppermute | solution.py:491
  13.2 15.0 %collective-permute-start.2 = (f32[8,6912]{1,0:T(8,128)S(1)}, f32[8,6912]{1,0:T(8,128)S(1)}, u32[]{:S(2)}, u32[]{:S(2)}) collective-permute-start(f32[8,6912]{1,0:T(8,128)S(1)} %get-tuple-element.28), channel_id=1, source_target_pairs={{0,1},{1,0},{2,3},{3,2},{4,5},{5,4},{6,7},{7,6},{8,9},{9,8},{10,11... | collective-permute-start | bytes 663560 | tf_op jit(solution)/shard_map/ppermute | solution.py:492
  15.8 9.3 %collective-permute-start.3 = (f32[8,1152]{1,0:T(8,128)S(1)}, f32[8,1152]{1,0:T(8,128)S(1)}, u32[]{:S(2)}, u32[]{:S(2)}) collective-permute-start(f32[8,1152]{1,0:T(8,128)S(1)} %get-tuple-element.29), channel_id=1, source_target_pairs={{0,3},{1,2},{2,1},{3,0},{4,7},{5,6},{6,5},{7,4},{8,11},{9,10},{10,... | collective-permute-start | bytes 110600 | tf_op jit(solution)/shard_map/ppermute | solution.py:495
  15.8 12.5 %collective-permute-start.4 = (f32[8,1152]{1,0:T(8,128)S(1)}, f32[8,1152]{1,0:T(8,128)S(1)}, u32[]{:S(2)}, u32[]{:S(2)}) collective-permute-start(f32[8,1152]{1,0:T(8,128)S(1)} %get-tuple-element.30), channel_id=1, source_target_pairs={{2,5},{3,4},{4,3},{5,2},{6,9},{7,8},{8,7},{9,6},{10,13},{11,12},{1... | collective-permute-start | bytes 110600 | tf_op jit(solution)/shard_map/ppermute | solution.py:494
  31.2 17.8 %collective-permute-start.5 = (f32[8,11520]{1,0:T(8,128)S(1)}, f32[8,11520]{1,0:T(8,128)S(1)}, u32[]{:S(2)}, u32[]{:S(2)}) collective-permute-start(f32[8,11520]{1,0:T(8,128)S(1)} %get-tuple-element.35), channel_id=1, source_target_pairs={{0,2},{2,0},{4,6},{6,4},{8,10},{10,8},{12,14},{14,12},{16,18},{18,... | collective-permute-start | bytes 1105928 | tf_op jit(solution)/shard_map/ppermute | solution.py:493
  31.3 17.7 %collective-permute-start.6 = (f32[8,11520]{1,0:T(8,128)S(1)}, f32[8,11520]{1,0:T(8,128)S(1)}, u32[]{:S(2)}, u32[]{:S(2)}) collective-permute-start(f32[8,11520]{1,0:T(8,128)S(1)} %get-tuple-element.36), channel_id=1, source_target_pairs={{2,4},{4,2},{6,8},{8,6},{10,12},{12,10},{14,16},{16,14},{18,20},{2... | collective-permute-start | bytes 1105928 | tf_op jit(solution)/shard_map/ppermute | solution.py:491
  34.0 15.0 %collective-permute-start.7 = (f32[8,6144]{1,0:T(8,128)S(1)}, f32[8,6144]{1,0:T(8,128)S(1)}, u32[]{:S(2)}, u32[]{:S(2)}) collective-permute-start(f32[8,6144]{1,0:T(8,128)S(1)} %get-tuple-element.37), channel_id=1, source_target_pairs={{0,1},{1,0},{2,3},{3,2},{4,5},{5,4},{6,7},{7,6},{8,9},{9,8},{10,11... | collective-permute-start | bytes 589832 | tf_op jit(solution)/shard_map/ppermute | solution.py:492
  36.5 8.2 %collective-permute-start.8 = (f32[8,1152]{1,0:T(8,128)S(1)}, f32[8,1152]{1,0:T(8,128)S(1)}, u32[]{:S(2)}, u32[]{:S(2)}) collective-permute-start(f32[8,1152]{1,0:T(8,128)S(1)} %get-tuple-element.38), channel_id=1, source_target_pairs={{0,3},{1,2},{2,1},{3,0},{4,7},{5,6},{6,5},{7,4},{8,11},{9,10},{10,... | collective-permute-start | bytes 110600 | tf_op jit(solution)/shard_map/ppermute | solution.py:495
  36.7 12.3 %collective-permute-start.9 = (f32[8,1152]{1,0:T(8,128)S(1)}, f32[8,1152]{1,0:T(8,128)S(1)}, u32[]{:S(2)}, u32[]{:S(2)}) collective-permute-start(f32[8,1152]{1,0:T(8,128)S(1)} %get-tuple-element.39), channel_id=1, source_target_pairs={{2,5},{3,4},{4,3},{5,2},{6,9},{7,8},{8,7},{9,6},{10,13},{11,12},{1... | collective-permute-start | bytes 110600 | tf_op jit(solution)/shard_map/ppermute | solution.py:494

commit v2 on v1

v2 whole, which is shorter than its diff:
```python
import jax
import jax.numpy as jnp
from jax import lax
from jax.experimental import pallas as pl
from jax.experimental.pallas import tpu as pltpu
from jax.sharding import PartitionSpec as P

TIME_SQUARE = 0.12
FINE_FACE = 0.5 * TIME_SQUARE
COARSE_FACE = 0.25 * 0.5 * TIME_SQUARE
PLANES = 4
ROWS = 8
FIELDS = 3
F32 = jnp.float32


def roll(x, shift, axis):
    return pltpu.roll(x, shift % x.shape[axis], axis)


def place():
    i = lax.axis_index("ax")
    s = lax.axis_index("xs")
    return (lax.rem(i, 2) == 1), (s == 0), (i > 0), (i < lax.axis_size("ax") - 1)


def iota(shape, dim):
    return lax.broadcasted_iota(jnp.int32, shape, dim)


def stiff_coefs(k, face, low_y, high_y, outer_row):
    width = k.shape[1]
    lane = iota(k.shape, 1)
    last = lane == width - 1
    start = lane == 0
    kp = jnp.where(last, 0.0, roll(k, -1, 1))
    km = jnp.where(start, 0.0, roll(k, 1, 1))
    full_p = face * (k + kp)
    full_m = face * (k + km)
    cyp = jnp.where(high_y, face * (k + roll(k, -1, 0)), 0.0)
    cym = jnp.where(low_y, face * (k + roll(k, 1, 0)), 0.0)
    edge = jnp.where(outer_row, face * k, 0.0)
    centre = 2.0 - (full_p + full_m + cyp + cym + edge)
    return jnp.where(last, 0.0, full_p), jnp.where(start, 0.0, full_m), cyp, cym, centre


def fine_coefs(k_ref, first, coef):
    shape = k_ref.shape[1:]
    row = iota(shape, 0)
    for z in range(PLANES - 1):
        coef[5, z] = FINE_FACE * (k_ref[z] + k_ref[z + 1])
    for z in range(PLANES):
        cxp, cxm, cyp, cym, centre = stiff_coefs(
            k_ref[z], FINE_FACE, row > 0, row < ROWS - 1, row == jnp.where(first, 0, ROWS - 1)
        )
        if z > 0:
            centre = centre - coef[5, z - 1]
        if z < PLANES - 1:
            centre = centre - coef[5, z]
        coef[0, z] = cxp
        coef[1, z] = cxm
        coef[2, z] = cyp
        coef[3, z] = cym
        coef[4, z] = centre


def fine_free(u_ref, before, c, z, coef, drive_term):
    u = u_ref[c, z]
    acc = coef[4, z] * u - before
    acc = acc + coef[0, z] * roll(u, -1, 1) + coef[1, z] * roll(u, 1, 1)
    acc = acc + coef[2, z] * roll(u, -1, 0) + coef[3, z] * roll(u, 1, 0)
    if z > 0:
        acc = acc + coef[5, z - 1] * u_ref[c, z - 1]
    if z < PLANES - 1:
        acc = acc + coef[5, z] * u_ref[c, z + 1]
    return acc + drive_term


def coarse_coefs(k, first):
    row = iota(k.shape, 0)
    inner = lax.rem(row, 4)
    cxp, cxm, cyp, cym, centre = stiff_coefs(
        k, COARSE_FACE, inner > 0, inner < 3, inner == jnp.where(first, 0, 3)
    )
    cz = COARSE_FACE * (k + roll(k, 4, 0))
    return cxp, cxm, cyp, cym, centre - cz, cz


def coarse_free(u, before, coefs, force):
    cxp, cxm, cyp, cym, centre, cz = coefs
    return (
        centre * u
        - before
        + cxp * roll(u, -1, 1)
        + cxm * roll(u, 1, 1)
        + cyp * roll(u, -1, 0)
        + cym * roll(u, 1, 0)
        + cz * roll(u, 4, 0)
        + force
    )


def group_drive(compartment, drive_ref, c):
    value = jnp.full(compartment.shape, drive_ref[c, 0], F32)
    for g in range(1, drive_ref.shape[1]):
        value = jnp.where(compartment == g, drive_ref[c, g], value)
    return value


def fine_row(r, width):
    if r < 24:
        return [(r % 8, (r // 8) * width, width)]
    half = width // 2
    return [(2 * (r - 24) + h, 3 * width, half) for h in range(2)]


def coarse_row(q, width, base):
    half = width // 2
    return [(q % 8, base + (q // 8) * half, half)]


def corner_fine(f, width):
    half = width // 2
    return [(2 * f + h, 0, half) for h in range(2)]


def corner_coarse(f, width):
    quarter = width // 4
    return [(2 * f + h, width // 2, quarter) for h in range(2)]


def put(buf, pieces, line):
    at = 0
    for row, lane, lanes in pieces:
        buf[row : row + 1, lane : lane + lanes] = line[:, at : at + lanes]
        at += lanes


def take(buf, pieces):
    parts = [buf[row : row + 1, lane : lane + lanes] for row, lane, lanes in pieces]
    return parts[0] if len(parts) == 1 else jnp.concatenate(parts, axis=1)


def spread(line, rows=ROWS):
    return jnp.broadcast_to(line, (rows, line.shape[1]))


def edge_line(tile, top_half, base=0, rows=ROWS):
    return jnp.where(top_half, tile[base + rows - 1 : base + rows], tile[base : base + 1])


def pack(odd, top_half, fine, coarse, stiff, coarse_stiff, a_buf, b_buf, y_buf, db_buf, width):
    half = width // 2
    quarter = width // 4
    with_k = stiff is not None
    fields = 7 if with_k else 6
    zero = jnp.zeros((2, half), F32)
    upper = iota((ROWS, half), 0) < 4

    def tile(f, z):
        return fine(f, z) if f < 6 else stiff(z)

    base = 3 * width + (half if with_k else 0)
    for f in range(fields):
        for z in range(PLANES):
            t = tile(f, z)
            line = edge_line(t, top_half)
            put(y_buf, fine_row(f * PLANES + z, width), line)
            if z == 0:
                low, low_line = t, line
        a_buf[:, f * width : (f + 1) * width] = jnp.where(odd, low, t)
        b_buf[:, f * width : (f + 1) * width] = jnp.where(odd, t, low)
        g = f if f < 3 else (3 if f == 6 else None)
        if g is not None:
            put(db_buf, corner_fine(g, width), jnp.where(odd, line, low_line))

    for f in range(fields):
        t = coarse(f) if f < 6 else coarse_stiff
        lines = [edge_line(t, top_half, 4 * zc, 4) for zc in range(2)]
        for zc in range(2):
            put(y_buf, coarse_row(2 * f + zc, width, base), lines[zc])
        g = f if f < 3 else (3 if f == 6 else None)
        if g is not None:
            put(db_buf, corner_coarse(g, width), jnp.where(odd, lines[1], lines[0]))
    if with_k:
        y_buf[6:8, base + half : base + 2 * half] = zero
    else:
        y_buf[4:8, base + half : base + 2 * half] = jnp.zeros((4, half), F32)
        db_buf[6:8, :] = jnp.zeros((2, db_buf.shape[1]), F32)

    at = fields * width
    for c in range(FIELDS):
        first, second = coarse(c), coarse(c + 3)
        low = jnp.where(upper, first, roll(second, 4, 0))
        high = jnp.where(upper, roll(first, 4, 0), second)
        a_buf[:, at : at + half] = jnp.where(odd, low, high)
        b_buf[:, at : at + half] = jnp.where(odd, high, low)
        at += half
    if with_k:
        some = iota((ROWS, quarter), 0) < 4
        low, high = coarse_stiff, roll(coarse_stiff, 4, 0)
        low = jnp.where(some, low[:, :quarter], roll(low[:, quarter:], 4, 0))
        high = jnp.where(some, high[:, :quarter], roll(high[:, quarter:], 4, 0))
        a_buf[:, at : at + quarter] = jnp.where(odd, low, high)
        b_buf[:, at : at + quarter] = jnp.where(odd, high, low)


def begin_kernel(
    mask_hbm, drive_hbm, comp_hbm, stiff_hbm, now_hbm, before_hbm,
    y_buf, b_buf, db_buf, a_buf, now, stiff, coef, force, w_out, cu_out, cw_out, ck_out, cf_out,
    mask, drive, comp, before, group, wide, sems,
):
    pairs = (
        (drive_hbm, drive), (mask_hbm, mask), (comp_hbm, comp), (stiff_hbm, stiff),
        (now_hbm, now), (before_hbm, before),
    )
    copies = [pltpu.make_async_copy(src, dst, sems.at[n]) for n, (src, dst) in enumerate(pairs)]
    for copy in copies:
        copy.start()
    odd, top_half, _, _ = place()
    width = stiff.shape[2]
    half = width // 2
    row = iota((ROWS, width), 0)
    even_row = lax.rem(row, 2) == 0

    for copy in copies[:3]:
        copy.wait()
    on = [mask[z].astype(F32) for z in range(PLANES)]
    for c in range(FIELDS):
        group[c] = group_drive(comp[...], drive, c)
    for c in range(FIELDS):
        for z in range(PLANES):
            force[c, z] = group[c] * (TIME_SQUARE * on[z])
    copies[3].wait()
    fine_coefs(stiff, top_half, coef)
    for copy in copies[4:]:
        copy.wait()

    def pooled(first, second):
        first = first + roll(first, -1, 0)
        second = second + roll(second, -1, 0)
        return jnp.where(even_row, first, roll(second, 1, 0))

    tiles = []
    for c in range(FIELDS):
        tiles.append(pooled(now[c, 0] + now[c, 1], now[c, 2] + now[c, 3]))
    for c in range(FIELDS):
        tiles.append(pooled(before[c, 0] + before[c, 1], before[c, 2] + before[c, 3]))
    tiles.append(pooled(stiff[0] + stiff[1], stiff[2] + stiff[3]))
    for c in range(FIELDS):
        tiles.append(pooled(group[c], group[c]))
    stacked = jnp.concatenate(tiles, axis=0)
    pool = jnp.where(iota((256, 128), 0) // 2 == iota((256, 128), 1), 0.125, 0.0)
    for q in range(width // 256):
        wide[q] = lax.dot_general(
            stacked[:, q * 256 : (q + 1) * 256], pool, (((1,), (0,)), ((), ())),
            precision=lax.Precision.HIGHEST, preferred_element_type=F32,
        )

    def coarse_tile(f):
        planes = [
            jnp.concatenate([wide[q, pl.ds(8 * f + zc, 4, stride=2), :] for q in range(half // 128)], axis=1)
            for zc in range(2)
        ]
        return jnp.concatenate(planes, axis=0)

    upper = iota((ROWS, half), 0) < 4
    weight = jnp.where(upper, on[0] + on[1], on[2] + on[3]) * TIME_SQUARE
    ck_out[...] = coarse_tile(6)
    coefs = coarse_coefs(ck_out[...], top_half)
    for c in range(FIELDS):
        cu_out[c] = coarse_tile(c)
        cf_out[c] = coarse_tile(7 + c) * weight
        cw_out[c] = coarse_free(cu_out[c], coarse_tile(3 + c), coefs, cf_out[c])

    for c in range(FIELDS):
        for z in range(PLANES):
            w_out[c, z] = fine_free(now, before[c, z], c, z, coef, force[c, z])
    pack(
        odd, top_half,
        lambda f, z: now[f, z] if f < 3 else w_out[f - 3, z],
        lambda f: cu_out[f] if f < 3 else cw_out[f - 3],
        lambda z: stiff[z], ck_out[...],
        a_buf, b_buf, y_buf, db_buf, width,
    )


class Halo:
    def __init__(self, bufs, with_k, odd, width):
        self.y, self.b, self.db, self.a, self.ya = bufs
        self.odd, self.width, self.with_k = odd, width, with_k
        self.fields = 7 if with_k else 6
        self.base = 3 * width + (width // 2 if with_k else 0)

    def low(self, at, lanes):
        return jnp.where(self.odd, self.a[:, at : at + lanes], self.b[:, at : at + lanes])

    def high(self, at, lanes):
        return jnp.where(self.odd, self.b[:, at : at + lanes], self.a[:, at : at + lanes])

    def plane_low(self, f):
        return self.low(f * self.width, self.width)

    def plane_high(self, f):
        return self.high(f * self.width, self.width)

    def rows(self, f, z):
        return spread(take(self.y, fine_row(f * PLANES + z, self.width)))

    def corners(self, f):
        near = [take(self.ya, fine_row(f * PLANES + z, self.width)) for z in (PLANES - 1, 0)]
        far = take(self.db, corner_fine(3 if f == 6 else f, self.width))
        low = jnp.where(self.odd, near[0], far)
        high = jnp.where(self.odd, far, near[1])
        return spread(low), spread(high)

    def coarse_rows(self, f, upper, buf=None):
        buf = self.y if buf is None else buf
        lines = [take(buf, coarse_row(2 * f + zc, self.width, self.base)) for zc in range(2)]
        return jnp.where(upper, spread(lines[0]), spread(lines[1]))

    def coarse_corner(self, f, upper):
        near = [take(self.ya, coarse_row(2 * f + zc, self.width, self.base)) for zc in (1, 0)]
        far = take(self.db, corner_coarse(3 if f == 6 else f, self.width))
        low = jnp.where(self.odd, near[0], far)
        high = jnp.where(self.odd, far, near[1])
        return jnp.where(upper, spread(low), spread(high))

    def coarse_planes(self, c, upper):
        half = self.width // 2
        at = self.fields * self.width + c * half
        low, high = self.low(at, half), self.high(at, half)
        return (
            jnp.where(upper, low, roll(high, 4, 0)),
            jnp.where(upper, roll(low, 4, 0), high),
        )

    def coarse_stiff_planes(self, upper):
        at = self.fields * self.width + 3 * (self.width // 2)
        low, high = self.low(at, self.width // 4), self.high(at, self.width // 4)
        return jnp.where(
            upper,
            jnp.concatenate([low, roll(low, 4, 0)], axis=1),
            jnp.concatenate([roll(high, 4, 0), high], axis=1),
        )


def faces(got, stiff, ck, halo, coarse_halo, top_half, has_low, has_high):
    shape = stiff.shape[1:]
    half = shape[1] // 2
    edge_row = iota(shape, 0) == jnp.where(top_half, ROWS - 1, 0)
    for z in range(PLANES):
        halo[z] = jnp.where(edge_row, FINE_FACE * (stiff[z] + got.rows(6, z)), 0.0)
    k_low, k_high = got.plane_low(6), got.plane_high(6)
    kd_low, kd_high = got.corners(6)
    halo[4] = FINE_FACE * (stiff[0] + k_low)
    halo[5] = FINE_FACE * (stiff[PLANES - 1] + k_high)
    halo[6] = jnp.where(edge_row, FINE_FACE * (k_low + kd_low), 0.0)
    halo[7] = jnp.where(edge_row, FINE_FACE * (k_high + kd_high), 0.0)
    halo[8] = FINE_FACE * (got.rows(6, 0) + kd_low)
    halo[9] = FINE_FACE * (got.rows(6, PLANES - 1) + kd_high)

    row = iota((ROWS, half), 0)
    upper = row < 4
    edge = lax.rem(row, 4) == jnp.where(top_half, 3, 0)
    k = ck[...]
    kz, ky, kd = got.coarse_stiff_planes(upper), got.coarse_rows(6, upper), got.coarse_corner(6, upper)
    coarse_halo[0] = COARSE_FACE * (k + kz)
    coarse_halo[1] = jnp.where(edge, COARSE_FACE * (k + ky), 0.0)
    coarse_halo[2] = jnp.where(edge, COARSE_FACE * (kz + kd), 0.0)
    coarse_halo[3] = COARSE_FACE * (ky + kd)
    coarse_halo[4] = jnp.where(upper, jnp.where(has_low, 1.0, 0.0), jnp.where(has_high, 1.0, 0.0))


def join(
    got, coef, halo, coarse_halo, force, now, free, cu_now, cu_free, ck, cf,
    mid, mid_y, mid_low, mid_high, coarse_mid, emit, emit_coarse, top_half, has_low, has_high,
):
    for c in range(FIELDS):
        d_low, d_high = got.corners(c)
        for z in range(PLANES):
            u = now[c, z]
            u_y = got.rows(c, z)
            flux = halo[z] * (u_y - u)
            new = free[c, z] + flux
            new_y = got.rows(3 + c, z) - flux
            if z == 0:
                other = got.plane_low(c)
                flux = halo[4] * (other - u)
                new = new + flux
                out = got.plane_low(3 + c) - flux + halo[6] * (d_low - other)
                mid_low[c] = jnp.where(has_low, out, 0.0)
                new_y = new_y + halo[8] * (d_low - u_y)
            if z == PLANES - 1:
                other = got.plane_high(c)
                flux = halo[5] * (other - u)
                new = new + flux
                out = got.plane_high(3 + c) - flux + halo[7] * (d_high - other)
                mid_high[c] = jnp.where(has_high, out, 0.0)
                new_y = new_y + halo[9] * (d_high - u_y)
            mid[c, z] = new
            mid_y[c, z] = new_y

        for z in range(PLANES):
            u = mid[c, z]
            new = fine_free(mid, now[c, z], c, z, coef, force[c, z])
            new = new + halo[z] * (mid_y[c, z] - u)
            if z == 0:
                new = new + halo[4] * (mid_low[c] - u)
            if z == PLANES - 1:
                new = new + halo[5] * (mid_high[c] - u)
            emit(c, z, new)

    upper = iota(cf.shape[1:], 0) < 4
    face_z, face_y, face_zd, face_yd, inside = [coarse_halo[n] for n in range(5)]
    coefs = coarse_coefs(ck[...], top_half)
    for c in range(FIELDS):
        u = cu_now[c]
        u_z, w_z = got.coarse_planes(c, upper)
        u_y = got.coarse_rows(c, upper)
        u_d = got.coarse_corner(c, upper)
        flux_z = face_z * (u_z - u)
        flux_y = face_y * (u_y - u)
        new = cu_free[c] + flux_z + flux_y
        new_z = inside * (w_z - flux_z + face_zd * (u_d - u_z))
        new_y = got.coarse_rows(3 + c, upper) - flux_y + face_yd * (u_d - u_y)
        coarse_mid[c] = new
        after = coarse_free(new, u, coefs, cf[c])
        emit_coarse(c, after + face_z * (new_z - new) + face_y * (new_y - new))
    return coefs


def middle_kernel(
    y_one, b_one, db_one, a_one, ya_one, coef, force, stiff, now, free, cu_now, cu_free, ck, cf,
    y_buf, b_buf, db_buf, a_buf, halo, coarse_halo, u_out, w_out, cu_out, cw_out,
    mid, mid_y, mid_low, mid_high, coarse_mid,
):
    odd, top_half, has_low, has_high = place()
    got = Halo((y_one, b_one, db_one, a_one, ya_one), True, odd, stiff.shape[2])
    faces(got, stiff, ck, halo, coarse_halo, top_half, has_low, has_high)

    def emit(c, z, value):
        u_out[c, z] = value

    def emit_coarse(c, value):
        cu_out[c] = value

    coefs = join(
        got, coef, halo, coarse_halo, force, now, free, cu_now, cu_free, ck, cf,
        mid, mid_y, mid_low, mid_high, coarse_mid, emit, emit_coarse, top_half, has_low, has_high,
    )
    for c in range(FIELDS):
        cw_out[c] = coarse_free(cu_out[c], coarse_mid[c], coefs, cf[c])
        for z in range(PLANES):
            w_out[c, z] = fine_free(u_out, mid[c, z], c, z, coef, force[c, z])
    pack(
        odd, top_half,
        lambda f, z: u_out[f, z] if f < 3 else w_out[f - 3, z],
        lambda f: cu_out[f] if f < 3 else cw_out[f - 3],
        None, None, a_buf, b_buf, y_buf, db_buf, stiff.shape[2],
    )


def end_kernel(
    y_two, b_two, db_two, a_two, ya_two, coef, force, halo, coarse_halo, now, free, cu_now, cu_free, ck, cf,
    u_hbm, cu_hbm,
    mid, mid_y, mid_low, mid_high, coarse_mid, last, coarse_last, sems,
):
    odd, top_half, has_low, has_high = place()
    got = Halo((y_two, b_two, db_two, a_two, ya_two), False, odd, coef.shape[3])
    copies = []

    def emit(c, z, value):
        last[c, z] = value
        if z == PLANES - 1:
            copies.append(pltpu.make_async_copy(last.at[c], u_hbm.at[c], sems.at[c]))
            copies[-1].start()

    def emit_coarse(c, value):
        for zc in range(2):
            coarse_last[c, zc] = value[4 * zc : 4 * zc + 4]

    join(
        got, coef, halo, coarse_halo, force, now, free, cu_now, cu_free, ck, cf,
        mid, mid_y, mid_low, mid_high, coarse_mid, emit, emit_coarse, top_half, has_low, has_high,
    )
    copies.append(pltpu.make_async_copy(coarse_last, cu_hbm, sems.at[FIELDS]))
    copies[-1].start()
    for copy in copies:
        copy.wait()


def struct(*shape):
    return jax.ShapeDtypeStruct(shape, F32)


def call(kernel, name, outs, scratch, operands, in_space=pltpu.VMEM, out_space=pltpu.VMEM, vmem=32):
    return pl.pallas_call(
        kernel,
        name=name,
        out_shape=outs,
        in_specs=[pl.BlockSpec(memory_space=in_space)] * len(operands),
        out_specs=[pl.BlockSpec(memory_space=out_space)] * len(outs),
        scratch_shapes=scratch,
        compiler_params=pltpu.CompilerParams(vmem_limit_bytes=vmem * 1024 * 1024),
    )(*operands)


def exchange(bufs):
    count = lax.axis_size("ax")
    pair_a = [(i, i ^ 1) for i in range(count)]
    pair_b = [(i, i + 1 if i % 2 else i - 1) for i in range(1, count - 1)]
    across = [(2 * i + s, 2 * j + 1 - s) for i, j in pair_b for s in (0, 1)]
    y, b, db, a = bufs
    y = lax.ppermute(y, "xs", [(0, 1), (1, 0)])
    b = lax.ppermute(b, "ax", pair_b)
    db = lax.ppermute(db, ("ax", "xs"), across)
    a = lax.ppermute(a, "ax", pair_a)
    y, db = lax.optimization_barrier((y, db))
    ya = lax.ppermute(y, "ax", pair_a)
    return y, b, db, a, ya


def local(displacement, previous, stiffness, tissue_mask, compartment, drive):
    width = displacement.shape[3]
    half = width // 2
    quarter = width // 4
    field = struct(FIELDS, PLANES, ROWS, width)
    coarse = struct(FIELDS, ROWS, half)

    def buffers(fields, with_k):
        plane = fields * width + 3 * half + (quarter if with_k else 0)
        rows = 3 * width + (3 * half if with_k else 2 * half)
        return [struct(ROWS, rows), struct(ROWS, plane), struct(ROWS, half + quarter), struct(ROWS, plane)]

    whole = pltpu.VMEM(field.shape, F32)
    tile = pltpu.VMEM((FIELDS, ROWS, width), F32)
    small = pltpu.VMEM(coarse.shape, F32)
    y, b, db, a, now, stiff, coef, force, w, cu, cw, ck, cf = call(
        begin_kernel,
        "restrict_and_first_step",
        buffers(7, True)
        + [field, struct(*stiffness.shape), struct(6, PLANES, ROWS, width), field, field]
        + [coarse, coarse, struct(ROWS, half), coarse],
        [
            pltpu.SMEM(tissue_mask.shape, jnp.int32),
            pltpu.SMEM(drive.shape, F32),
            pltpu.VMEM(compartment.shape, jnp.int32),
            whole,
            tile,
            pltpu.VMEM((half // 128, 10 * ROWS, 128), F32),
            pltpu.SemaphoreType.DMA((6,)),
        ],
        [
            pltpu.with_memory_space_constraint(x, pltpu.HBM)
            for x in (tissue_mask, drive, compartment, stiffness, displacement, previous)
        ],
        in_space=pltpu.HBM,
    )
    one = exchange((y, b, db, a))
    steps = [whole, whole, tile, tile, small]
    y, b, db, a, halo, coarse_halo, u, w, cu, cw = call(
        middle_kernel,
        "two_steps",
        buffers(6, False)
        + [struct(10, ROWS, width), struct(5, ROWS, half), field, field, coarse, coarse],
        steps,
        one + (coef, force, stiff, now, w, cu, cw, ck, cf),
    )
    two = exchange((y, b, db, a))
    return call(
        end_kernel,
        "last_steps",
        [field, struct(FIELDS, 2, 4, half)],
        steps + [whole, pltpu.VMEM((FIELDS, 2, 4, half), F32), pltpu.SemaphoreType.DMA((FIELDS + 1,))],
        two + (coef, force, halo, coarse_halo, u, w, cu, cw, ck, cf),
        out_space=pltpu.HBM,
    )


def solution(mesh):
    placed = (
        P(None, "ax", "xs", None),
        P(None, "ax", "xs", None),
        P("ax", "xs", None),
        P("ax"),
        P("xs", None),
        P(),
    )

    def run(*args):
        return tuple(local(*args))

    return jax.shard_map(
        run,
        mesh=mesh,
        in_specs=placed,
        out_specs=(P(None, "ax", "xs", None), P(None, "ax", "xs", None)),
        check_vma=False,
    )
```

time: 52.3 us -> 45.1 us (0.86)
  the two profiles are of different devices: /device:TPU:130 before, /device:TPU:128 now
where the time goes in v2:
time: 45.1 us; the launch traced here: 44.6 us
  starting transfers between devices  24 us (53%)
  waiting for transfers between devices  13 us (29%)
  Pallas kernels  6.84 us (15%)
  between operations  0.72 us (2%)
    ppermute x2, starting transfers between devices, exchange(): db = lax.ppermute(db, ('ax', 'xs'), across)  11.3 us
    ppermute x2, waiting for transfers between devices, exchange(): db = lax.ppermute(db, ('ax', 'xs'), across)  10.1 us
    ppermute x2, starting transfers between devices, exchange(): b = lax.ppermute(b, 'ax', pair_b)  7.67 us
    pallas_call x3, Pallas kernels, call(): pl.pallas_call(kernel, name=name, out_shape=outs, in_specs=[pl.BlockSpec(...  6.84 us
    ppermute x2, starting transfers between devices, exchange(): y = lax.ppermute(y, 'xs', [(0, 1), (1, 0)])  4.9 us
    ppermute x2, waiting for transfers between devices, exchange(): ya = lax.ppermute(y, 'ax', pair_a)  2.88 us
  transfers between devices with their start and end apart: 10, of which 4 were waited for; matrix products, arithmetic and copies ran while one was open for 0% of the time, Pallas kernels for 0%

profile of v2, /device:TPU:128, one launch (start us, length us, event | category | flops | bytes accessed | tf_op | source)
XLA Modules:
  0.0 44.6 jit_solution(13562906660500933547)
XLA Ops:
  0.6 2.9 %restrict_and_first_step.1 = (f32[8,6912]{1,0:T(8,128)S(1)}, f32[8,13440]{1,0:T(8,128)S(1)}, f32[8,1152]{1,0:T(8,128)S(1)}, f32[8,13440]{1,0:T(8,128)S(1)}, f32[...) custom-call(s32[4]{0:T(128)} %mask_hbm.1, ...), custom_call_target="tpu_custom_call" | custom-call | tf_op jit(solution)/shard_map/restrict_and_first_step/pallas_call | solution.py:498
  3.6 3.1 %collective-permute-start = (f32[8,6912]{1,0:T(8,128)S(1)}, f32[8,6912]{1,0:T(8,128)S(1)}, u32[]{:S(2)}, u32[]{:S(2)}) collective-permute-start(f32[8,6912]{1,0:T(8,128)S(1)} %get-tuple-element.29), channel_id=1, source_target_pairs={{0,1},{1,0},{2,3},{3,2},{4,5},{5,4},{6,7},{7,6},{8,9},{9,8},{10,11... | collective-permute-start | bytes 663560 | tf_op jit(solution)/shard_map/ppermute | solution.py:515
  6.7 3.6 %collective-permute-start.2 = (f32[8,13440]{1,0:T(8,128)S(1)}, f32[8,13440]{1,0:T(8,128)S(1)}, u32[]{:S(2)}, u32[]{:S(2)}) collective-permute-start(f32[8,13440]{1,0:T(8,128)S(1)} %get-tuple-element.32), channel_id=1, source_target_pairs={{2,4},{4,2},{6,8},{8,6},{10,12},{12,10},{14,16},{16,14},{18,20},{2... | collective-permute-start | bytes 1290248 | tf_op jit(solution)/shard_map/ppermute | solution.py:516
  10.3 0.1 collective-permute-start.3
  10.4 5.2 %collective-permute-start.1 = (f32[8,1152]{1,0:T(8,128)S(1)}, f32[8,1152]{1,0:T(8,128)S(1)}, u32[]{:S(2)}, u32[]{:S(2)}) collective-permute-start(f32[8,1152]{1,0:T(8,128)S(1)} %get-tuple-element.30), channel_id=1, source_target_pairs={{2,5},{3,4},{4,3},{5,2},{6,9},{7,8},{8,7},{9,6},{10,13},{11,12},{1... | collective-permute-start | bytes 110600 | tf_op jit(solution)/shard_map/ppermute | solution.py:517
  15.6 5.5 %collective-permute-done.1.db_one = f32[8,1152]{1,0:T(8,128)S(1)} collective-permute-done((f32[8,1152]{1,0:T(8,128)S(1)}, f32[8,1152]{1,0:T(8,128)S(1)}, u32[]{:S(2)}, u32[]{:S(2)}) %collective-permute-start.1) | collective-permute-done | bytes 36896 | tf_op jit(solution)/shard_map/ppermute | solution.py:517
  21.1 0.0 collective-permute-done.y_one
  21.1 0.0 collective-permute-start.4
  21.1 0.0 collective-permute-done.2.b_one
  21.1 0.0 collective-permute-done.3.a_one
  21.2 1.5 %collective-permute-done.4.ya_one = f32[8,6912]{1,0:T(8,128)S(1)} collective-permute-done((f32[8,6912]{1,0:T(8,128)S(1)}, f32[8,6912]{1,0:T(8,128)S(1)}, u32[]{:S(2)}, u32[]{:S(2)}) %collective-permute-start.4) | collective-permute-done | bytes 221216 | tf_op jit(solution)/shard_map/ppermute | solution.py:520
  22.6 2.0 %two_steps.1 = (f32[8,6144]{1,0:T(8,128)S(1)}, f32[8,11520]{1,0:T(8,128)S(1)}, f32[8,1152]{1,0:T(8,128)S(1)}, f32[8,11520]{1,0:T(8,128)S(1)}, f32[10,8,1536]{2,1...) custom-call(f32[8,6912]{1,0:T(8,128)S(1)} %collective-permute-done.y, ...), custom_call_target="tpu_custom_call" | custom-call | tf_op jit(solution)/shard_map/two_steps/pallas_call | solution.py:498
  24.7 1.8 %collective-permute-start.5 = (f32[8,6144]{1,0:T(8,128)S(1)}, f32[8,6144]{1,0:T(8,128)S(1)}, u32[]{:S(2)}, u32[]{:S(2)}) collective-permute-start(f32[8,6144]{1,0:T(8,128)S(1)} %get-tuple-element.44), channel_id=1, source_target_pairs={{0,1},{1,0},{2,3},{3,2},{4,5},{5,4},{6,7},{7,6},{8,9},{9,8},{10,11... | collective-permute-start | bytes 589832 | tf_op jit(solution)/shard_map/ppermute | solution.py:515
  26.4 4.0 %collective-permute-start.7 = (f32[8,11520]{1,0:T(8,128)S(1)}, f32[8,11520]{1,0:T(8,128)S(1)}, u32[]{:S(2)}, u32[]{:S(2)}) collective-permute-start(f32[8,11520]{1,0:T(8,128)S(1)} %get-tuple-element.47), channel_id=1, source_target_pairs={{2,4},{4,2},{6,8},{8,6},{10,12},{12,10},{14,16},{16,14},{18,20},{2... | collective-permute-start | bytes 1105928 | tf_op jit(solution)/shard_map/ppermute | solution.py:516
  30.5 0.1 collective-permute-start.8
  30.6 6.1 %collective-permute-start.6 = (f32[8,1152]{1,0:T(8,128)S(1)}, f32[8,1152]{1,0:T(8,128)S(1)}, u32[]{:S(2)}, u32[]{:S(2)}) collective-permute-start(f32[8,1152]{1,0:T(8,128)S(1)} %get-tuple-element.45), channel_id=1, source_target_pairs={{2,5},{3,4},{4,3},{5,2},{6,9},{7,8},{8,7},{9,6},{10,13},{11,12},{1... | collective-permute-start | bytes 110600 | tf_op jit(solution)/shard_map/ppermute | solution.py:517
  36.7 4.6 %collective-permute-done.6.db_two = f32[8,1152]{1,0:T(8,128)S(1)} collective-permute-done((f32[8,1152]{1,0:T(8,128)S(1)}, f32[8,1152]{1,0:T(8,128)S(1)}, u32[]{:S(2)}, u32[]{:S(2)}) %collective-permute-start.6) | collective-permute-done | bytes 36896 | tf_op jit(solution)/shard_map/ppermute | solution.py:517
  41.3 0.0 collective-permute-done.5.y_two
  41.3 0.0 collective-permute-start.9
  41.3 0.0 collective-permute-done.7.b_two
  41.3 0.0 collective-permute-done.8.a_two
  41.3 1.4 %collective-permute-done.9.ya_two = f32[8,6144]{1,0:T(8,128)S(1)} collective-permute-done((f32[8,6144]{1,0:T(8,128)S(1)}, f32[8,6144]{1,0:T(8,128)S(1)}, u32[]{:S(2)}, u32[]{:S(2)}) %collective-permute-start.9) | collective-permute-done | bytes 196640 | tf_op jit(solution)/shard_map/ppermute | solution.py:520
  42.7 1.9 %last_steps.1 = (f32[3,4,8,1536]{3,2,1,0:T(8,128)}, f32[3,2,4,768]{3,2,1,0:T(4,128)}) custom-call(f32[8,6144]{1,0:T(8,128)S(1)} %collective-permute-done.5.y_two, f32[8,11520]{1,0:T(8,128)S(1)} %collective-permute-done.7.b_two, f32[8,1152]{1,0:T(8,128)S(1)} %collective-permute-done.6.db_two, f32[8,11520]{1,0:T(8,128)S(1)} %collective-permute-done.8.a_two, ...), custom_call_target="tpu_custom_call" | custom-call | tf_op jit(solution)/shard_map/last_steps/pallas_call | solution.py:498
Async XLA Ops:
  3.6 17.6 %collective-permute-start = (f32[8,6912]{1,0:T(8,128)S(1)}, f32[8,6912]{1,0:T(8,128)S(1)}, u32[]{:S(2)}, u32[]{:S(2)}) collective-permute-start(f32[8,6912]{1,0:T(8,128)S(1)} %get-tuple-element.29), channel_id=1, source_target_pairs={{0,1},{1,0},{2,3},{3,2},{4,5},{5,4},{6,7},{7,6},{8,9},{9,8},{10,11... | collective-permute-start | bytes 663560 | tf_op jit(solution)/shard_map/ppermute | solution.py:515
  6.7 14.5 %collective-permute-start.2 = (f32[8,13440]{1,0:T(8,128)S(1)}, f32[8,13440]{1,0:T(8,128)S(1)}, u32[]{:S(2)}, u32[]{:S(2)}) collective-permute-start(f32[8,13440]{1,0:T(8,128)S(1)} %get-tuple-element.32), channel_id=1, source_target_pairs={{2,4},{4,2},{6,8},{8,6},{10,12},{12,10},{14,16},{16,14},{18,20},{2... | collective-permute-start | bytes 1290248 | tf_op jit(solution)/shard_map/ppermute | solution.py:516
  10.3 10.8 %collective-permute-start.3 = (f32[8,13440]{1,0:T(8,128)S(1)}, f32[8,13440]{1,0:T(8,128)S(1)}, u32[]{:S(2)}, u32[]{:S(2)}) collective-permute-start(f32[8,13440]{1,0:T(8,128)S(1)} %get-tuple-element.34), channel_id=1, source_target_pairs={{0,2},{2,0},{4,6},{6,4},{8,10},{10,8},{12,14},{14,12},{16,18},{18,... | collective-permute-start | bytes 1290248 | tf_op jit(solution)/shard_map/ppermute | solution.py:518
  10.4 10.7 %collective-permute-start.1 = (f32[8,1152]{1,0:T(8,128)S(1)}, f32[8,1152]{1,0:T(8,128)S(1)}, u32[]{:S(2)}, u32[]{:S(2)}) collective-permute-start(f32[8,1152]{1,0:T(8,128)S(1)} %get-tuple-element.30), channel_id=1, source_target_pairs={{2,5},{3,4},{4,3},{5,2},{6,9},{7,8},{8,7},{9,6},{10,13},{11,12},{1... | collective-permute-start | bytes 110600 | tf_op jit(solution)/shard_map/ppermute | solution.py:517
  21.1 1.5 %collective-permute-start.4 = (f32[8,6912]{1,0:T(8,128)S(1)}, f32[8,6912]{1,0:T(8,128)S(1)}, u32[]{:S(2)}, u32[]{:S(2)}) collective-permute-start(f32[8,6912]{1,0:T(8,128)S(1)} %collective-permute-done.y_one), channel_id=1, source_target_pairs={{0,2},{2,0},{4,6},{6,4},{8,10},{10,8},{12,14},{14,12},{16,18},{18,... | collective-permute-start | bytes 663560 | tf_op jit(solution)/shard_map/ppermute | solution.py:520
  24.7 16.6 %collective-permute-start.5 = (f32[8,6144]{1,0:T(8,128)S(1)}, f32[8,6144]{1,0:T(8,128)S(1)}, u32[]{:S(2)}, u32[]{:S(2)}) collective-permute-start(f32[8,6144]{1,0:T(8,128)S(1)} %get-tuple-element.44), channel_id=1, source_target_pairs={{0,1},{1,0},{2,3},{3,2},{4,5},{5,4},{6,7},{7,6},{8,9},{9,8},{10,11... | collective-permute-start | bytes 589832 | tf_op jit(solution)/shard_map/ppermute | solution.py:515
  26.4 14.9 %collective-permute-start.7 = (f32[8,11520]{1,0:T(8,128)S(1)}, f32[8,11520]{1,0:T(8,128)S(1)}, u32[]{:S(2)}, u32[]{:S(2)}) collective-permute-start(f32[8,11520]{1,0:T(8,128)S(1)} %get-tuple-element.47), channel_id=1, source_target_pairs={{2,4},{4,2},{6,8},{8,6},{10,12},{12,10},{14,16},{16,14},{18,20},{2... | collective-permute-start | bytes 1105928 | tf_op jit(solution)/shard_map/ppermute | solution.py:516
  30.5 10.8 %collective-permute-start.8 = (f32[8,11520]{1,0:T(8,128)S(1)}, f32[8,11520]{1,0:T(8,128)S(1)}, u32[]{:S(2)}, u32[]{:S(2)}) collective-permute-start(f32[8,11520]{1,0:T(8,128)S(1)} %get-tuple-element.49), channel_id=1, source_target_pairs={{0,2},{2,0},{4,6},{6,4},{8,10},{10,8},{12,14},{14,12},{16,18},{18,... | collective-permute-start | bytes 1105928 | tf_op jit(solution)/shard_map/ppermute | solution.py:518
  30.6 10.7 %collective-permute-start.6 = (f32[8,1152]{1,0:T(8,128)S(1)}, f32[8,1152]{1,0:T(8,128)S(1)}, u32[]{:S(2)}, u32[]{:S(2)}) collective-permute-start(f32[8,1152]{1,0:T(8,128)S(1)} %get-tuple-element.45), channel_id=1, source_target_pairs={{2,5},{3,4},{4,3},{5,2},{6,9},{7,8},{8,7},{9,6},{10,13},{11,12},{1... | collective-permute-start | bytes 110600 | tf_op jit(solution)/shard_map/ppermute | solution.py:517
  41.3 1.4 %collective-permute-start.9 = (f32[8,6144]{1,0:T(8,128)S(1)}, f32[8,6144]{1,0:T(8,128)S(1)}, u32[]{:S(2)}, u32[]{:S(2)}) collective-permute-start(f32[8,6144]{1,0:T(8,128)S(1)} %collective-permute-done.5.y_two), channel_id=1, source_target_pairs={{0,2},{2,0},{4,6},{6,4},{8,10},{10,8},{12,14},{14,12},{16,18},{18,... | collective-permute-start | bytes 589832 | tf_op jit(solution)/shard_map/ppermute | solution.py:520

commit v3 on v2

--- a/solution.py
+++ b/solution.py
@@ -12,6 +12,7 @@
 ROWS = 8
 FIELDS = 3
 F32 = jnp.float32
+PAD = 128
 
 
 def roll(x, shift, axis):
@@ -119,14 +120,14 @@
     return [(q % 8, base + (q // 8) * half, half)]
 
 
-def corner_fine(f, width):
+def corner_fine(f, width, base=0):
     half = width // 2
-    return [(2 * f + h, 0, half) for h in range(2)]
-
-
-def corner_coarse(f, width):
+    return [(2 * f + h, base, half) for h in range(2)]
+
+
+def corner_coarse(f, width, base=0):
     quarter = width // 4
-    return [(2 * f + h, width // 2, quarter) for h in range(2)]
+    return [(2 * f + h, base + width // 2, quarter) for h in range(2)]
 
 
 def put(buf, pieces, line):
@@ -161,6 +162,7 @@
         return fine(f, z) if f < 6 else stiff(z)
 
     base = 3 * width + (half if with_k else 0)
+    tail = base + 2 * half
     for f in range(fields):
         for z in range(PLANES):
             t = tile(f, z)
@@ -173,6 +175,7 @@
         g = f if f < 3 else (3 if f == 6 else None)
         if g is not None:
             put(db_buf, corner_fine(g, width), jnp.where(odd, line, low_line))
+            put(y_buf, corner_fine(g, width, tail), jnp.where(odd, low_line, line))
 
     for f in range(fields):
         t = coarse(f) if f < 6 else coarse_stiff
@@ -182,10 +185,13 @@
         g = f if f < 3 else (3 if f == 6 else None)
         if g is not None:
             put(db_buf, corner_coarse(g, width), jnp.where(odd, lines[1], lines[0]))
+            put(y_buf, corner_coarse(g, width, tail), jnp.where(odd, lines[0], lines[1]))
+    db_buf[:, half + quarter :] = jnp.zeros((ROWS, db_buf.shape[1] - half - quarter), F32)
     if with_k:
         y_buf[6:8, base + half : base + 2 * half] = zero
     else:
         y_buf[4:8, base + half : base + 2 * half] = jnp.zeros((4, half), F32)
+        y_buf[6:8, tail:] = jnp.zeros((2, half + quarter), F32)
         db_buf[6:8, :] = jnp.zeros((2, db_buf.shape[1]), F32)
 
     at = fields * width
@@ -308,10 +314,9 @@
         return spread(take(self.y, fine_row(f * PLANES + z, self.width)))
 
     def corners(self, f):
-        near = [take(self.ya, fine_row(f * PLANES + z, self.width)) for z in (PLANES - 1, 0)]
-        far = take(self.db, corner_fine(3 if f == 6 else f, self.width))
-        low = jnp.where(self.odd, near[0], far)
-        high = jnp.where(self.odd, far, near[1])
+        pieces = corner_fine(3 if f == 6 else f, self.width)
+        near, far = take(self.ya, pieces), take(self.db, pieces)
+        low, high = jnp.where(self.odd, near, far), jnp.where(self.odd, far, near)
         return spread(low), spread(high)
 
     def coarse_rows(self, f, upper, buf=None):
@@ -320,10 +325,9 @@
         return jnp.where(upper, spread(lines[0]), spread(lines[1]))
 
     def coarse_corner(self, f, upper):
-        near = [take(self.ya, coarse_row(2 * f + zc, self.width, self.base)) for zc in (1, 0)]
-        far = take(self.db, corner_coarse(3 if f == 6 else f, self.width))
-        low = jnp.where(self.odd, near[0], far)
-        high = jnp.where(self.odd, far, near[1])
+        pieces = corner_coarse(3 if f == 6 else f, self.width)
+        near, far = take(self.ya, pieces), take(self.db, pieces)
+        low, high = jnp.where(self.odd, near, far), jnp.where(self.odd, far, near)
         return jnp.where(upper, spread(low), spread(high))
 
     def coarse_planes(self, c, upper):
@@ -506,7 +510,7 @@
     )(*operands)
 
 
-def exchange(bufs):
+def exchange(bufs, corner):
     count = lax.axis_size("ax")
     pair_a = [(i, i ^ 1) for i in range(count)]
     pair_b = [(i, i + 1 if i % 2 else i - 1) for i in range(1, count - 1)]
@@ -516,8 +520,7 @@
     b = lax.ppermute(b, "ax", pair_b)
     db = lax.ppermute(db, ("ax", "xs"), across)
     a = lax.ppermute(a, "ax", pair_a)
-    y, db = lax.optimization_barrier((y, db))
-    ya = lax.ppermute(y, "ax", pair_a)
+    ya = lax.ppermute(y[:, y.shape[1] - corner :], "ax", pair_a)
     return y, b, db, a, ya
 
 
@@ -530,8 +533,8 @@
 
     def buffers(fields, with_k):
         plane = fields * width + 3 * half + (quarter if with_k else 0)
-        rows = 3 * width + (3 * half if with_k else 2 * half)
-        return [struct(ROWS, rows), struct(ROWS, plane), struct(ROWS, half + quarter), struct(ROWS, plane)]
+        rows = 3 * width + (3 * half if with_k else 2 * half) + half + quarter
+        return [struct(ROWS, rows), struct(ROWS, plane), struct(ROWS, half + quarter + PAD), struct(ROWS, plane)]
 
     whole = pltpu.VMEM(field.shape, F32)
     tile = pltpu.VMEM((FIELDS, ROWS, width), F32)
@@ -557,7 +560,7 @@
         ],
         in_space=pltpu.HBM,
     )
-    one = exchange((y, b, db, a))
+    one = exchange((y, b, db, a), half + quarter)
     steps = [whole, whole, tile, tile, small]
     y, b, db, a, halo, coarse_halo, u, w, cu, cw = call(
         middle_kernel,
@@ -567,7 +570,7 @@
         steps,
         one + (coef, force, stiff, now, w, cu, cw, ck, cf),
     )
-    two = exchange((y, b, db, a))
+    two = exchange((y, b, db, a), half + quarter)
     return call(
         end_kernel,
         "last_steps",

time: 45.1 us -> 46.8 us (1.038)
  waiting for transfers between devices: 13 us -> 13.9 us
  starting transfers between devices: 24 us -> 24.7 us
    ppermute x2, waiting for transfers between devices: 0.01 us -> 11.5 us  [exchange(): y = lax.ppermute(y, 'xs', [(0, 1), (1, 0)])]
    ppermute x2, waiting for transfers between devices: 10.1 us -> 0.01 us  [exchange(): db = lax.ppermute(db, ('ax', 'xs'), across)]
    ppermute x2, starting transfers between devices: 11.3 us -> 12.9 us  [exchange(): db = lax.ppermute(db, ('ax', 'xs'), across)]
    ppermute x2, starting transfers between devices: 7.67 us -> 6.75 us  [exchange(): b = lax.ppermute(b, 'ax', pair_b)]
    ppermute x2, waiting for transfers between devices: 2.88 us -> 2.41 us  [exchange(): ya = lax.ppermute(y[:, y.shape[1] - corner:], 'ax', pair_a)]
where the time goes in v3:
time: 46.8 us; the launch traced here: 46.3 us
  starting transfers between devices  24.7 us (53%)
  waiting for transfers between devices  13.9 us (30%)
  Pallas kernels  6.95 us (15%)
  between operations  0.7 us (1%)
    ppermute x2, starting transfers between devices, exchange(): db = lax.ppermute(db, ('ax', 'xs'), across)  12.9 us
    ppermute x2, waiting for transfers between devices, exchange(): y = lax.ppermute(y, 'xs', [(0, 1), (1, 0)])  11.5 us
    pallas_call x3, Pallas kernels, call(): pl.pallas_call(kernel, name=name, out_shape=outs, in_specs=[pl.BlockSpec(...  6.95 us
    ppermute x2, starting transfers between devices, exchange(): b = lax.ppermute(b, 'ax', pair_b)  6.75 us
    ppermute x2, starting transfers between devices, exchange(): y = lax.ppermute(y, 'xs', [(0, 1), (1, 0)])  4.54 us
    ppermute x2, waiting for transfers between devices, exchange(): ya = lax.ppermute(y[:, y.shape[1] - corner:], 'ax', pair_a)  2.41 us
  transfers between devices with their start and end apart: 10, of which 4 were waited for; matrix products, arithmetic and copies ran while one was open for 0% of the time, Pallas kernels for 0%

profile of v3, /device:TPU:128, one launch (start us, length us, event | category | flops | bytes accessed | tf_op | source)
XLA Modules:
  0.0 46.3 jit_solution(17439453422984052625)
XLA Ops:
  0.6 2.9 %restrict_and_first_step.1 = (f32[8,8064]{1,0:T(8,128)S(1)}, f32[8,13440]{1,0:T(8,128)S(1)}, f32[8,1280]{1,0:T(8,128)S(1)}, f32[8,13440]{1,0:T(8,128)S(1)}, f32[...) custom-call(s32[4]{0:T(128)} %mask_hbm.1, ...), custom_call_target="tpu_custom_call" | custom-call | tf_op jit(solution)/shard_map/restrict_and_first_step/pallas_call | solution.py:502
  3.6 4.8 %collective-permute-start.1 = (f32[8,13440]{1,0:T(8,128)S(1)}, f32[8,13440]{1,0:T(8,128)S(1)}, u32[]{:S(2)}, u32[]{:S(2)}) collective-permute-start(f32[8,13440]{1,0:T(8,128)S(1)} %get-tuple-element.26), channel_id=1, source_target_pairs={{2,4},{4,2},{6,8},{8,6},{10,12},{12,10},{14,16},{16,14},{18,20},{2... | collective-permute-start | bytes 1290248 | tf_op jit(solution)/shard_map/ppermute | solution.py:520
  8.4 0.1 collective-permute-start.3
  8.5 2.8 %collective-permute-start = (f32[8,8064]{1,0:T(8,128)S(1)}, f32[8,8064]{1,0:T(8,128)S(1)}, u32[]{:S(2)}, u32[]{:S(2)}) collective-permute-start(f32[8,8064]{1,0:T(8,128)S(1)} %get-tuple-element.25), channel_id=1, source_target_pairs={{0,1},{1,0},{2,3},{3,2},{4,5},{5,4},{6,7},{7,6},{8,9},{9,8},{10,11... | collective-permute-start | bytes 774152 | tf_op jit(solution)/shard_map/ppermute | solution.py:519
  11.3 4.6 %collective-permute-start.2 = (f32[8,1280]{1,0:T(8,128)S(1)}, f32[8,1280]{1,0:T(8,128)S(1)}, u32[]{:S(2)}, u32[]{:S(2)}) collective-permute-start(f32[8,1280]{1,0:T(8,128)S(1)} %get-tuple-element.27), channel_id=1, source_target_pairs={{2,5},{3,4},{4,3},{5,2},{6,9},{7,8},{8,7},{9,6},{10,13},{11,12},{1... | collective-permute-start | bytes 122888 | tf_op jit(solution)/shard_map/ppermute | solution.py:521
  15.9 7.8 %collective-permute-done.y_one = f32[8,8064]{1,0:T(8,128)S(1)} collective-permute-done((f32[8,8064]{1,0:T(8,128)S(1)}, f32[8,8064]{1,0:T(8,128)S(1)}, u32[]{:S(2)}, u32[]{:S(2)}) %collective-permute-start) | collective-permute-done | bytes 258080 | tf_op jit(solution)/shard_map/ppermute | solution.py:519
  23.7 0.0 collective-permute-start.4
  23.7 0.0 collective-permute-done.2.db_one
  23.7 1.2 %collective-permute-done.4.ya_one = f32[8,1152]{1,0:T(8,128)S(1)} collective-permute-done((f32[8,1152]{1,0:T(8,128)S(1)}, f32[8,1152]{1,0:T(8,128)S(1)}, u32[]{:S(2)}, u32[]{:S(2)}) %collective-permute-start.4) | collective-permute-done | bytes 36896 | tf_op jit(solution)/shard_map/ppermute | solution.py:523
  24.9 0.0 collective-permute-done.1.b_one
  24.9 0.0 collective-permute-done.3.a_one
  24.9 2.1 %two_steps.1 = (f32[8,7296]{1,0:T(8,128)S(1)}, f32[8,11520]{1,0:T(8,128)S(1)}, f32[8,1280]{1,0:T(8,128)S(1)}, f32[8,11520]{1,0:T(8,128)S(1)}, f32[10,8,1536]{2,1...) custom-call(f32[8,8064]{1,0:T(8,128)S(1)} %collective-permute-done.y, ...), custom_call_target="tpu_custom_call" | custom-call | tf_op jit(solution)/shard_map/two_steps/pallas_call | solution.py:502
  27.0 1.9 %collective-permute-start.6 = (f32[8,11520]{1,0:T(8,128)S(1)}, f32[8,11520]{1,0:T(8,128)S(1)}, u32[]{:S(2)}, u32[]{:S(2)}) collective-permute-start(f32[8,11520]{1,0:T(8,128)S(1)} %get-tuple-element.39), channel_id=1, source_target_pairs={{2,4},{4,2},{6,8},{8,6},{10,12},{12,10},{14,16},{16,14},{18,20},{2... | collective-permute-start | bytes 1105928 | tf_op jit(solution)/shard_map/ppermute | solution.py:520
  29.0 0.4 collective-permute-start.8
  29.4 1.7 %collective-permute-start.5 = (f32[8,7296]{1,0:T(8,128)S(1)}, f32[8,7296]{1,0:T(8,128)S(1)}, u32[]{:S(2)}, u32[]{:S(2)}) collective-permute-start(f32[8,7296]{1,0:T(8,128)S(1)} %get-tuple-element.38), channel_id=1, source_target_pairs={{0,1},{1,0},{2,3},{3,2},{4,5},{5,4},{6,7},{7,6},{8,9},{9,8},{10,11... | collective-permute-start | bytes 700424 | tf_op jit(solution)/shard_map/ppermute | solution.py:519
  31.1 8.3 %collective-permute-start.7 = (f32[8,1280]{1,0:T(8,128)S(1)}, f32[8,1280]{1,0:T(8,128)S(1)}, u32[]{:S(2)}, u32[]{:S(2)}) collective-permute-start(f32[8,1280]{1,0:T(8,128)S(1)} %get-tuple-element.40), channel_id=1, source_target_pairs={{2,5},{3,4},{4,3},{5,2},{6,9},{7,8},{8,7},{9,6},{10,13},{11,12},{1... | collective-permute-start | bytes 122888 | tf_op jit(solution)/shard_map/ppermute | solution.py:521
  39.4 3.8 %collective-permute-done.5.y_two = f32[8,7296]{1,0:T(8,128)S(1)} collective-permute-done((f32[8,7296]{1,0:T(8,128)S(1)}, f32[8,7296]{1,0:T(8,128)S(1)}, u32[]{:S(2)}, u32[]{:S(2)}) %collective-permute-start.5) | collective-permute-done | bytes 233504 | tf_op jit(solution)/shard_map/ppermute | solution.py:519
  43.1 0.0 collective-permute-start.9
  43.2 0.0 collective-permute-done.7.db_two
  43.2 1.2 %collective-permute-done.9.ya_two = f32[8,1152]{1,0:T(8,128)S(1)} collective-permute-done((f32[8,1152]{1,0:T(8,128)S(1)}, f32[8,1152]{1,0:T(8,128)S(1)}, u32[]{:S(2)}, u32[]{:S(2)}) %collective-permute-start.9) | collective-permute-done | bytes 36896 | tf_op jit(solution)/shard_map/ppermute | solution.py:523
  44.4 0.0 collective-permute-done.6.b_two
  44.4 0.0 collective-permute-done.8.a_two
  44.4 1.9 %last_steps.1 = (f32[3,4,8,1536]{3,2,1,0:T(8,128)}, f32[3,2,4,768]{3,2,1,0:T(4,128)}) custom-call(f32[8,7296]{1,0:T(8,128)S(1)} %collective-permute-done.5.y_two, f32[8,11520]{1,0:T(8,128)S(1)} %collective-permute-done.6.b_two, f32[8,1280]{1,0:T(8,128)S(1)} %collective-permute-done.7.db_two, f32[8,11520]{1,0:T(8,128)S(1)} %collective-permute-done.8.a_two, ...), custom_call_target="tpu_custom_call" | custom-call | tf_op jit(solution)/shard_map/last_steps/pallas_call | solution.py:502
  (2 shorter events, 0.0 us)
Async XLA Ops:
  3.6 21.4 %collective-permute-start.1 = (f32[8,13440]{1,0:T(8,128)S(1)}, f32[8,13440]{1,0:T(8,128)S(1)}, u32[]{:S(2)}, u32[]{:S(2)}) collective-permute-start(f32[8,13440]{1,0:T(8,128)S(1)} %get-tuple-element.26), channel_id=1, source_target_pairs={{2,4},{4,2},{6,8},{8,6},{10,12},{12,10},{14,16},{16,14},{18,20},{2... | collective-permute-start | bytes 1290248 | tf_op jit(solution)/shard_map/ppermute | solution.py:520
  8.4 16.5 %collective-permute-start.3 = (f32[8,13440]{1,0:T(8,128)S(1)}, f32[8,13440]{1,0:T(8,128)S(1)}, u32[]{:S(2)}, u32[]{:S(2)}) collective-permute-start(f32[8,13440]{1,0:T(8,128)S(1)} %get-tuple-element.28), channel_id=1, source_target_pairs={{0,2},{2,0},{4,6},{6,4},{8,10},{10,8},{12,14},{14,12},{16,18},{18,... | collective-permute-start | bytes 1290248 | tf_op jit(solution)/shard_map/ppermute | solution.py:522
  8.5 15.2 %collective-permute-start = (f32[8,8064]{1,0:T(8,128)S(1)}, f32[8,8064]{1,0:T(8,128)S(1)}, u32[]{:S(2)}, u32[]{:S(2)}) collective-permute-start(f32[8,8064]{1,0:T(8,128)S(1)} %get-tuple-element.25), channel_id=1, source_target_pairs={{0,1},{1,0},{2,3},{3,2},{4,5},{5,4},{6,7},{7,6},{8,9},{9,8},{10,11... | collective-permute-start | bytes 774152 | tf_op jit(solution)/shard_map/ppermute | solution.py:519
  11.3 12.4 %collective-permute-start.2 = (f32[8,1280]{1,0:T(8,128)S(1)}, f32[8,1280]{1,0:T(8,128)S(1)}, u32[]{:S(2)}, u32[]{:S(2)}) collective-permute-start(f32[8,1280]{1,0:T(8,128)S(1)} %get-tuple-element.27), channel_id=1, source_target_pairs={{2,5},{3,4},{4,3},{5,2},{6,9},{7,8},{8,7},{9,6},{10,13},{11,12},{1... | collective-permute-start | bytes 122888 | tf_op jit(solution)/shard_map/ppermute | solution.py:521
  23.7 1.2 %collective-permute-start.4 = (f32[8,1152]{1,0:T(8,128)S(1)}, f32[8,1152]{1,0:T(8,128)S(1)}, u32[]{:S(2)}, u32[]{:S(2)}) collective-permute-start(f32[8,1152]{1,0:T(8,128)S(1)} %slice.8), channel_id=1, source_target_pairs={{0,2},{2,0},{4,6},{6,4},{8,10},{10,8},{12,14},{14,12},{16,18},{18,... | collective-permute-start | bytes 110600 | tf_op jit(solution)/shard_map/ppermute | solution.py:523
  27.0 17.3 %collective-permute-start.6 = (f32[8,11520]{1,0:T(8,128)S(1)}, f32[8,11520]{1,0:T(8,128)S(1)}, u32[]{:S(2)}, u32[]{:S(2)}) collective-permute-start(f32[8,11520]{1,0:T(8,128)S(1)} %get-tuple-element.39), channel_id=1, source_target_pairs={{2,4},{4,2},{6,8},{8,6},{10,12},{12,10},{14,16},{16,14},{18,20},{2... | collective-permute-start | bytes 1105928 | tf_op jit(solution)/shard_map/ppermute | solution.py:520
  29.0 15.4 %collective-permute-start.8 = (f32[8,11520]{1,0:T(8,128)S(1)}, f32[8,11520]{1,0:T(8,128)S(1)}, u32[]{:S(2)}, u32[]{:S(2)}) collective-permute-start(f32[8,11520]{1,0:T(8,128)S(1)} %get-tuple-element.41), channel_id=1, source_target_pairs={{0,2},{2,0},{4,6},{6,4},{8,10},{10,8},{12,14},{14,12},{16,18},{18,... | collective-permute-start | bytes 1105928 | tf_op jit(solution)/shard_map/ppermute | solution.py:522
  29.4 13.8 %collective-permute-start.5 = (f32[8,7296]{1,0:T(8,128)S(1)}, f32[8,7296]{1,0:T(8,128)S(1)}, u32[]{:S(2)}, u32[]{:S(2)}) collective-permute-start(f32[8,7296]{1,0:T(8,128)S(1)} %get-tuple-element.38), channel_id=1, source_target_pairs={{0,1},{1,0},{2,3},{3,2},{4,5},{5,4},{6,7},{7,6},{8,9},{9,8},{10,11... | collective-permute-start | bytes 700424 | tf_op jit(solution)/shard_map/ppermute | solution.py:519
  31.1 12.1 %collective-permute-start.7 = (f32[8,1280]{1,0:T(8,128)S(1)}, f32[8,1280]{1,0:T(8,128)S(1)}, u32[]{:S(2)}, u32[]{:S(2)}) collective-permute-start(f32[8,1280]{1,0:T(8,128)S(1)} %get-tuple-element.40), channel_id=1, source_target_pairs={{2,5},{3,4},{4,3},{5,2},{6,9},{7,8},{8,7},{9,6},{10,13},{11,12},{1... | collective-permute-start | bytes 122888 | tf_op jit(solution)/shard_map/ppermute | solution.py:521
  43.1 1.2 %collective-permute-start.9 = (f32[8,1152]{1,0:T(8,128)S(1)}, f32[8,1152]{1,0:T(8,128)S(1)}, u32[]{:S(2)}, u32[]{:S(2)}) collective-permute-start(f32[8,1152]{1,0:T(8,128)S(1)} %slice.9), channel_id=1, source_target_pairs={{0,2},{2,0},{4,6},{6,4},{8,10},{10,8},{12,14},{14,12},{16,18},{18,... | collective-permute-start | bytes 110600 | tf_op jit(solution)/shard_map/ppermute | solution.py:523

commit v4 on v2

--- a/solution.py
+++ b/solution.py
@@ -1,3 +1,5 @@
+import functools
+
 import jax
 import jax.numpy as jnp
 from jax import lax
@@ -308,10 +310,9 @@
         return spread(take(self.y, fine_row(f * PLANES + z, self.width)))
 
     def corners(self, f):
-        near = [take(self.ya, fine_row(f * PLANES + z, self.width)) for z in (PLANES - 1, 0)]
-        far = take(self.db, corner_fine(3 if f == 6 else f, self.width))
-        low = jnp.where(self.odd, near[0], far)
-        high = jnp.where(self.odd, far, near[1])
+        pieces = corner_fine(3 if f == 6 else f, self.width)
+        near, far = take(self.ya, pieces), take(self.db, pieces)
+        low, high = jnp.where(self.odd, near, far), jnp.where(self.odd, far, near)
         return spread(low), spread(high)
 
     def coarse_rows(self, f, upper, buf=None):
@@ -320,10 +321,9 @@
         return jnp.where(upper, spread(lines[0]), spread(lines[1]))
 
     def coarse_corner(self, f, upper):
-        near = [take(self.ya, coarse_row(2 * f + zc, self.width, self.base)) for zc in (1, 0)]
-        far = take(self.db, corner_coarse(3 if f == 6 else f, self.width))
-        low = jnp.where(self.odd, near[0], far)
-        high = jnp.where(self.odd, far, near[1])
+        pieces = corner_coarse(3 if f == 6 else f, self.width)
+        near, far = take(self.ya, pieces), take(self.db, pieces)
+        low, high = jnp.where(self.odd, near, far), jnp.where(self.odd, far, near)
         return jnp.where(upper, spread(low), spread(high))
 
     def coarse_planes(self, c, upper):
@@ -506,7 +506,33 @@
     )(*operands)
 
 
-def exchange(bufs):
+def corner_kernel(width, with_k, y_ref, out_ref):
+    odd = place()[0]
+    base = 3 * width + (width // 2 if with_k else 0)
+    for g in range(4 if with_k else 3):
+        f = 6 if g == 3 else g
+        fine = [take(y_ref, fine_row(f * PLANES + z, width)) for z in (0, PLANES - 1)]
+        coarse = [take(y_ref, coarse_row(2 * f + zc, width, base)) for zc in range(2)]
+        put(out_ref, corner_fine(g, width), jnp.where(odd, fine[0], fine[1]))
+        put(out_ref, corner_coarse(g, width), jnp.where(odd, coarse[0], coarse[1]))
+    if not with_k:
+        out_ref[6:8, :] = jnp.zeros((2, out_ref.shape[1]), F32)
+
+
+def corner_lines(y, width, with_k):
+    vmem = pl.BlockSpec(memory_space=pltpu.VMEM)
+    return pl.pallas_call(
+        functools.partial(corner_kernel, width, with_k),
+        name="corner_lines",
+        out_shape=struct(ROWS, width // 2 + width // 4),
+        in_specs=[vmem],
+        out_specs=vmem,
+        cost_estimate=pl.CostEstimate(flops=2_000_000_000, bytes_accessed=1024, transcendentals=0),
+        compiler_params=pltpu.CompilerParams(vmem_limit_bytes=16 * 1024 * 1024),
+    )(y)
+
+
+def exchange(bufs, width, with_k):
     count = lax.axis_size("ax")
     pair_a = [(i, i ^ 1) for i in range(count)]
     pair_b = [(i, i + 1 if i % 2 else i - 1) for i in range(1, count - 1)]
@@ -516,8 +542,7 @@
     b = lax.ppermute(b, "ax", pair_b)
     db = lax.ppermute(db, ("ax", "xs"), across)
     a = lax.ppermute(a, "ax", pair_a)
-    y, db = lax.optimization_barrier((y, db))
-    ya = lax.ppermute(y, "ax", pair_a)
+    ya = lax.ppermute(corner_lines(y, width, with_k), "ax", pair_a)
     return y, b, db, a, ya
 
 
@@ -557,7 +582,7 @@
         ],
         in_space=pltpu.HBM,
     )
-    one = exchange((y, b, db, a))
+    one = exchange((y, b, db, a), width, True)
     steps = [whole, whole, tile, tile, small]
     y, b, db, a, halo, coarse_halo, u, w, cu, cw = call(
         middle_kernel,
@@ -567,7 +592,7 @@
         steps,
         one + (coef, force, stiff, now, w, cu, cw, ck, cf),
     )
-    two = exchange((y, b, db, a))
+    two = exchange((y, b, db, a), width, False)
     return call(
         end_kernel,
         "last_steps",

time: 45.1 us -> 42 us (0.931)
  waiting for transfers between devices: 13 us -> 9.86 us
    ppermute x2, waiting for transfers between devices: 2.88 us -> 0.01 us  [exchange(): ya = lax.ppermute(corner_lines(y, width, with_k), 'ax', pair_a)]
  transfers between devices with their start and end apart: 10 -> 10, of which waited for: 4 -> 2; matrix products, arithmetic and copies ran while one was open for 0% -> 0% of each run, Pallas kernels for 0% -> 0%
where the time goes in v4:
time: 42 us; the launch traced here: 41.7 us
  starting transfers between devices  24.2 us (58%)
  waiting for transfers between devices  9.86 us (23%)
  Pallas kernels  6.92 us (16%)
  between operations  0.75 us (2%)
    ppermute x2, starting transfers between devices, exchange(): db = lax.ppermute(db, ('ax', 'xs'), across)  11.3 us
    ppermute x2, waiting for transfers between devices, exchange(): db = lax.ppermute(db, ('ax', 'xs'), across)  9.83 us
    ppermute x2, starting transfers between devices, exchange(): b = lax.ppermute(b, 'ax', pair_b)  7.67 us
    pallas_call x3, Pallas kernels, call(): pl.pallas_call(kernel, name=name, out_shape=outs, in_specs=[pl.BlockSpec(...  6.87 us
    ppermute x2, starting transfers between devices, exchange(): y = lax.ppermute(y, 'xs', [(0, 1), (1, 0)])  4.9 us
  transfers between devices with their start and end apart: 10, of which 2 were waited for; matrix products, arithmetic and copies ran while one was open for 0% of the time, Pallas kernels for 0%

profile of v4, /device:TPU:128, one launch (start us, length us, event | category | flops | bytes accessed | tf_op | source)
XLA Modules:
  0.0 41.7 jit_solution(15754953660319907750)
XLA Ops:
  0.6 2.9 %restrict_and_first_step.1 = (f32[8,6912]{1,0:T(8,128)S(1)}, f32[8,13440]{1,0:T(8,128)S(1)}, f32[8,1152]{1,0:T(8,128)S(1)}, f32[8,13440]{1,0:T(8,128)S(1)}, f32[...) custom-call(s32[4]{0:T(128)} %mask_hbm.1, ...), custom_call_target="tpu_custom_call" | custom-call | tf_op jit(solution)/shard_map/restrict_and_first_step/pallas_call | solution.py:498
  3.5 3.1 %collective-permute-start = (f32[8,6912]{1,0:T(8,128)S(1)}, f32[8,6912]{1,0:T(8,128)S(1)}, u32[]{:S(2)}, u32[]{:S(2)}) collective-permute-start(f32[8,6912]{1,0:T(8,128)S(1)} %get-tuple-element.25), channel_id=1, source_target_pairs={{0,1},{1,0},{2,3},{3,2},{4,5},{5,4},{6,7},{7,6},{8,9},{9,8},{10,11... | collective-permute-start | bytes 663560 | tf_op jit(solution)/shard_map/ppermute | solution.py:541
  6.6 3.6 %collective-permute-start.1 = (f32[8,13440]{1,0:T(8,128)S(1)}, f32[8,13440]{1,0:T(8,128)S(1)}, u32[]{:S(2)}, u32[]{:S(2)}) collective-permute-start(f32[8,13440]{1,0:T(8,128)S(1)} %get-tuple-element.26), channel_id=1, source_target_pairs={{2,4},{4,2},{6,8},{8,6},{10,12},{12,10},{14,16},{16,14},{18,20},{2... | collective-permute-start | bytes 1290248 | tf_op jit(solution)/shard_map/ppermute | solution.py:542
  10.3 0.1 collective-permute-start.3
  10.4 5.2 %collective-permute-start.2 = (f32[8,1152]{1,0:T(8,128)S(1)}, f32[8,1152]{1,0:T(8,128)S(1)}, u32[]{:S(2)}, u32[]{:S(2)}) collective-permute-start(f32[8,1152]{1,0:T(8,128)S(1)} %get-tuple-element.27), channel_id=1, source_target_pairs={{2,5},{3,4},{4,3},{5,2},{6,9},{7,8},{8,7},{9,6},{10,13},{11,12},{1... | collective-permute-start | bytes 110600 | tf_op jit(solution)/shard_map/ppermute | solution.py:543
  15.6 0.0 collective-permute-done.y_ref.y_one
  15.6 0.1 collective-permute-start.4
  15.7 5.4 %collective-permute-done.2.db_one = f32[8,1152]{1,0:T(8,128)S(1)} collective-permute-done((f32[8,1152]{1,0:T(8,128)S(1)}, f32[8,1152]{1,0:T(8,128)S(1)}, u32[]{:S(2)}, u32[]{:S(2)}) %collective-permute-start.2) | collective-permute-done | bytes 36896 | tf_op jit(solution)/shard_map/ppermute | solution.py:543
  21.1 0.0 collective-permute-done.4.ya_one
  21.1 0.0 collective-permute-done.1.b_one
  21.1 0.0 collective-permute-done.3.a_one
  21.1 2.0 %two_steps.1 = (f32[8,6144]{1,0:T(8,128)S(1)}, f32[8,11520]{1,0:T(8,128)S(1)}, f32[8,1152]{1,0:T(8,128)S(1)}, f32[8,11520]{1,0:T(8,128)S(1)}, f32[10,8,1536]{2,1...) custom-call(f32[8,6912]{1,0:T(8,128)S(1)} %collective-permute-done.y, ...), custom_call_target="tpu_custom_call" | custom-call | tf_op jit(solution)/shard_map/two_steps/pallas_call | solution.py:498
  23.2 1.8 %collective-permute-start.5 = (f32[8,6144]{1,0:T(8,128)S(1)}, f32[8,6144]{1,0:T(8,128)S(1)}, u32[]{:S(2)}, u32[]{:S(2)}) collective-permute-start(f32[8,6144]{1,0:T(8,128)S(1)} %get-tuple-element.38), channel_id=1, source_target_pairs={{0,1},{1,0},{2,3},{3,2},{4,5},{5,4},{6,7},{7,6},{8,9},{9,8},{10,11... | collective-permute-start | bytes 589832 | tf_op jit(solution)/shard_map/ppermute | solution.py:541
  24.9 4.0 %collective-permute-start.6 = (f32[8,11520]{1,0:T(8,128)S(1)}, f32[8,11520]{1,0:T(8,128)S(1)}, u32[]{:S(2)}, u32[]{:S(2)}) collective-permute-start(f32[8,11520]{1,0:T(8,128)S(1)} %get-tuple-element.39), channel_id=1, source_target_pairs={{2,4},{4,2},{6,8},{8,6},{10,12},{12,10},{14,16},{16,14},{18,20},{2... | collective-permute-start | bytes 1105928 | tf_op jit(solution)/shard_map/ppermute | solution.py:542
  29.0 0.1 collective-permute-start.8
  29.1 6.1 %collective-permute-start.7 = (f32[8,1152]{1,0:T(8,128)S(1)}, f32[8,1152]{1,0:T(8,128)S(1)}, u32[]{:S(2)}, u32[]{:S(2)}) collective-permute-start(f32[8,1152]{1,0:T(8,128)S(1)} %get-tuple-element.40), channel_id=1, source_target_pairs={{2,5},{3,4},{4,3},{5,2},{6,9},{7,8},{8,7},{9,6},{10,13},{11,12},{1... | collective-permute-start | bytes 110600 | tf_op jit(solution)/shard_map/ppermute | solution.py:543
  35.2 0.0 collective-permute-done.5.y_ref.y_two
  35.2 0.1 collective-permute-start.9
  35.3 4.5 %collective-permute-done.7.db_two = f32[8,1152]{1,0:T(8,128)S(1)} collective-permute-done((f32[8,1152]{1,0:T(8,128)S(1)}, f32[8,1152]{1,0:T(8,128)S(1)}, u32[]{:S(2)}, u32[]{:S(2)}) %collective-permute-start.7) | collective-permute-done | bytes 36896 | tf_op jit(solution)/shard_map/ppermute | solution.py:543
  39.8 0.0 collective-permute-done.9.ya_two
  39.8 0.0 collective-permute-done.6.b_two
  39.8 0.0 collective-permute-done.8.a_two
  39.8 1.9 %last_steps.1 = (f32[3,4,8,1536]{3,2,1,0:T(8,128)}, f32[3,2,4,768]{3,2,1,0:T(4,128)}) custom-call(f32[8,6144]{1,0:T(8,128)S(1)} %collective-permute-done.5.y_ref.y_two, f32[8,11520]{1,0:T(8,128)S(1)} %collective-permute-done.6.b_two, f32[8,1152]{1,0:T(8,128)S(1)} %collective-permute-done.7.db_two, f32[8,11520]{1,0:T(8,128)S(1)} %collective-permute-done.8.a_two, ...), custom_call_target="tpu_custom_call" | custom-call | tf_op jit(solution)/shard_map/last_steps/pallas_call | solution.py:498
  (2 shorter events, 0.1 us)
Async XLA Ops:
  3.5 12.0 %collective-permute-start = (f32[8,6912]{1,0:T(8,128)S(1)}, f32[8,6912]{1,0:T(8,128)S(1)}, u32[]{:S(2)}, u32[]{:S(2)}) collective-permute-start(f32[8,6912]{1,0:T(8,128)S(1)} %get-tuple-element.25), channel_id=1, source_target_pairs={{0,1},{1,0},{2,3},{3,2},{4,5},{5,4},{6,7},{7,6},{8,9},{9,8},{10,11... | collective-permute-start | bytes 663560 | tf_op jit(solution)/shard_map/ppermute | solution.py:541
  6.6 14.5 %collective-permute-start.1 = (f32[8,13440]{1,0:T(8,128)S(1)}, f32[8,13440]{1,0:T(8,128)S(1)}, u32[]{:S(2)}, u32[]{:S(2)}) collective-permute-start(f32[8,13440]{1,0:T(8,128)S(1)} %get-tuple-element.26), channel_id=1, source_target_pairs={{2,4},{4,2},{6,8},{8,6},{10,12},{12,10},{14,16},{16,14},{18,20},{2... | collective-permute-start | bytes 1290248 | tf_op jit(solution)/shard_map/ppermute | solution.py:542
  10.3 10.8 %collective-permute-start.3 = (f32[8,13440]{1,0:T(8,128)S(1)}, f32[8,13440]{1,0:T(8,128)S(1)}, u32[]{:S(2)}, u32[]{:S(2)}) collective-permute-start(f32[8,13440]{1,0:T(8,128)S(1)} %get-tuple-element.28), channel_id=1, source_target_pairs={{0,2},{2,0},{4,6},{6,4},{8,10},{10,8},{12,14},{14,12},{16,18},{18,... | collective-permute-start | bytes 1290248 | tf_op jit(solution)/shard_map/ppermute | solution.py:544
  10.4 10.7 %collective-permute-start.2 = (f32[8,1152]{1,0:T(8,128)S(1)}, f32[8,1152]{1,0:T(8,128)S(1)}, u32[]{:S(2)}, u32[]{:S(2)}) collective-permute-start(f32[8,1152]{1,0:T(8,128)S(1)} %get-tuple-element.27), channel_id=1, source_target_pairs={{2,5},{3,4},{4,3},{5,2},{6,9},{7,8},{8,7},{9,6},{10,13},{11,12},{1... | collective-permute-start | bytes 110600 | tf_op jit(solution)/shard_map/ppermute | solution.py:543
  15.6 5.5 %collective-permute-start.4 = (f32[8,1152]{1,0:T(8,128)S(1)}, f32[8,1152]{1,0:T(8,128)S(1)}, u32[]{:S(2)}, u32[]{:S(2)}) collective-permute-start(f32[8,1152]{1,0:T(8,128)S(1)} %corner_lines.2), channel_id=1, source_target_pairs={{0,2},{2,0},{4,6},{6,4},{8,10},{10,8},{12,14},{14,12},{16,18},{18,... | collective-permute-start | bytes 110600 | tf_op jit(solution)/shard_map/ppermute | solution.py:545
  23.2 12.0 %collective-permute-start.5 = (f32[8,6144]{1,0:T(8,128)S(1)}, f32[8,6144]{1,0:T(8,128)S(1)}, u32[]{:S(2)}, u32[]{:S(2)}) collective-permute-start(f32[8,6144]{1,0:T(8,128)S(1)} %get-tuple-element.38), channel_id=1, source_target_pairs={{0,1},{1,0},{2,3},{3,2},{4,5},{5,4},{6,7},{7,6},{8,9},{9,8},{10,11... | collective-permute-start | bytes 589832 | tf_op jit(solution)/shard_map/ppermute | solution.py:541
  24.9 14.9 %collective-permute-start.6 = (f32[8,11520]{1,0:T(8,128)S(1)}, f32[8,11520]{1,0:T(8,128)S(1)}, u32[]{:S(2)}, u32[]{:S(2)}) collective-permute-start(f32[8,11520]{1,0:T(8,128)S(1)} %get-tuple-element.39), channel_id=1, source_target_pairs={{2,4},{4,2},{6,8},{8,6},{10,12},{12,10},{14,16},{16,14},{18,20},{2... | collective-permute-start | bytes 1105928 | tf_op jit(solution)/shard_map/ppermute | solution.py:542
  29.0 10.8 %collective-permute-start.8 = (f32[8,11520]{1,0:T(8,128)S(1)}, f32[8,11520]{1,0:T(8,128)S(1)}, u32[]{:S(2)}, u32[]{:S(2)}) collective-permute-start(f32[8,11520]{1,0:T(8,128)S(1)} %get-tuple-element.41), channel_id=1, source_target_pairs={{0,2},{2,0},{4,6},{6,4},{8,10},{10,8},{12,14},{14,12},{16,18},{18,... | collective-permute-start | bytes 1105928 | tf_op jit(solution)/shard_map/ppermute | solution.py:544
  29.1 10.7 %collective-permute-start.7 = (f32[8,1152]{1,0:T(8,128)S(1)}, f32[8,1152]{1,0:T(8,128)S(1)}, u32[]{:S(2)}, u32[]{:S(2)}) collective-permute-start(f32[8,1152]{1,0:T(8,128)S(1)} %get-tuple-element.40), channel_id=1, source_target_pairs={{2,5},{3,4},{4,3},{5,2},{6,9},{7,8},{8,7},{9,6},{10,13},{11,12},{1... | collective-permute-start | bytes 110600 | tf_op jit(solution)/shard_map/ppermute | solution.py:543
  35.2 4.6 %collective-permute-start.9 = (f32[8,1152]{1,0:T(8,128)S(1)}, f32[8,1152]{1,0:T(8,128)S(1)}, u32[]{:S(2)}, u32[]{:S(2)}) collective-permute-start(f32[8,1152]{1,0:T(8,128)S(1)} %corner_lines.3), channel_id=1, source_target_pairs={{0,2},{2,0},{4,6},{6,4},{8,10},{10,8},{12,14},{14,12},{16,18},{18,... | collective-permute-start | bytes 110600 | tf_op jit(solution)/shard_map/ppermute | solution.py:545

commit v5 on v2

v5 whole, which is shorter than its diff:
```python
import functools

import jax
import jax.numpy as jnp
from jax import lax
from jax.experimental import pallas as pl
from jax.experimental.pallas import tpu as pltpu
from jax.sharding import PartitionSpec as P

TIME_SQUARE = 0.12
FINE_FACE = 0.5 * TIME_SQUARE
COARSE_FACE = 0.25 * 0.5 * TIME_SQUARE
PLANES = 4
ROWS = 8
FIELDS = 3
F32 = jnp.float32
PAD = 128


def roll(x, shift, axis):
    return pltpu.roll(x, shift % x.shape[axis], axis)


def place():
    i = lax.axis_index("ax")
    odd = lax.rem(i, 2) == 1
    has_far = jnp.logical_and(i > 0, i < lax.axis_size("ax") - 1)

    def plane(n, count=PLANES):
        return jnp.where(odd, count - 1 - n, n)

    return lax.axis_index("xs") == 0, has_far, plane


def iota(shape, dim):
    return lax.broadcasted_iota(jnp.int32, shape, dim)


def stiff_coefs(k, face, low_y, high_y, outer_row):
    width = k.shape[1]
    lane = iota(k.shape, 1)
    last = lane == width - 1
    start = lane == 0
    kp = jnp.where(last, 0.0, roll(k, -1, 1))
    km = jnp.where(start, 0.0, roll(k, 1, 1))
    full_p = face * (k + kp)
    full_m = face * (k + km)
    cyp = jnp.where(high_y, face * (k + roll(k, -1, 0)), 0.0)
    cym = jnp.where(low_y, face * (k + roll(k, 1, 0)), 0.0)
    edge = jnp.where(outer_row, face * k, 0.0)
    centre = 2.0 - (full_p + full_m + cyp + cym + edge)
    return jnp.where(last, 0.0, full_p), jnp.where(start, 0.0, full_m), cyp, cym, centre


def fine_coefs(k_ref, first, coef):
    shape = k_ref.shape[1:]
    row = iota(shape, 0)
    for z in range(PLANES - 1):
        coef[5, z] = FINE_FACE * (k_ref[z] + k_ref[z + 1])
    for z in range(PLANES):
        cxp, cxm, cyp, cym, centre = stiff_coefs(
            k_ref[z], FINE_FACE, row > 0, row < ROWS - 1, row == jnp.where(first, 0, ROWS - 1)
        )
        if z > 0:
            centre = centre - coef[5, z - 1]
        if z < PLANES - 1:
            centre = centre - coef[5, z]
        coef[0, z] = cxp
        coef[1, z] = cxm
        coef[2, z] = cyp
        coef[3, z] = cym
        coef[4, z] = centre


def fine_free(field, before, z, coef, drive_term):
    u = field(z)
    acc = coef[4, z] * u - before
    acc = acc + coef[0, z] * roll(u, -1, 1) + coef[1, z] * roll(u, 1, 1)
    acc = acc + coef[2, z] * roll(u, -1, 0) + coef[3, z] * roll(u, 1, 0)
    if z > 0:
        acc = acc + coef[5, z - 1] * field(z - 1)
    if z < PLANES - 1:
        acc = acc + coef[5, z] * field(z + 1)
    return acc + drive_term


def coarse_coefs(k, first):
    row = iota(k.shape, 0)
    inner = lax.rem(row, 4)
    cxp, cxm, cyp, cym, centre = stiff_coefs(
        k, COARSE_FACE, inner > 0, inner < 3, inner == jnp.where(first, 0, 3)
    )
    cz = COARSE_FACE * (k + roll(k, 4, 0))
    return cxp, cxm, cyp, cym, centre - cz, cz


def coarse_free(u, before, coefs, force):
    cxp, cxm, cyp, cym, centre, cz = coefs
    return (
        centre * u
        - before
        + cxp * roll(u, -1, 1)
        + cxm * roll(u, 1, 1)
        + cyp * roll(u, -1, 0)
        + cym * roll(u, 1, 0)
        + cz * roll(u, 4, 0)
        + force
    )


def group_drive(compartment, drive_ref, c):
    value = jnp.full(compartment.shape, drive_ref[c, 0], F32)
    for g in range(1, drive_ref.shape[1]):
        value = jnp.where(compartment == g, drive_ref[c, g], value)
    return value


def fine_row(r, width):
    if r < 24:
        return [(r % 8, (r // 8) * width, width)]
    half = width // 2
    return [(2 * (r - 24) + h, 3 * width, half) for h in range(2)]


def coarse_row(q, width, base):
    half = width // 2
    return [(q % 8, base + (q // 8) * half, half)]


def corner_fine(f, width):
    half = width // 2
    return [(2 * f + h, 0, half) for h in range(2)]


def corner_coarse(f, width):
    quarter = width // 4
    return [(2 * f + h, width // 2, quarter) for h in range(2)]


def put(buf, pieces, line):
    at = 0
    for row, lane, lanes in pieces:
        buf[row : row + 1, lane : lane + lanes] = line[:, at : at + lanes]
        at += lanes


def take(buf, pieces):
    parts = [buf[row : row + 1, lane : lane + lanes] for row, lane, lanes in pieces]
    return parts[0] if len(parts) == 1 else jnp.concatenate(parts, axis=1)


def spread(line, rows=ROWS):
    return jnp.broadcast_to(line, (rows, line.shape[1]))


def edge_line(tile, top_half, base=0, rows=ROWS):
    return jnp.where(top_half, tile[base + rows - 1 : base + rows], tile[base : base + 1])


def pack(top_half, fine, coarse, stiff, coarse_stiff, a_buf, b_buf, y_buf, db_buf, width):
    half = width // 2
    quarter = width // 4
    with_k = stiff is not None
    fields = 7 if with_k else 6
    upper = iota((ROWS, half), 0) < 4
    base = 3 * width + (half if with_k else 0)
    for f in range(fields):
        for z in range(PLANES):
            t = fine(f, z) if f < 6 else stiff(z)
            line = edge_line(t, top_half)
            put(y_buf, fine_row(f * PLANES + z, width), line)
            if z == 0:
                b_buf[:, f * width : (f + 1) * width] = t
                if f < 3 or f == 6:
                    put(db_buf, corner_fine(min(f, 3), width), line)
            if z == PLANES - 1:
                a_buf[:, f * width : (f + 1) * width] = t

    for f in range(fields):
        t = coarse(f) if f < 6 else coarse_stiff
        for zc in range(2):
            line = edge_line(t, top_half, 4 * zc, 4)
            put(y_buf, coarse_row(2 * f + zc, width, base), line)
            if zc == 0 and (f < 3 or f == 6):
                put(db_buf, corner_coarse(min(f, 3), width), line)
    db_buf[:, half + quarter :] = jnp.zeros((ROWS, db_buf.shape[1] - half - quarter), F32)
    if with_k:
        y_buf[6:8, base + half : base + 2 * half] = jnp.zeros((2, half), F32)
    else:
        y_buf[4:8, base + half : base + 2 * half] = jnp.zeros((4, half), F32)
        db_buf[6:8, :] = jnp.zeros((2, db_buf.shape[1]), F32)

    at = fields * width
    for c in range(FIELDS):
        first, second = coarse(c), coarse(c + 3)
        b_buf[:, at : at + half] = jnp.where(upper, first, roll(second, 4, 0))
        a_buf[:, at : at + half] = jnp.where(upper, roll(first, 4, 0), second)
        at += half
    if with_k:
        some = iota((ROWS, quarter), 0) < 4
        for buf, k in ((b_buf, coarse_stiff), (a_buf, roll(coarse_stiff, 4, 0))):
            buf[:, at : at + quarter] = jnp.where(some, k[:, :quarter], roll(k[:, quarter:], 4, 0))


def begin_kernel(
    mask_hbm, drive_hbm, comp_hbm, stiff_hbm, now_hbm, before_hbm,
    y_buf, b_buf, db_buf, a_buf, now, stiff, coef, force, w_out, cu_out, cw_out, ck_out, cf_out,
    mask, drive, comp, before, group, wide, sems,
):
    top_half, _, plane = place()
    pairs = [(drive_hbm, drive), (mask_hbm, mask), (comp_hbm, comp)]
    pairs += [(stiff_hbm.at[plane(n)], stiff.at[n]) for n in range(PLANES)]
    pairs += [(now_hbm.at[:, plane(n)], now.at[:, n]) for n in range(PLANES)]
    pairs += [(before_hbm.at[:, plane(n)], before.at[:, n]) for n in range(PLANES)]
    copies = [pltpu.make_async_copy(src, dst, sems.at[n]) for n, (src, dst) in enumerate(pairs)]
    for copy in copies:
        copy.start()
    width = stiff.shape[2]
    half = width // 2
    row = iota((ROWS, width), 0)
    even_row = lax.rem(row, 2) == 0

    for copy in copies[:3]:
        copy.wait()
    on = [mask[plane(n)].astype(F32) for n in range(PLANES)]
    for c in range(FIELDS):
        group[c] = group_drive(comp[...], drive, c)
    for c in range(FIELDS):
        for z in range(PLANES):
            force[c, z] = group[c] * (TIME_SQUARE * on[z])
    for copy in copies[3 : 3 + PLANES]:
        copy.wait()
    fine_coefs(stiff, top_half, coef)
    for copy in copies[3 + PLANES :]:
        copy.wait()

    def pooled(first, second):
        first = first + roll(first, -1, 0)
        second = second + roll(second, -1, 0)
        return jnp.where(even_row, first, roll(second, 1, 0))

    tiles = []
    for c in range(FIELDS):
        tiles.append(pooled(now[c, 0] + now[c, 1], now[c, 2] + now[c, 3]))
    for c in range(FIELDS):
        tiles.append(pooled(before[c, 0] + before[c, 1], before[c, 2] + before[c, 3]))
    tiles.append(pooled(stiff[0] + stiff[1], stiff[2] + stiff[3]))
    for c in range(FIELDS):
        tiles.append(pooled(group[c], group[c]))
    stacked = jnp.concatenate(tiles, axis=0)
    pool = jnp.where(iota((256, 128), 0) // 2 == iota((256, 128), 1), 0.125, 0.0)
    for q in range(width // 256):
        wide[q] = lax.dot_general(
            stacked[:, q * 256 : (q + 1) * 256], pool, (((1,), (0,)), ((), ())),
            precision=lax.Precision.HIGHEST, preferred_element_type=F32,
        )

    def coarse_tile(f):
        planes = [
            jnp.concatenate([wide[q, pl.ds(8 * f + zc, 4, stride=2), :] for q in range(half // 128)], axis=1)
            for zc in range(2)
        ]
        return jnp.concatenate(planes, axis=0)

    upper = iota((ROWS, half), 0) < 4
    weight = jnp.where(upper, on[0] + on[1], on[2] + on[3]) * TIME_SQUARE
    ck_out[...] = coarse_tile(6)
    coefs = coarse_coefs(ck_out[...], top_half)
    for c in range(FIELDS):
        cu_out[c] = coarse_tile(c)
        cf_out[c] = coarse_tile(7 + c) * weight
        cw_out[c] = coarse_free(cu_out[c], coarse_tile(3 + c), coefs, cf_out[c])

    for c in range(FIELDS):
        for z in range(PLANES):
            w_out[c, z] = fine_free(lambda n: now[c, n], before[c, z], z, coef, force[c, z])
    pack(
        top_half,
        lambda f, z: now[f, z] if f < 3 else w_out[f - 3, z],
        lambda f: cu_out[f] if f < 3 else cw_out[f - 3],
        lambda z: stiff[z], ck_out[...],
        a_buf, b_buf, y_buf, db_buf, width,
    )


class Got:
    def __init__(self, with_k, width, y=None, a=None, ya=None, b=None, db=None):
        self.y, self.a, self.ya, self.b, self.db = y, a, ya, b, db
        self.width = width
        self.fields = 7 if with_k else 6
        self.base = 3 * width + (width // 2 if with_k else 0)

    def plane(self, buf, f):
        return buf[:, f * self.width : (f + 1) * self.width]

    def rows(self, f, z):
        return spread(take(self.y, fine_row(f * PLANES + z, self.width)))

    def corner(self, buf, f):
        return spread(take(buf, corner_fine(min(f, 3), self.width)))

    def coarse_rows(self, f, upper):
        lines = [take(self.y, coarse_row(2 * f + zc, self.width, self.base)) for zc in range(2)]
        return jnp.where(upper, spread(lines[0]), spread(lines[1]))

    def coarse_corner(self, f, upper):
        pieces = corner_coarse(min(f, 3), self.width)
        return jnp.where(upper, spread(take(self.db, pieces)), spread(take(self.ya, pieces)))

    def coarse_planes(self, c, upper):
        half = self.width // 2
        at = self.fields * self.width + c * half
        low, high = self.b[:, at : at + half], self.a[:, at : at + half]
        return (
            jnp.where(upper, low, roll(high, 4, 0)),
            jnp.where(upper, roll(low, 4, 0), high),
        )

    def coarse_stiff_planes(self, upper):
        quarter = self.width // 4
        at = self.fields * self.width + 2 * quarter * FIELDS
        low, high = self.b[:, at : at + quarter], self.a[:, at : at + quarter]
        return jnp.where(
            upper,
            jnp.concatenate([low, roll(low, 4, 0)], axis=1),
            jnp.concatenate([roll(high, 4, 0), high], axis=1),
        )


LAST = PLANES - 1


def near_faces(got, stiff, halo, top_half):
    edge = iota(stiff.shape[1:], 0) == jnp.where(top_half, ROWS - 1, 0)
    for z in range(PLANES):
        halo[z] = jnp.where(edge, FINE_FACE * (stiff[z] + got.rows(6, z)), 0.0)
    k, kd = got.plane(got.a, 6), got.corner(got.ya, 6)
    halo[4] = FINE_FACE * (stiff[LAST] + k)
    halo[5] = jnp.where(edge, FINE_FACE * (k + kd), 0.0)
    halo[6] = FINE_FACE * (got.rows(6, LAST) + kd)


def far_faces(got, stiff, halo, top_half):
    edge = iota(stiff.shape[1:], 0) == jnp.where(top_half, ROWS - 1, 0)
    k, kd = got.plane(got.b, 6), got.corner(got.db, 6)
    halo[0] = FINE_FACE * (stiff[0] + k)
    halo[1] = jnp.where(edge, FINE_FACE * (k + kd), 0.0)
    halo[2] = FINE_FACE * (got.rows(6, 0) + kd)


def coarse_faces(got, ck, halo, top_half, has_far):
    row = iota(ck.shape, 0)
    upper = row < 4
    edge = lax.rem(row, 4) == jnp.where(top_half, 3, 0)
    k = ck[...]
    kz, ky, kd = got.coarse_stiff_planes(upper), got.coarse_rows(6, upper), got.coarse_corner(6, upper)
    halo[0] = COARSE_FACE * (k + kz)
    halo[1] = jnp.where(edge, COARSE_FACE * (k + ky), 0.0)
    halo[2] = jnp.where(edge, COARSE_FACE * (kz + kd), 0.0)
    halo[3] = COARSE_FACE * (ky + kd)
    halo[4] = jnp.where(upper, jnp.where(has_far, 1.0, 0.0), 1.0)


def early(got, coef, halo, force, now, free, mid, mid_y, mid_a, part):
    for c in range(FIELDS):
        for z in range(PLANES):
            u = now[c, z]
            u_y = got.rows(c, z)
            flux = halo[z] * (u_y - u)
            new = free[c, z] + flux
            new_y = got.rows(3 + c, z) - flux
            if z == LAST:
                other, corner = got.plane(got.a, c), got.corner(got.ya, c)
                flux = halo[4] * (other - u)
                new = new + flux
                mid_a[c] = got.plane(got.a, 3 + c) - flux + halo[5] * (corner - other)
                new_y = new_y + halo[6] * (corner - u_y)
            mid[c, z] = new
            mid_y[c, z] = new_y
        for z in (2, 3):
            u = mid[c, z]
            new = fine_free(lambda n: mid[c, n], now[c, z], z, coef, force[c, z])
            new = new + halo[z] * (mid_y[c, z] - u)
            if z == LAST:
                new = new + halo[4] * (mid_a[c] - u)
            part[c, z - 2] = new


def late(got, coef, near, far, force, now, mid, mid_y, first, emit, has_far):
    for c in range(FIELDS):
        u = now[c, 0]
        other, corner = got.plane(got.b, c), got.corner(got.db, c)
        flux = far[0] * (other - u)
        first[c] = mid[c, 0] + flux
        beyond = got.plane(got.b, 3 + c) - flux + far[1] * (corner - other)
        beyond = jnp.where(has_far, beyond, 0.0)
        new_y = mid_y[c, 0] + far[2] * (corner - got.rows(c, 0))

        def field(n):
            return first[c] if n == 0 else mid[c, n]

        u = first[c]
        new = fine_free(field, now[c, 0], 0, coef, force[c, 0])
        emit(c, 0, new + near[0] * (new_y - u) + far[0] * (beyond - u))
        new = fine_free(field, now[c, 1], 1, coef, force[c, 1])
        emit(c, 1, new + near[1] * (mid_y[c, 1] - mid[c, 1]))


def coarse_steps(got, halo, cu_now, cu_free, ck, cf, top_half, emit):
    upper = iota(cf.shape[1:], 0) < 4
    face_z, face_y, face_zd, face_yd, inside = [halo[n] for n in range(5)]
    coefs = coarse_coefs(ck[...], top_half)
    for c in range(FIELDS):
        u = cu_now[c]
        u_z, w_z = got.coarse_planes(c, upper)
        u_y = got.coarse_rows(c, upper)
        u_d = got.coarse_corner(c, upper)
        flux_z = face_z * (u_z - u)
        flux_y = face_y * (u_y - u)
        new = cu_free[c] + flux_z + flux_y
        new_z = inside * (w_z - flux_z + face_zd * (u_d - u_z))
        new_y = got.coarse_rows(3 + c, upper) - flux_y + face_yd * (u_d - u_y)
        after = coarse_free(new, u, coefs, cf[c])
        emit(c, new, after + face_z * (new_z - new) + face_y * (new_y - new), coefs)


def early_two_kernel(
    y, a, ya, coef, force, stiff, now, free,
    halo, mid, mid_y, part, w_part,
    mid_a,
):
    got = Got(True, stiff.shape[2], y=y, a=a, ya=ya)
    near_faces(got, stiff, halo, place()[0])
    early(got, coef, halo, force, now, free, mid, mid_y, mid_a, part)
    for c in range(FIELDS):
        w_part[c] = fine_free(lambda n: part[c, n - 2], mid[c, LAST], LAST, coef, force[c, LAST])


def late_two_kernel(
    y, b, db, a, ya, coef, force, stiff, now, near, mid, mid_y, part, w_part, cu_now, cu_free, ck, cf,
    y_buf, b_buf, db_buf, a_buf, far, coarse_halo, u_out, w_out, cu_out, cw_out,
    first,
):
    top_half, has_far, _ = place()
    got = Got(True, stiff.shape[2], y=y, a=a, ya=ya, b=b, db=db)
    far_faces(got, stiff, far, top_half)
    coarse_faces(got, ck, coarse_halo, top_half, has_far)

    def emit(c, z, value):
        u_out[c, z] = value

    def emit_coarse(c, before, value, coefs):
        cu_out[c] = value
        cw_out[c] = coarse_free(value, before, coefs, cf[c])

    late(got, coef, near, far, force, now, mid, mid_y, first, emit, has_far)
    coarse_steps(got, coarse_halo, cu_now, cu_free, ck, cf, top_half, emit_coarse)
    for c in range(FIELDS):
        for z in (2, 3):
            u_out[c, z] = part[c, z - 2]
        w_out[c, LAST] = w_part[c]
        for z in range(LAST):
            before = first[c] if z == 0 else mid[c, z]
            w_out[c, z] = fine_free(lambda n: u_out[c, n], before, z, coef, force[c, z])
    pack(
        top_half,
        lambda f, z: u_out[f, z] if f < 3 else w_out[f - 3, z],
        lambda f: cu_out[f] if f < 3 else cw_out[f - 3],
        None, None, a_buf, b_buf, y_buf, db_buf, stiff.shape[2],
    )


def early_last_kernel(
    y, a, ya, coef, force, halo, now, free,
    mid, mid_y, part,
    mid_a,
):
    got = Got(False, coef.shape[3], y=y, a=a, ya=ya)
    early(got, coef, halo, force, now, free, mid, mid_y, mid_a, part)


def late_last_kernel(
    y, b, db, a, ya, coef, force, now, near, far, mid, mid_y, part, cu_now, cu_free, ck, cf, coarse_halo,
    u_hbm, cu_hbm,
    first, last, coarse_last, sems,
):
    top_half, has_far, plane = place()
    got = Got(False, coef.shape[3], y=y, a=a, ya=ya, b=b, db=db)
    copies = []

    def send(src, dst):
        copies.append(pltpu.make_async_copy(src, dst, sems.at[len(copies)]))
        copies[-1].start()

    for z in (2, 3):
        send(part.at[:, z - 2], u_hbm.at[:, plane(z)])

    def emit(c, z, value):
        last[c, z] = value
        send(last.at[c, z], u_hbm.at[c, plane(z)])

    def emit_coarse(c, before, value, coefs):
        for zc in range(2):
            coarse_last[c, zc] = value[4 * zc : 4 * zc + 4]

    coarse_steps(got, coarse_halo, cu_now, cu_free, ck, cf, top_half, emit_coarse)
    for zc in range(2):
        send(coarse_last.at[:, zc], cu_hbm.at[:, plane(zc, 2)])
    late(got, coef, near, far, force, now, mid, mid_y, first, emit, has_far)
    for copy in copies:
        copy.wait()


def struct(*shape):
    return jax.ShapeDtypeStruct(shape, F32)


def call(kernel, name, outs, scratch, operands, in_space=pltpu.VMEM, out_space=pltpu.VMEM, flops=None):
    estimate = None
    if flops is not None:
        estimate = pl.CostEstimate(flops=flops, bytes_accessed=1024, transcendentals=0)
    return pl.pallas_call(
        kernel,
        name=name,
        out_shape=outs,
        in_specs=[pl.BlockSpec(memory_space=in_space)] * len(operands),
        out_specs=[pl.BlockSpec(memory_space=out_space)] * len(outs),
        scratch_shapes=scratch,
        cost_estimate=estimate,
        compiler_params=pltpu.CompilerParams(vmem_limit_bytes=32 * 1024 * 1024),
    )(*operands)


def corner_kernel(width, with_k, y_ref, out_ref):
    base = 3 * width + (width // 2 if with_k else 0)
    for g in range(4 if with_k else 3):
        f = 6 if g == 3 else g
        put(out_ref, corner_fine(g, width), take(y_ref, fine_row(f * PLANES + LAST, width)))
        put(out_ref, corner_coarse(g, width), take(y_ref, coarse_row(2 * f + 1, width, base)))
    if not with_k:
        out_ref[6:8, :] = jnp.zeros((2, out_ref.shape[1]), F32)


def exchange(bufs, width, with_k):
    count = lax.axis_size("ax")
    pair_a = [(i, i ^ 1) for i in range(count)]
    pair_b = [(i, i + 1 if i % 2 else i - 1) for i in range(1, count - 1)]
    across = [(2 * i + s, 2 * j + 1 - s) for i, j in pair_b for s in (0, 1)]
    y, b, db, a = bufs
    y = lax.ppermute(y, "xs", [(0, 1), (1, 0)])
    b = lax.ppermute(b, "ax", pair_b)
    db = lax.ppermute(db, ("ax", "xs"), across)
    a = lax.ppermute(a, "ax", pair_a)
    kernel = functools.partial(corner_kernel, width, with_k)
    (line,) = call(kernel, "corner_lines", [struct(ROWS, width // 2 + width // 4)], [], (y,), flops=CORNER_FLOPS)
    ya = lax.ppermute(line, "ax", pair_a)
    return y, b, db, a, ya


CORNER_FLOPS = 2_000_000_000
EARLY_FLOPS = 1


def local(displacement, previous, stiffness, tissue_mask, compartment, drive):
    width = displacement.shape[3]
    half = width // 2
    quarter = width // 4
    field = struct(FIELDS, PLANES, ROWS, width)
    coarse = struct(FIELDS, ROWS, half)
    part = struct(FIELDS, 2, ROWS, width)
    tile = struct(FIELDS, ROWS, width)

    def buffers(fields, with_k):
        plane = fields * width + 3 * half + (quarter if with_k else 0)
        rows = 3 * width + (3 * half if with_k else 2 * half)
        return [struct(ROWS, rows), struct(ROWS, plane), struct(ROWS, half + quarter + PAD), struct(ROWS, plane)]

    scratch_tile = pltpu.VMEM(tile.shape, F32)
    y, b, db, a, now, stiff, coef, force, w, cu, cw, ck, cf = call(
        begin_kernel,
        "restrict_and_first_step",
        buffers(7, True)
        + [field, struct(*stiffness.shape), struct(6, PLANES, ROWS, width), field, field]
        + [coarse, coarse, struct(ROWS, half), coarse],
        [
            pltpu.SMEM(tissue_mask.shape, jnp.int32),
            pltpu.SMEM(drive.shape, F32),
            pltpu.VMEM(compartment.shape, jnp.int32),
            pltpu.VMEM(field.shape, F32),
            scratch_tile,
            pltpu.VMEM((half // 128, 10 * ROWS, 128), F32),
            pltpu.SemaphoreType.DMA((3 + 3 * PLANES,)),
        ],
        [
            pltpu.with_memory_space_constraint(x, pltpu.HBM)
            for x in (tissue_mask, drive, compartment, stiffness, displacement, previous)
        ],
        in_space=pltpu.HBM,
    )
    y, b, db, a, ya = exchange((y, b, db, a), width, True)
    near, mid, mid_y, done, w_done = call(
        early_two_kernel,
        "early_two_steps",
        [struct(7, ROWS, width), field, field, part, tile],
        [scratch_tile],
        (y, a, ya, coef, force, stiff, now, w),
        flops=EARLY_FLOPS,
    )
    y, b, db, a, far, coarse_halo, u, w, cu, cw = call(
        late_two_kernel,
        "late_two_steps",
        buffers(6, False) + [struct(3, ROWS, width), struct(5, ROWS, half), field, field, coarse, coarse],
        [scratch_tile],
        (y, b, db, a, ya, coef, force, stiff, now, near, mid, mid_y, done, w_done, cu, cw, ck, cf),
    )
    y, b, db, a, ya = exchange((y, b, db, a), width, False)
    mid, mid_y, done = call(
        early_last_kernel,
        "early_last_steps",
        [field, field, part],
        [scratch_tile],
        (y, a, ya, coef, force, near, u, w),
        flops=EARLY_FLOPS,
    )
    return call(
        late_last_kernel,
        "late_last_steps",
        [field, struct(FIELDS, 2, 4, half)],
        [
            scratch_tile,
            pltpu.VMEM(part.shape, F32),
            pltpu.VMEM((FIELDS, 2, 4, half), F32),
            pltpu.SemaphoreType.DMA((10,)),
        ],
        (y, b, db, a, ya, coef, force, u, near, far, mid, mid_y, done, cu, cw, ck, cf, coarse_halo),
        out_space=pltpu.HBM,
    )


def solution(mesh):
    placed = (
        P(None, "ax", "xs", None),
        P(None, "ax", "xs", None),
        P("ax", "xs", None),
        P("ax"),
        P("xs", None),
        P(),
    )

    def run(*args):
        return tuple(local(*args))

    return jax.shard_map(
        run,
        mesh=mesh,
        in_specs=placed,
        out_specs=(P(None, "ax", "xs", None), P(None, "ax", "xs", None)),
        check_vma=False,
    )
```

time: 45.1 us -> 41.7 us (0.925)
  waiting for transfers between devices: 13 us -> 9.01 us
    ppermute x2, waiting for transfers between devices: 10.1 us -> 6.6 us  [exchange(): db = lax.ppermute(db, ('ax', 'xs'), across)]
    ppermute x2, starting transfers between devices: 7.67 us -> 8.9 us  [exchange(): b = lax.ppermute(b, 'ax', pair_b)]
    ppermute x2, starting transfers between devices: 4.9 us -> 4.05 us  [exchange(): y = lax.ppermute(y, 'xs', [(0, 1), (1, 0)])]
    ppermute x2, waiting for transfers between devices: 2.88 us -> 2.4 us  [exchange(): ya = lax.ppermute(line, 'ax', pair_a)]
    pallas_call x3 -> x7, Pallas kernels: 6.84 us -> 7.08 us  [call(): pl.pallas_call(kernel, name=name, out_shape=outs, in_specs=[pl.BlockSpec(...]
  transfers between devices with their start and end apart: 10 -> 10, of which waited for: 4 -> 4; matrix products, arithmetic and copies ran while one was open for 0% -> 0% of each run, Pallas kernels for 0% -> 3%
where the time goes in v5:
time: 41.7 us; the launch traced here: 40.9 us
  starting transfers between devices  24 us (58%)
  waiting for transfers between devices  9.01 us (22%)
  Pallas kernels  7.08 us (17%)
  between operations  0.74 us (2%)
    ppermute x2, starting transfers between devices, exchange(): db = lax.ppermute(db, ('ax', 'xs'), across)  10.9 us
    ppermute x2, starting transfers between devices, exchange(): b = lax.ppermute(b, 'ax', pair_b)  8.9 us
    pallas_call x7, Pallas kernels, call(): pl.pallas_call(kernel, name=name, out_shape=outs, in_specs=[pl.BlockSpec(...  7.08 us
    ppermute x2, waiting for transfers between devices, exchange(): db = lax.ppermute(db, ('ax', 'xs'), across)  6.6 us
    ppermute x2, starting transfers between devices, exchange(): y = lax.ppermute(y, 'xs', [(0, 1), (1, 0)])  4.05 us
    ppermute x2, waiting for transfers between devices, exchange(): ya = lax.ppermute(line, 'ax', pair_a)  2.4 us
  transfers between devices with their start and end apart: 10, of which 4 were waited for; matrix products, arithmetic and copies ran while one was open for 0% of the time, Pallas kernels for 3%

profile of v5, /device:TPU:128, one launch (start us, length us, event | category | flops | bytes accessed | tf_op | source)
XLA Modules:
  0.0 40.9 jit_solution(11089960060247172731)
XLA Ops:
  0.6 3.0 %restrict_and_first_step.1 = (f32[8,6912]{1,0:T(8,128)S(1)}, f32[8,13440]{1,0:T(8,128)S(1)}, f32[8,1280]{1,0:T(8,128)S(1)}, f32[8,13440]{1,0:T(8,128)S(1)}, f32[...) custom-call(s32[4]{0:T(128)} %mask_hbm.1, ...), custom_call_target="tpu_custom_call" | custom-call | tf_op jit(solution)/shard_map/restrict_and_first_step/pallas_call | solution.py:522
  3.7 3.1 %collective-permute-start = (f32[8,6912]{1,0:T(8,128)S(1)}, f32[8,6912]{1,0:T(8,128)S(1)}, u32[]{:S(2)}, u32[]{:S(2)}) collective-permute-start(f32[8,6912]{1,0:T(8,128)S(1)} %get-tuple-element.33), channel_id=1, source_target_pairs={{0,1},{1,0},{2,3},{3,2},{4,5},{5,4},{6,7},{7,6},{8,9},{9,8},{10,11... | collective-permute-start | bytes 663560 | tf_op jit(solution)/shard_map/ppermute | solution.py:550
  6.8 0.0 collective-permute-start.3
  6.8 4.6 %collective-permute-start.1 = (f32[8,13440]{1,0:T(8,128)S(1)}, f32[8,13440]{1,0:T(8,128)S(1)}, u32[]{:S(2)}, u32[]{:S(2)}) collective-permute-start(f32[8,13440]{1,0:T(8,128)S(1)} %get-tuple-element.34), channel_id=1, source_target_pairs={{2,4},{4,2},{6,8},{8,6},{10,12},{12,10},{14,16},{16,14},{18,20},{2... | collective-permute-start | bytes 1290248 | tf_op jit(solution)/shard_map/ppermute | solution.py:551
  11.4 4.2 %collective-permute-start.2 = (f32[8,1280]{1,0:T(8,128)S(1)}, f32[8,1280]{1,0:T(8,128)S(1)}, u32[]{:S(2)}, u32[]{:S(2)}) collective-permute-start(f32[8,1280]{1,0:T(8,128)S(1)} %get-tuple-element.35), channel_id=1, source_target_pairs={{2,5},{3,4},{4,3},{5,2},{6,9},{7,8},{8,7},{9,6},{10,13},{11,12},{1... | collective-permute-start | bytes 122888 | tf_op jit(solution)/shard_map/ppermute | solution.py:552
  15.6 0.0 collective-permute-done.y_ref.y
  15.6 0.1 collective-permute-start.4
  15.8 1.2 %collective-permute-done.4.ya = f32[8,1152]{1,0:T(8,128)S(1)} collective-permute-done((f32[8,1152]{1,0:T(8,128)S(1)}, f32[8,1152]{1,0:T(8,128)S(1)}, u32[]{:S(2)}, u32[]{:S(2)}) %collective-permute-start.4) | collective-permute-done | bytes 36896 | tf_op jit(solution)/shard_map/ppermute | solution.py:556
  17.0 0.0 collective-permute-done.3.a
  17.0 0.7 %early_two_steps.1 = (f32[7,8,1536]{2,1,0:T(8,128)S(1)}, f32[3,4,8,1536]{3,2,1,0:T(8,128)S(1)}, f32[3,4,8,1536]{3,2,1,0:T(8,128)S(1)}, f32[3,2,8,1536]{3,2,1,0:T(8,128)S(1)}, f32[3,8,1536]{2,1,0:T(8,128)S(1)}) custom-call(f32[8,6912]{1,0:T(8,128)S(1)} %collective-permute-done.y_ref.y, f32[8,13440]{1,0:T(8,128)S(1)} %collective-permute-done.3.a, ...), custom_call_target="tpu_custom_call" | custom-call | flops 1 | bytes 1024 | tf_op jit(solution)/shard_map/early_two_steps/pallas_call | solution.py:522
  17.7 4.5 %collective-permute-done.2.db = f32[8,1280]{1,0:T(8,128)S(1)} collective-permute-done((f32[8,1280]{1,0:T(8,128)S(1)}, f32[8,1280]{1,0:T(8,128)S(1)}, u32[]{:S(2)}, u32[]{:S(2)}) %collective-permute-start.2) | collective-permute-done | bytes 40992 | tf_op jit(solution)/shard_map/ppermute | solution.py:552
  22.1 0.0 collective-permute-done.1.b
  22.1 1.4 %late_two_steps.1 = (f32[8,6144]{1,0:T(8,128)S(1)}, f32[8,11520]{1,0:T(8,128)S(1)}, f32[8,1280]{1,0:T(8,128)S(1)}, f32[8,11520]{1,0:T(8,128)S(1)}, f32[3,8,1536]...) custom-call(f32[8,6912]{1,0:T(8,128)S(1)} %collective-permute-done.y, ...), custom_call_target="tpu_custom_call" | custom-call | tf_op jit(solution)/shard_map/late_two_steps/pallas_call | solution.py:522
  23.5 0.9 %collective-permute-start.5 = (f32[8,6144]{1,0:T(8,128)S(1)}, f32[8,6144]{1,0:T(8,128)S(1)}, u32[]{:S(2)}, u32[]{:S(2)}) collective-permute-start(f32[8,6144]{1,0:T(8,128)S(1)} %get-tuple-element.51), channel_id=1, source_target_pairs={{0,1},{1,0},{2,3},{3,2},{4,5},{5,4},{6,7},{7,6},{8,9},{9,8},{10,11... | collective-permute-start | bytes 589832 | tf_op jit(solution)/shard_map/ppermute | solution.py:550
  24.5 0.0 collective-permute-start.8
  24.5 4.3 %collective-permute-start.6 = (f32[8,11520]{1,0:T(8,128)S(1)}, f32[8,11520]{1,0:T(8,128)S(1)}, u32[]{:S(2)}, u32[]{:S(2)}) collective-permute-start(f32[8,11520]{1,0:T(8,128)S(1)} %get-tuple-element.52), channel_id=1, source_target_pairs={{2,4},{4,2},{6,8},{8,6},{10,12},{12,10},{14,16},{16,14},{18,20},{2... | collective-permute-start | bytes 1105928 | tf_op jit(solution)/shard_map/ppermute | solution.py:551
  28.8 6.7 %collective-permute-start.7 = (f32[8,1280]{1,0:T(8,128)S(1)}, f32[8,1280]{1,0:T(8,128)S(1)}, u32[]{:S(2)}, u32[]{:S(2)}) collective-permute-start(f32[8,1280]{1,0:T(8,128)S(1)} %get-tuple-element.53), channel_id=1, source_target_pairs={{2,5},{3,4},{4,3},{5,2},{6,9},{7,8},{8,7},{9,6},{10,13},{11,12},{1... | collective-permute-start | bytes 122888 | tf_op jit(solution)/shard_map/ppermute | solution.py:552
  35.5 0.0 collective-permute-done.5.y_ref.y
  35.5 0.1 collective-permute-start.9
  35.6 1.2 %collective-permute-done.9.ya = f32[8,1152]{1,0:T(8,128)S(1)} collective-permute-done((f32[8,1152]{1,0:T(8,128)S(1)}, f32[8,1152]{1,0:T(8,128)S(1)}, u32[]{:S(2)}, u32[]{:S(2)}) %collective-permute-start.9) | collective-permute-done | bytes 36896 | tf_op jit(solution)/shard_map/ppermute | solution.py:556
  36.8 0.0 collective-permute-done.8.a
  36.8 0.6 %early_last_steps.1 = (f32[3,4,8,1536]{3,2,1,0:T(8,128)S(1)}, f32[3,4,8,1536]{3,2,1,0:T(8,128)S(1)}, f32[3,2,8,1536]{3,2,1,0:T(8,128)S(1)}) custom-call(f32[8,6144]{1,0:T(8,128)S(1)} %collective-permute-done.5.y_ref.y, f32[8,11520]{1,0:T(8,128)S(1)} %collective-permute-done.8.a, f32[8,1152]{1,0:T(8,128)S(1)} %collective-permute-done.9.ya, ...), custom_call_target="tpu_custom_call" | custom-call | flops 1 | bytes 1024 | tf_op jit(solution)/shard_map/early_last_steps/pallas_call | solution.py:522
  37.4 2.1 %collective-permute-done.7.db = f32[8,1280]{1,0:T(8,128)S(1)} collective-permute-done((f32[8,1280]{1,0:T(8,128)S(1)}, f32[8,1280]{1,0:T(8,128)S(1)}, u32[]{:S(2)}, u32[]{:S(2)}) %collective-permute-start.7) | collective-permute-done | bytes 40992 | tf_op jit(solution)/shard_map/ppermute | solution.py:552
  39.5 1.3 %late_last_steps.1 = (f32[3,4,8,1536]{3,2,1,0:T(8,128)}, f32[3,2,4,768]{3,2,1,0:T(4,128)}) custom-call(f32[8,6144]{1,0:T(8,128)S(1)} %collective-permute-done.5.y_ref.y, f32[8,11520]{1,0:T(8,128)S(1)} %collective-permute-done.6.b, f32[8,1280]{1,0:T(8,128)S(1)} %collective-permute-done.7.db, f32[8,11520]{1,0:T(8,128)S(1)} %collective-permute-done.8.a, ...), custom_call_target="tpu_custom_call" | custom-call | tf_op jit(solution)/shard_map/late_last_steps/pallas_call | solution.py:522
  (3 shorter events, 0.0 us)
Async XLA Ops:
  3.7 11.9 %collective-permute-start = (f32[8,6912]{1,0:T(8,128)S(1)}, f32[8,6912]{1,0:T(8,128)S(1)}, u32[]{:S(2)}, u32[]{:S(2)}) collective-permute-start(f32[8,6912]{1,0:T(8,128)S(1)} %get-tuple-element.33), channel_id=1, source_target_pairs={{0,1},{1,0},{2,3},{3,2},{4,5},{5,4},{6,7},{7,6},{8,9},{9,8},{10,11... | collective-permute-start | bytes 663560 | tf_op jit(solution)/shard_map/ppermute | solution.py:550
  6.8 10.2 %collective-permute-start.3 = (f32[8,13440]{1,0:T(8,128)S(1)}, f32[8,13440]{1,0:T(8,128)S(1)}, u32[]{:S(2)}, u32[]{:S(2)}) collective-permute-start(f32[8,13440]{1,0:T(8,128)S(1)} %get-tuple-element.36), channel_id=1, source_target_pairs={{0,2},{2,0},{4,6},{6,4},{8,10},{10,8},{12,14},{14,12},{16,18},{18,... | collective-permute-start | bytes 1290248 | tf_op jit(solution)/shard_map/ppermute | solution.py:553
  6.8 15.4 %collective-permute-start.1 = (f32[8,13440]{1,0:T(8,128)S(1)}, f32[8,13440]{1,0:T(8,128)S(1)}, u32[]{:S(2)}, u32[]{:S(2)}) collective-permute-start(f32[8,13440]{1,0:T(8,128)S(1)} %get-tuple-element.34), channel_id=1, source_target_pairs={{2,4},{4,2},{6,8},{8,6},{10,12},{12,10},{14,16},{16,14},{18,20},{2... | collective-permute-start | bytes 1290248 | tf_op jit(solution)/shard_map/ppermute | solution.py:551
  11.4 10.8 %collective-permute-start.2 = (f32[8,1280]{1,0:T(8,128)S(1)}, f32[8,1280]{1,0:T(8,128)S(1)}, u32[]{:S(2)}, u32[]{:S(2)}) collective-permute-start(f32[8,1280]{1,0:T(8,128)S(1)} %get-tuple-element.35), channel_id=1, source_target_pairs={{2,5},{3,4},{4,3},{5,2},{6,9},{7,8},{8,7},{9,6},{10,13},{11,12},{1... | collective-permute-start | bytes 122888 | tf_op jit(solution)/shard_map/ppermute | solution.py:552
  15.6 1.3 %collective-permute-start.4 = (f32[8,1152]{1,0:T(8,128)S(1)}, f32[8,1152]{1,0:T(8,128)S(1)}, u32[]{:S(2)}, u32[]{:S(2)}) collective-permute-start(f32[8,1152]{1,0:T(8,128)S(1)} %corner_lines.2), channel_id=1, source_target_pairs={{0,2},{2,0},{4,6},{6,4},{8,10},{10,8},{12,14},{14,12},{16,18},{18,... | collective-permute-start | bytes 110600 | tf_op jit(solution)/shard_map/ppermute | solution.py:556
  23.5 11.9 %collective-permute-start.5 = (f32[8,6144]{1,0:T(8,128)S(1)}, f32[8,6144]{1,0:T(8,128)S(1)}, u32[]{:S(2)}, u32[]{:S(2)}) collective-permute-start(f32[8,6144]{1,0:T(8,128)S(1)} %get-tuple-element.51), channel_id=1, source_target_pairs={{0,1},{1,0},{2,3},{3,2},{4,5},{5,4},{6,7},{7,6},{8,9},{9,8},{10,11... | collective-permute-start | bytes 589832 | tf_op jit(solution)/shard_map/ppermute | solution.py:550
  24.5 12.3 %collective-permute-start.8 = (f32[8,11520]{1,0:T(8,128)S(1)}, f32[8,11520]{1,0:T(8,128)S(1)}, u32[]{:S(2)}, u32[]{:S(2)}) collective-permute-start(f32[8,11520]{1,0:T(8,128)S(1)} %get-tuple-element.54), channel_id=1, source_target_pairs={{0,2},{2,0},{4,6},{6,4},{8,10},{10,8},{12,14},{14,12},{16,18},{18,... | collective-permute-start | bytes 1105928 | tf_op jit(solution)/shard_map/ppermute | solution.py:553
  24.5 15.1 %collective-permute-start.6 = (f32[8,11520]{1,0:T(8,128)S(1)}, f32[8,11520]{1,0:T(8,128)S(1)}, u32[]{:S(2)}, u32[]{:S(2)}) collective-permute-start(f32[8,11520]{1,0:T(8,128)S(1)} %get-tuple-element.52), channel_id=1, source_target_pairs={{2,4},{4,2},{6,8},{8,6},{10,12},{12,10},{14,16},{16,14},{18,20},{2... | collective-permute-start | bytes 1105928 | tf_op jit(solution)/shard_map/ppermute | solution.py:551
  28.8 10.8 %collective-permute-start.7 = (f32[8,1280]{1,0:T(8,128)S(1)}, f32[8,1280]{1,0:T(8,128)S(1)}, u32[]{:S(2)}, u32[]{:S(2)}) collective-permute-start(f32[8,1280]{1,0:T(8,128)S(1)} %get-tuple-element.53), channel_id=1, source_target_pairs={{2,5},{3,4},{4,3},{5,2},{6,9},{7,8},{8,7},{9,6},{10,13},{11,12},{1... | collective-permute-start | bytes 122888 | tf_op jit(solution)/shard_map/ppermute | solution.py:552
  35.5 1.3 %collective-permute-start.9 = (f32[8,1152]{1,0:T(8,128)S(1)}, f32[8,1152]{1,0:T(8,128)S(1)}, u32[]{:S(2)}, u32[]{:S(2)}) collective-permute-start(f32[8,1152]{1,0:T(8,128)S(1)} %corner_lines.3), channel_id=1, source_target_pairs={{0,2},{2,0},{4,6},{6,4},{8,10},{10,8},{12,14},{14,12},{16,18},{18,... | collective-permute-start | bytes 110600 | tf_op jit(solution)/shard_map/ppermute | solution.py:556

commit v6 on v5

--- a/solution.py
+++ b/solution.py
@@ -15,6 +15,7 @@
 FIELDS = 3
 F32 = jnp.float32
 PAD = 128
+PAD_B = 128
 
 
 def roll(x, shift, axis):
@@ -183,6 +184,7 @@
             put(y_buf, coarse_row(2 * f + zc, width, base), line)
             if zc == 0 and (f < 3 or f == 6):
                 put(db_buf, corner_coarse(min(f, 3), width), line)
+    b_buf[:, a_buf.shape[1] :] = jnp.zeros((ROWS, b_buf.shape[1] - a_buf.shape[1]), F32)
     db_buf[:, half + quarter :] = jnp.zeros((ROWS, db_buf.shape[1] - half - quarter), F32)
     if with_k:
         y_buf[6:8, base + half : base + 2 * half] = jnp.zeros((2, half), F32)
@@ -248,12 +250,20 @@
     for c in range(FIELDS):
         tiles.append(pooled(group[c], group[c]))
     stacked = jnp.concatenate(tiles, axis=0)
-    pool = jnp.where(iota((256, 128), 0) // 2 == iota((256, 128), 1), 0.125, 0.0)
+    parts = []
+    rest = stacked
+    for _ in range(3):
+        parts.append(rest.astype(jnp.bfloat16))
+        rest = rest - parts[-1].astype(F32)
+    stacked = jnp.concatenate(parts, axis=0)
+    pool = jnp.where(iota((256, 128), 0) // 2 == iota((256, 128), 1), 0.125, 0.0).astype(jnp.bfloat16)
+    count = 10 * ROWS
     for q in range(width // 256):
-        wide[q] = lax.dot_general(
+        sums = lax.dot_general(
             stacked[:, q * 256 : (q + 1) * 256], pool, (((1,), (0,)), ((), ())),
-            precision=lax.Precision.HIGHEST, preferred_element_type=F32,
+            preferred_element_type=F32,
         )
+        wide[q] = sums[:count] + (sums[count : 2 * count] + sums[2 * count :])
 
     def coarse_tile(f):
         planes = [
@@ -573,7 +583,7 @@
     def buffers(fields, with_k):
         plane = fields * width + 3 * half + (quarter if with_k else 0)
         rows = 3 * width + (3 * half if with_k else 2 * half)
-        return [struct(ROWS, rows), struct(ROWS, plane), struct(ROWS, half + quarter + PAD), struct(ROWS, plane)]
+        return [struct(ROWS, rows), struct(ROWS, plane + PAD_B), struct(ROWS, half + quarter + PAD), struct(ROWS, plane)]
 
     scratch_tile = pltpu.VMEM(tile.shape, F32)
     y, b, db, a, now, stiff, coef, force, w, cu, cw, ck, cf = call(

time: 41.7 us -> 40.7 us (0.976); the launches traced: 40.9 us -> 40.5 us
    ppermute x2, starting transfers between devices: 8.9 us -> 7.63 us  [exchange(): b = lax.ppermute(b, 'ax', pair_b)]
    ppermute x2, starting transfers between devices: 4.05 us -> 4.94 us  [exchange(): y = lax.ppermute(y, 'xs', [(0, 1), (1, 0)])]
where the time goes in v6:
time: 40.7 us; the launch traced here: 40.5 us
  starting transfers between devices  24.2 us (59%)
  waiting for transfers between devices  8.64 us (21%)
  Pallas kernels  6.87 us (17%)
  between operations  0.75 us (2%)
    ppermute x2, starting transfers between devices, exchange(): db = lax.ppermute(db, ('ax', 'xs'), across)  11.3 us
    ppermute x2, starting transfers between devices, exchange(): b = lax.ppermute(b, 'ax', pair_b)  7.63 us
    pallas_call x7, Pallas kernels, call(): pl.pallas_call(kernel, name=name, out_shape=outs, in_specs=[pl.BlockSpec(...  6.87 us
    ppermute x2, waiting for transfers between devices, exchange(): db = lax.ppermute(db, ('ax', 'xs'), across)  6.22 us
    ppermute x2, starting transfers between devices, exchange(): y = lax.ppermute(y, 'xs', [(0, 1), (1, 0)])  4.94 us
    ppermute x2, waiting for transfers between devices, exchange(): ya = lax.ppermute(line, 'ax', pair_a)  2.4 us
  transfers between devices with their start and end apart: 10, of which 4 were waited for; matrix products, arithmetic and copies ran while one was open for 0% of the time, Pallas kernels for 3%

profile of v6, /device:TPU:128, one launch (start us, length us, event | category | flops | bytes accessed | tf_op | source)
XLA Modules:
  0.0 40.5 jit_solution(5915284098602187100)
XLA Ops:
  0.6 2.8 %restrict_and_first_step.1 = (f32[8,6912]{1,0:T(8,128)S(1)}, f32[8,13568]{1,0:T(8,128)S(1)}, f32[8,1280]{1,0:T(8,128)S(1)}, f32[8,13440]{1,0:T(8,128)S(1)}, f32[...) custom-call(s32[4]{0:T(128)} %mask_hbm.1, ...), custom_call_target="tpu_custom_call" | custom-call | tf_op jit(solution)/shard_map/restrict_and_first_step/pallas_call | solution.py:532
  3.5 3.1 %collective-permute-start = (f32[8,6912]{1,0:T(8,128)S(1)}, f32[8,6912]{1,0:T(8,128)S(1)}, u32[]{:S(2)}, u32[]{:S(2)}) collective-permute-start(f32[8,6912]{1,0:T(8,128)S(1)} %get-tuple-element.33), channel_id=1, source_target_pairs={{0,1},{1,0},{2,3},{3,2},{4,5},{5,4},{6,7},{7,6},{8,9},{9,8},{10,11... | collective-permute-start | bytes 663560 | tf_op jit(solution)/shard_map/ppermute | solution.py:560
  6.6 3.6 %collective-permute-start.1 = (f32[8,13568]{1,0:T(8,128)S(1)}, f32[8,13568]{1,0:T(8,128)S(1)}, u32[]{:S(2)}, u32[]{:S(2)}) collective-permute-start(f32[8,13568]{1,0:T(8,128)S(1)} %get-tuple-element.34), channel_id=1, source_target_pairs={{2,4},{4,2},{6,8},{8,6},{10,12},{12,10},{14,16},{16,14},{18,20},{2... | collective-permute-start | bytes 1302536 | tf_op jit(solution)/shard_map/ppermute | solution.py:561
  10.2 0.1 collective-permute-start.3
  10.3 5.2 %collective-permute-start.2 = (f32[8,1280]{1,0:T(8,128)S(1)}, f32[8,1280]{1,0:T(8,128)S(1)}, u32[]{:S(2)}, u32[]{:S(2)}) collective-permute-start(f32[8,1280]{1,0:T(8,128)S(1)} %get-tuple-element.35), channel_id=1, source_target_pairs={{2,5},{3,4},{4,3},{5,2},{6,9},{7,8},{8,7},{9,6},{10,13},{11,12},{1... | collective-permute-start | bytes 122888 | tf_op jit(solution)/shard_map/ppermute | solution.py:562
  15.5 0.0 collective-permute-done.y_ref.y
  15.6 0.1 collective-permute-start.4
  15.7 1.2 %collective-permute-done.4.ya = f32[8,1152]{1,0:T(8,128)S(1)} collective-permute-done((f32[8,1152]{1,0:T(8,128)S(1)}, f32[8,1152]{1,0:T(8,128)S(1)}, u32[]{:S(2)}, u32[]{:S(2)}) %collective-permute-start.4) | collective-permute-done | bytes 36896 | tf_op jit(solution)/shard_map/ppermute | solution.py:566
  16.9 0.7 %early_two_steps.1 = (f32[7,8,1536]{2,1,0:T(8,128)S(1)}, f32[3,4,8,1536]{3,2,1,0:T(8,128)S(1)}, f32[3,4,8,1536]{3,2,1,0:T(8,128)S(1)}, f32[3,2,8,1536]{3,2,1,0:T(8,128)S(1)}, f32[3,8,1536]{2,1,0:T(8,128)S(1)}) custom-call(f32[8,6912]{1,0:T(8,128)S(1)} %collective-permute-done.y_ref.y, f32[8,13440]{1,0:T(8,128)S(1)} %collective-permute-done.3.a, ...), custom_call_target="tpu_custom_call" | custom-call | flops 1 | bytes 1024 | tf_op jit(solution)/shard_map/early_two_steps/pallas_call | solution.py:532
  17.6 3.5 %collective-permute-done.2.db = f32[8,1280]{1,0:T(8,128)S(1)} collective-permute-done((f32[8,1280]{1,0:T(8,128)S(1)}, f32[8,1280]{1,0:T(8,128)S(1)}, u32[]{:S(2)}, u32[]{:S(2)}) %collective-permute-start.2) | collective-permute-done | bytes 40992 | tf_op jit(solution)/shard_map/ppermute | solution.py:562
  21.1 0.0 collective-permute-done.1.b
  21.1 1.4 %late_two_steps.1 = (f32[8,6144]{1,0:T(8,128)S(1)}, f32[8,11648]{1,0:T(8,128)S(1)}, f32[8,1280]{1,0:T(8,128)S(1)}, f32[8,11520]{1,0:T(8,128)S(1)}, f32[3,8,1536]...) custom-call(f32[8,6912]{1,0:T(8,128)S(1)} %collective-permute-done.y, ...), custom_call_target="tpu_custom_call" | custom-call | tf_op jit(solution)/shard_map/late_two_steps/pallas_call | solution.py:532
  22.5 1.8 %collective-permute-start.5 = (f32[8,6144]{1,0:T(8,128)S(1)}, f32[8,6144]{1,0:T(8,128)S(1)}, u32[]{:S(2)}, u32[]{:S(2)}) collective-permute-start(f32[8,6144]{1,0:T(8,128)S(1)} %get-tuple-element.51), channel_id=1, source_target_pairs={{0,1},{1,0},{2,3},{3,2},{4,5},{5,4},{6,7},{7,6},{8,9},{9,8},{10,11... | collective-permute-start | bytes 589832 | tf_op jit(solution)/shard_map/ppermute | solution.py:560
  24.3 4.0 %collective-permute-start.6 = (f32[8,11648]{1,0:T(8,128)S(1)}, f32[8,11648]{1,0:T(8,128)S(1)}, u32[]{:S(2)}, u32[]{:S(2)}) collective-permute-start(f32[8,11648]{1,0:T(8,128)S(1)} %get-tuple-element.52), channel_id=1, source_target_pairs={{2,4},{4,2},{6,8},{8,6},{10,12},{12,10},{14,16},{16,14},{18,20},{2... | collective-permute-start | bytes 1118216 | tf_op jit(solution)/shard_map/ppermute | solution.py:561
  28.3 0.1 collective-permute-start.8
  28.4 6.1 %collective-permute-start.7 = (f32[8,1280]{1,0:T(8,128)S(1)}, f32[8,1280]{1,0:T(8,128)S(1)}, u32[]{:S(2)}, u32[]{:S(2)}) collective-permute-start(f32[8,1280]{1,0:T(8,128)S(1)} %get-tuple-element.53), channel_id=1, source_target_pairs={{2,5},{3,4},{4,3},{5,2},{6,9},{7,8},{8,7},{9,6},{10,13},{11,12},{1... | collective-permute-start | bytes 122888 | tf_op jit(solution)/shard_map/ppermute | solution.py:562
  34.5 0.0 collective-permute-done.5.y_ref.y
  34.5 0.1 collective-permute-start.9
  34.6 1.2 %collective-permute-done.9.ya = f32[8,1152]{1,0:T(8,128)S(1)} collective-permute-done((f32[8,1152]{1,0:T(8,128)S(1)}, f32[8,1152]{1,0:T(8,128)S(1)}, u32[]{:S(2)}, u32[]{:S(2)}) %collective-permute-start.9) | collective-permute-done | bytes 36896 | tf_op jit(solution)/shard_map/ppermute | solution.py:566
  35.8 0.0 collective-permute-done.8.a
  35.9 0.6 %early_last_steps.1 = (f32[3,4,8,1536]{3,2,1,0:T(8,128)S(1)}, f32[3,4,8,1536]{3,2,1,0:T(8,128)S(1)}, f32[3,2,8,1536]{3,2,1,0:T(8,128)S(1)}) custom-call(f32[8,6144]{1,0:T(8,128)S(1)} %collective-permute-done.5.y_ref.y, f32[8,11520]{1,0:T(8,128)S(1)} %collective-permute-done.8.a, f32[8,1152]{1,0:T(8,128)S(1)} %collective-permute-done.9.ya, ...), custom_call_target="tpu_custom_call" | custom-call | flops 1 | bytes 1024 | tf_op jit(solution)/shard_map/early_last_steps/pallas_call | solution.py:532
  36.4 2.7 %collective-permute-done.7.db = f32[8,1280]{1,0:T(8,128)S(1)} collective-permute-done((f32[8,1280]{1,0:T(8,128)S(1)}, f32[8,1280]{1,0:T(8,128)S(1)}, u32[]{:S(2)}, u32[]{:S(2)}) %collective-permute-start.7) | collective-permute-done | bytes 40992 | tf_op jit(solution)/shard_map/ppermute | solution.py:562
  39.2 0.0 collective-permute-done.6.b
  39.2 1.3 %late_last_steps.1 = (f32[3,4,8,1536]{3,2,1,0:T(8,128)}, f32[3,2,4,768]{3,2,1,0:T(4,128)}) custom-call(f32[8,6144]{1,0:T(8,128)S(1)} %collective-permute-done.5.y_ref.y, f32[8,11648]{1,0:T(8,128)S(1)} %collective-permute-done.6.b, f32[8,1280]{1,0:T(8,128)S(1)} %collective-permute-done.7.db, f32[8,11520]{1,0:T(8,128)S(1)} %collective-permute-done.8.a, ...), custom_call_target="tpu_custom_call" | custom-call | tf_op jit(solution)/shard_map/late_last_steps/pallas_call | solution.py:532
  (3 shorter events, 0.0 us)
Async XLA Ops:
  3.5 12.0 %collective-permute-start = (f32[8,6912]{1,0:T(8,128)S(1)}, f32[8,6912]{1,0:T(8,128)S(1)}, u32[]{:S(2)}, u32[]{:S(2)}) collective-permute-start(f32[8,6912]{1,0:T(8,128)S(1)} %get-tuple-element.33), channel_id=1, source_target_pairs={{0,1},{1,0},{2,3},{3,2},{4,5},{5,4},{6,7},{7,6},{8,9},{9,8},{10,11... | collective-permute-start | bytes 663560 | tf_op jit(solution)/shard_map/ppermute | solution.py:560
  6.6 14.5 %collective-permute-start.1 = (f32[8,13568]{1,0:T(8,128)S(1)}, f32[8,13568]{1,0:T(8,128)S(1)}, u32[]{:S(2)}, u32[]{:S(2)}) collective-permute-start(f32[8,13568]{1,0:T(8,128)S(1)} %get-tuple-element.34), channel_id=1, source_target_pairs={{2,4},{4,2},{6,8},{8,6},{10,12},{12,10},{14,16},{16,14},{18,20},{2... | collective-permute-start | bytes 1302536 | tf_op jit(solution)/shard_map/ppermute | solution.py:561
  10.2 6.6 %collective-permute-start.3 = (f32[8,13440]{1,0:T(8,128)S(1)}, f32[8,13440]{1,0:T(8,128)S(1)}, u32[]{:S(2)}, u32[]{:S(2)}) collective-permute-start(f32[8,13440]{1,0:T(8,128)S(1)} %get-tuple-element.36), channel_id=1, source_target_pairs={{0,2},{2,0},{4,6},{6,4},{8,10},{10,8},{12,14},{14,12},{16,18},{18,... | collective-permute-start | bytes 1290248 | tf_op jit(solution)/shard_map/ppermute | solution.py:563
  10.3 10.8 %collective-permute-start.2 = (f32[8,1280]{1,0:T(8,128)S(1)}, f32[8,1280]{1,0:T(8,128)S(1)}, u32[]{:S(2)}, u32[]{:S(2)}) collective-permute-start(f32[8,1280]{1,0:T(8,128)S(1)} %get-tuple-element.35), channel_id=1, source_target_pairs={{2,5},{3,4},{4,3},{5,2},{6,9},{7,8},{8,7},{9,6},{10,13},{11,12},{1... | collective-permute-start | bytes 122888 | tf_op jit(solution)/shard_map/ppermute | solution.py:562
  15.6 1.3 %collective-permute-start.4 = (f32[8,1152]{1,0:T(8,128)S(1)}, f32[8,1152]{1,0:T(8,128)S(1)}, u32[]{:S(2)}, u32[]{:S(2)}) collective-permute-start(f32[8,1152]{1,0:T(8,128)S(1)} %corner_lines.2), channel_id=1, source_target_pairs={{0,2},{2,0},{4,6},{6,4},{8,10},{10,8},{12,14},{14,12},{16,18},{18,... | collective-permute-start | bytes 110600 | tf_op jit(solution)/shard_map/ppermute | solution.py:566
  22.5 12.0 %collective-permute-start.5 = (f32[8,6144]{1,0:T(8,128)S(1)}, f32[8,6144]{1,0:T(8,128)S(1)}, u32[]{:S(2)}, u32[]{:S(2)}) collective-permute-start(f32[8,6144]{1,0:T(8,128)S(1)} %get-tuple-element.51), channel_id=1, source_target_pairs={{0,1},{1,0},{2,3},{3,2},{4,5},{5,4},{6,7},{7,6},{8,9},{9,8},{10,11... | collective-permute-start | bytes 589832 | tf_op jit(solution)/shard_map/ppermute | solution.py:560
  24.3 14.9 %collective-permute-start.6 = (f32[8,11648]{1,0:T(8,128)S(1)}, f32[8,11648]{1,0:T(8,128)S(1)}, u32[]{:S(2)}, u32[]{:S(2)}) collective-permute-start(f32[8,11648]{1,0:T(8,128)S(1)} %get-tuple-element.52), channel_id=1, source_target_pairs={{2,4},{4,2},{6,8},{8,6},{10,12},{12,10},{14,16},{16,14},{18,20},{2... | collective-permute-start | bytes 1118216 | tf_op jit(solution)/shard_map/ppermute | solution.py:561
  28.3 7.5 %collective-permute-start.8 = (f32[8,11520]{1,0:T(8,128)S(1)}, f32[8,11520]{1,0:T(8,128)S(1)}, u32[]{:S(2)}, u32[]{:S(2)}) collective-permute-start(f32[8,11520]{1,0:T(8,128)S(1)} %get-tuple-element.54), channel_id=1, source_target_pairs={{0,2},{2,0},{4,6},{6,4},{8,10},{10,8},{12,14},{14,12},{16,18},{18,... | collective-permute-start | bytes 1105928 | tf_op jit(solution)/shard_map/ppermute | solution.py:563
  28.4 10.8 %collective-permute-start.7 = (f32[8,1280]{1,0:T(8,128)S(1)}, f32[8,1280]{1,0:T(8,128)S(1)}, u32[]{:S(2)}, u32[]{:S(2)}) collective-permute-start(f32[8,1280]{1,0:T(8,128)S(1)} %get-tuple-element.53), channel_id=1, source_target_pairs={{2,5},{3,4},{4,3},{5,2},{6,9},{7,8},{8,7},{9,6},{10,13},{11,12},{1... | collective-permute-start | bytes 122888 | tf_op jit(solution)/shard_map/ppermute | solution.py:562
  34.5 1.3 %collective-permute-start.9 = (f32[8,1152]{1,0:T(8,128)S(1)}, f32[8,1152]{1,0:T(8,128)S(1)}, u32[]{:S(2)}, u32[]{:S(2)}) collective-permute-start(f32[8,1152]{1,0:T(8,128)S(1)} %corner_lines.3), channel_id=1, source_target_pairs={{0,2},{2,0},{4,6},{6,4},{8,10},{10,8},{12,14},{14,12},{16,18},{18,... | collective-permute-start | bytes 110600 | tf_op jit(solution)/shard_map/ppermute | solution.py:566

commit v7 on v6

--- a/solution.py
+++ b/solution.py
@@ -233,7 +233,7 @@
     for copy in copies[3 : 3 + PLANES]:
         copy.wait()
     fine_coefs(stiff, top_half, coef)
-    for copy in copies[3 + PLANES :]:
+    for copy in copies[3 + PLANES : 3 + 2 * PLANES]:
         copy.wait()
 
     def pooled(first, second):
@@ -244,6 +244,10 @@
     tiles = []
     for c in range(FIELDS):
         tiles.append(pooled(now[c, 0] + now[c, 1], now[c, 2] + now[c, 3]))
+        for z in range(PLANES):
+            w_out[c, z] = fine_free(lambda n: now[c, n], 0.0, z, coef, force[c, z])
+    for copy in copies[3 + 2 * PLANES :]:
+        copy.wait()
     for c in range(FIELDS):
         tiles.append(pooled(before[c, 0] + before[c, 1], before[c, 2] + before[c, 3]))
     tiles.append(pooled(stiff[0] + stiff[1], stiff[2] + stiff[3]))
@@ -283,7 +287,7 @@
 
     for c in range(FIELDS):
         for z in range(PLANES):
-            w_out[c, z] = fine_free(lambda n: now[c, n], before[c, z], z, coef, force[c, z])
+            w_out[c, z] = w_out[c, z] - before[c, z]
     pack(
         top_half,
         lambda f, z: now[f, z] if f < 3 else w_out[f - 3, z],

time: 40.7 us -> 40.6 us (level)
  no operation moved by 1% of the time
where the time goes in v7:
time: 40.6 us; the launch traced here: 40.4 us
  starting transfers between devices  24.2 us (60%)
  waiting for transfers between devices  8.64 us (21%)
  Pallas kernels  6.74 us (17%)
  between operations  0.75 us (2%)
    ppermute x2, starting transfers between devices, exchange(): db = lax.ppermute(db, ('ax', 'xs'), across)  11.3 us
    ppermute x2, starting transfers between devices, exchange(): b = lax.ppermute(b, 'ax', pair_b)  7.63 us
    pallas_call x7, Pallas kernels, call(): pl.pallas_call(kernel, name=name, out_shape=outs, in_specs=[pl.BlockSpec(...  6.74 us
    ppermute x2, waiting for transfers between devices, exchange(): db = lax.ppermute(db, ('ax', 'xs'), across)  6.22 us
    ppermute x2, starting transfers between devices, exchange(): y = lax.ppermute(y, 'xs', [(0, 1), (1, 0)])  4.95 us
    ppermute x2, waiting for transfers between devices, exchange(): ya = lax.ppermute(line, 'ax', pair_a)  2.4 us
  transfers between devices with their start and end apart: 10, of which 4 were waited for; matrix products, arithmetic and copies ran while one was open for 0% of the time, Pallas kernels for 3%

profile of v7, /device:TPU:128, one launch (start us, length us, event | category | flops | bytes accessed | tf_op | source)
XLA Modules:
  0.0 40.4 jit_solution(995233220563523832)
XLA Ops:
  0.6 2.7 %restrict_and_first_step.1 = (f32[8,6912]{1,0:T(8,128)S(1)}, f32[8,13568]{1,0:T(8,128)S(1)}, f32[8,1280]{1,0:T(8,128)S(1)}, f32[8,13440]{1,0:T(8,128)S(1)}, f32[...) custom-call(s32[4]{0:T(128)} %mask_hbm.1, ...), custom_call_target="tpu_custom_call" | custom-call | tf_op jit(solution)/shard_map/restrict_and_first_step/pallas_call | solution.py:536
  3.3 3.1 %collective-permute-start = (f32[8,6912]{1,0:T(8,128)S(1)}, f32[8,6912]{1,0:T(8,128)S(1)}, u32[]{:S(2)}, u32[]{:S(2)}) collective-permute-start(f32[8,6912]{1,0:T(8,128)S(1)} %get-tuple-element.33), channel_id=1, source_target_pairs={{0,1},{1,0},{2,3},{3,2},{4,5},{5,4},{6,7},{7,6},{8,9},{9,8},{10,11... | collective-permute-start | bytes 663560 | tf_op jit(solution)/shard_map/ppermute | solution.py:564
  6.5 3.6 %collective-permute-start.1 = (f32[8,13568]{1,0:T(8,128)S(1)}, f32[8,13568]{1,0:T(8,128)S(1)}, u32[]{:S(2)}, u32[]{:S(2)}) collective-permute-start(f32[8,13568]{1,0:T(8,128)S(1)} %get-tuple-element.34), channel_id=1, source_target_pairs={{2,4},{4,2},{6,8},{8,6},{10,12},{12,10},{14,16},{16,14},{18,20},{2... | collective-permute-start | bytes 1302536 | tf_op jit(solution)/shard_map/ppermute | solution.py:565
  10.1 0.1 collective-permute-start.3
  10.2 5.2 %collective-permute-start.2 = (f32[8,1280]{1,0:T(8,128)S(1)}, f32[8,1280]{1,0:T(8,128)S(1)}, u32[]{:S(2)}, u32[]{:S(2)}) collective-permute-start(f32[8,1280]{1,0:T(8,128)S(1)} %get-tuple-element.35), channel_id=1, source_target_pairs={{2,5},{3,4},{4,3},{5,2},{6,9},{7,8},{8,7},{9,6},{10,13},{11,12},{1... | collective-permute-start | bytes 122888 | tf_op jit(solution)/shard_map/ppermute | solution.py:566
  15.4 0.0 collective-permute-done.y_ref.y
  15.4 0.1 collective-permute-start.4
  15.5 1.2 %collective-permute-done.4.ya = f32[8,1152]{1,0:T(8,128)S(1)} collective-permute-done((f32[8,1152]{1,0:T(8,128)S(1)}, f32[8,1152]{1,0:T(8,128)S(1)}, u32[]{:S(2)}, u32[]{:S(2)}) %collective-permute-start.4) | collective-permute-done | bytes 36896 | tf_op jit(solution)/shard_map/ppermute | solution.py:570
  16.7 0.0 collective-permute-done.3.a
  16.7 0.7 %early_two_steps.1 = (f32[7,8,1536]{2,1,0:T(8,128)S(1)}, f32[3,4,8,1536]{3,2,1,0:T(8,128)S(1)}, f32[3,4,8,1536]{3,2,1,0:T(8,128)S(1)}, f32[3,2,8,1536]{3,2,1,0:T(8,128)S(1)}, f32[3,8,1536]{2,1,0:T(8,128)S(1)}) custom-call(f32[8,6912]{1,0:T(8,128)S(1)} %collective-permute-done.y_ref.y, f32[8,13440]{1,0:T(8,128)S(1)} %collective-permute-done.3.a, ...), custom_call_target="tpu_custom_call" | custom-call | flops 1 | bytes 1024 | tf_op jit(solution)/shard_map/early_two_steps/pallas_call | solution.py:536
  17.5 3.5 %collective-permute-done.2.db = f32[8,1280]{1,0:T(8,128)S(1)} collective-permute-done((f32[8,1280]{1,0:T(8,128)S(1)}, f32[8,1280]{1,0:T(8,128)S(1)}, u32[]{:S(2)}, u32[]{:S(2)}) %collective-permute-start.2) | collective-permute-done | bytes 40992 | tf_op jit(solution)/shard_map/ppermute | solution.py:566
  21.0 0.0 collective-permute-done.1.b
  21.0 1.4 %late_two_steps.1 = (f32[8,6144]{1,0:T(8,128)S(1)}, f32[8,11648]{1,0:T(8,128)S(1)}, f32[8,1280]{1,0:T(8,128)S(1)}, f32[8,11520]{1,0:T(8,128)S(1)}, f32[3,8,1536]...) custom-call(f32[8,6912]{1,0:T(8,128)S(1)} %collective-permute-done.y, ...), custom_call_target="tpu_custom_call" | custom-call | tf_op jit(solution)/shard_map/late_two_steps/pallas_call | solution.py:536
  22.3 1.8 %collective-permute-start.5 = (f32[8,6144]{1,0:T(8,128)S(1)}, f32[8,6144]{1,0:T(8,128)S(1)}, u32[]{:S(2)}, u32[]{:S(2)}) collective-permute-start(f32[8,6144]{1,0:T(8,128)S(1)} %get-tuple-element.51), channel_id=1, source_target_pairs={{0,1},{1,0},{2,3},{3,2},{4,5},{5,4},{6,7},{7,6},{8,9},{9,8},{10,11... | collective-permute-start | bytes 589832 | tf_op jit(solution)/shard_map/ppermute | solution.py:564
  24.2 4.0 %collective-permute-start.6 = (f32[8,11648]{1,0:T(8,128)S(1)}, f32[8,11648]{1,0:T(8,128)S(1)}, u32[]{:S(2)}, u32[]{:S(2)}) collective-permute-start(f32[8,11648]{1,0:T(8,128)S(1)} %get-tuple-element.52), channel_id=1, source_target_pairs={{2,4},{4,2},{6,8},{8,6},{10,12},{12,10},{14,16},{16,14},{18,20},{2... | collective-permute-start | bytes 1118216 | tf_op jit(solution)/shard_map/ppermute | solution.py:565
  28.2 0.1 collective-permute-start.8
  28.3 6.1 %collective-permute-start.7 = (f32[8,1280]{1,0:T(8,128)S(1)}, f32[8,1280]{1,0:T(8,128)S(1)}, u32[]{:S(2)}, u32[]{:S(2)}) collective-permute-start(f32[8,1280]{1,0:T(8,128)S(1)} %get-tuple-element.53), channel_id=1, source_target_pairs={{2,5},{3,4},{4,3},{5,2},{6,9},{7,8},{8,7},{9,6},{10,13},{11,12},{1... | collective-permute-start | bytes 122888 | tf_op jit(solution)/shard_map/ppermute | solution.py:566
  34.4 0.0 collective-permute-done.5.y_ref.y
  34.4 0.1 collective-permute-start.9
  34.5 1.2 %collective-permute-done.9.ya = f32[8,1152]{1,0:T(8,128)S(1)} collective-permute-done((f32[8,1152]{1,0:T(8,128)S(1)}, f32[8,1152]{1,0:T(8,128)S(1)}, u32[]{:S(2)}, u32[]{:S(2)}) %collective-permute-start.9) | collective-permute-done | bytes 36896 | tf_op jit(solution)/shard_map/ppermute | solution.py:570
  35.7 0.0 collective-permute-done.8.a
  35.7 0.6 %early_last_steps.1 = (f32[3,4,8,1536]{3,2,1,0:T(8,128)S(1)}, f32[3,4,8,1536]{3,2,1,0:T(8,128)S(1)}, f32[3,2,8,1536]{3,2,1,0:T(8,128)S(1)}) custom-call(f32[8,6144]{1,0:T(8,128)S(1)} %collective-permute-done.5.y_ref.y, f32[8,11520]{1,0:T(8,128)S(1)} %collective-permute-done.8.a, f32[8,1152]{1,0:T(8,128)S(1)} %collective-permute-done.9.ya, ...), custom_call_target="tpu_custom_call" | custom-call | flops 1 | bytes 1024 | tf_op jit(solution)/shard_map/early_last_steps/pallas_call | solution.py:536
  36.3 2.7 %collective-permute-done.7.db = f32[8,1280]{1,0:T(8,128)S(1)} collective-permute-done((f32[8,1280]{1,0:T(8,128)S(1)}, f32[8,1280]{1,0:T(8,128)S(1)}, u32[]{:S(2)}, u32[]{:S(2)}) %collective-permute-start.7) | collective-permute-done | bytes 40992 | tf_op jit(solution)/shard_map/ppermute | solution.py:566
  39.0 1.3 %late_last_steps.1 = (f32[3,4,8,1536]{3,2,1,0:T(8,128)}, f32[3,2,4,768]{3,2,1,0:T(4,128)}) custom-call(f32[8,6144]{1,0:T(8,128)S(1)} %collective-permute-done.5.y_ref.y, f32[8,11648]{1,0:T(8,128)S(1)} %collective-permute-done.6.b, f32[8,1280]{1,0:T(8,128)S(1)} %collective-permute-done.7.db, f32[8,11520]{1,0:T(8,128)S(1)} %collective-permute-done.8.a, ...), custom_call_target="tpu_custom_call" | custom-call | tf_op jit(solution)/shard_map/late_last_steps/pallas_call | solution.py:536
  (3 shorter events, 0.0 us)
Async XLA Ops:
  3.3 12.0 %collective-permute-start = (f32[8,6912]{1,0:T(8,128)S(1)}, f32[8,6912]{1,0:T(8,128)S(1)}, u32[]{:S(2)}, u32[]{:S(2)}) collective-permute-start(f32[8,6912]{1,0:T(8,128)S(1)} %get-tuple-element.33), channel_id=1, source_target_pairs={{0,1},{1,0},{2,3},{3,2},{4,5},{5,4},{6,7},{7,6},{8,9},{9,8},{10,11... | collective-permute-start | bytes 663560 | tf_op jit(solution)/shard_map/ppermute | solution.py:564
  6.5 14.5 %collective-permute-start.1 = (f32[8,13568]{1,0:T(8,128)S(1)}, f32[8,13568]{1,0:T(8,128)S(1)}, u32[]{:S(2)}, u32[]{:S(2)}) collective-permute-start(f32[8,13568]{1,0:T(8,128)S(1)} %get-tuple-element.34), channel_id=1, source_target_pairs={{2,4},{4,2},{6,8},{8,6},{10,12},{12,10},{14,16},{16,14},{18,20},{2... | collective-permute-start | bytes 1302536 | tf_op jit(solution)/shard_map/ppermute | solution.py:565
  10.1 6.6 %collective-permute-start.3 = (f32[8,13440]{1,0:T(8,128)S(1)}, f32[8,13440]{1,0:T(8,128)S(1)}, u32[]{:S(2)}, u32[]{:S(2)}) collective-permute-start(f32[8,13440]{1,0:T(8,128)S(1)} %get-tuple-element.36), channel_id=1, source_target_pairs={{0,2},{2,0},{4,6},{6,4},{8,10},{10,8},{12,14},{14,12},{16,18},{18,... | collective-permute-start | bytes 1290248 | tf_op jit(solution)/shard_map/ppermute | solution.py:567
  10.2 10.8 %collective-permute-start.2 = (f32[8,1280]{1,0:T(8,128)S(1)}, f32[8,1280]{1,0:T(8,128)S(1)}, u32[]{:S(2)}, u32[]{:S(2)}) collective-permute-start(f32[8,1280]{1,0:T(8,128)S(1)} %get-tuple-element.35), channel_id=1, source_target_pairs={{2,5},{3,4},{4,3},{5,2},{6,9},{7,8},{8,7},{9,6},{10,13},{11,12},{1... | collective-permute-start | bytes 122888 | tf_op jit(solution)/shard_map/ppermute | solution.py:566
  15.4 1.3 %collective-permute-start.4 = (f32[8,1152]{1,0:T(8,128)S(1)}, f32[8,1152]{1,0:T(8,128)S(1)}, u32[]{:S(2)}, u32[]{:S(2)}) collective-permute-start(f32[8,1152]{1,0:T(8,128)S(1)} %corner_lines.2), channel_id=1, source_target_pairs={{0,2},{2,0},{4,6},{6,4},{8,10},{10,8},{12,14},{14,12},{16,18},{18,... | collective-permute-start | bytes 110600 | tf_op jit(solution)/shard_map/ppermute | solution.py:570
  22.3 12.0 %collective-permute-start.5 = (f32[8,6144]{1,0:T(8,128)S(1)}, f32[8,6144]{1,0:T(8,128)S(1)}, u32[]{:S(2)}, u32[]{:S(2)}) collective-permute-start(f32[8,6144]{1,0:T(8,128)S(1)} %get-tuple-element.51), channel_id=1, source_target_pairs={{0,1},{1,0},{2,3},{3,2},{4,5},{5,4},{6,7},{7,6},{8,9},{9,8},{10,11... | collective-permute-start | bytes 589832 | tf_op jit(solution)/shard_map/ppermute | solution.py:564
  24.2 14.9 %collective-permute-start.6 = (f32[8,11648]{1,0:T(8,128)S(1)}, f32[8,11648]{1,0:T(8,128)S(1)}, u32[]{:S(2)}, u32[]{:S(2)}) collective-permute-start(f32[8,11648]{1,0:T(8,128)S(1)} %get-tuple-element.52), channel_id=1, source_target_pairs={{2,4},{4,2},{6,8},{8,6},{10,12},{12,10},{14,16},{16,14},{18,20},{2... | collective-permute-start | bytes 1118216 | tf_op jit(solution)/shard_map/ppermute | solution.py:565
  28.2 7.5 %collective-permute-start.8 = (f32[8,11520]{1,0:T(8,128)S(1)}, f32[8,11520]{1,0:T(8,128)S(1)}, u32[]{:S(2)}, u32[]{:S(2)}) collective-permute-start(f32[8,11520]{1,0:T(8,128)S(1)} %get-tuple-element.54), channel_id=1, source_target_pairs={{0,2},{2,0},{4,6},{6,4},{8,10},{10,8},{12,14},{14,12},{16,18},{18,... | collective-permute-start | bytes 1105928 | tf_op jit(solution)/shard_map/ppermute | solution.py:567
  28.3 10.8 %collective-permute-start.7 = (f32[8,1280]{1,0:T(8,128)S(1)}, f32[8,1280]{1,0:T(8,128)S(1)}, u32[]{:S(2)}, u32[]{:S(2)}) collective-permute-start(f32[8,1280]{1,0:T(8,128)S(1)} %get-tuple-element.53), channel_id=1, source_target_pairs={{2,5},{3,4},{4,3},{5,2},{6,9},{7,8},{8,7},{9,6},{10,13},{11,12},{1... | collective-permute-start | bytes 122888 | tf_op jit(solution)/shard_map/ppermute | solution.py:566
  34.4 1.3 %collective-permute-start.9 = (f32[8,1152]{1,0:T(8,128)S(1)}, f32[8,1152]{1,0:T(8,128)S(1)}, u32[]{:S(2)}, u32[]{:S(2)}) collective-permute-start(f32[8,1152]{1,0:T(8,128)S(1)} %corner_lines.3), channel_id=1, source_target_pairs={{0,2},{2,0},{4,6},{6,4},{8,10},{10,8},{12,14},{14,12},{16,18},{18,... | collective-permute-start | bytes 110600 | tf_op jit(solution)/shard_map/ppermute | solution.py:570

commit v8 on v7

--- a/solution.py
+++ b/solution.py
@@ -125,6 +125,8 @@
 
 def coarse_row(q, width, base):
     half = width // 2
+    if q >= 8 and base == 3 * width:
+        return [(2 * (q - 8) + h, base + half, half // 2) for h in range(2)]
     return [(q % 8, base + (q // 8) * half, half)]
 
 
@@ -189,7 +191,6 @@
     if with_k:
         y_buf[6:8, base + half : base + 2 * half] = jnp.zeros((2, half), F32)
     else:
-        y_buf[4:8, base + half : base + 2 * half] = jnp.zeros((4, half), F32)
         db_buf[6:8, :] = jnp.zeros((2, db_buf.shape[1]), F32)
 
     at = fields * width
@@ -586,7 +587,7 @@
 
     def buffers(fields, with_k):
         plane = fields * width + 3 * half + (quarter if with_k else 0)
-        rows = 3 * width + (3 * half if with_k else 2 * half)
+        rows = 3 * width + (3 * half if with_k else half + quarter)
         return [struct(ROWS, rows), struct(ROWS, plane + PAD_B), struct(ROWS, half + quarter + PAD), struct(ROWS, plane)]
 
     scratch_tile = pltpu.VMEM(tile.shape, F32)

time: 40.6 us -> 40.5 us (level)
  no operation moved by 1% of the time
where the time goes in v8:
time: 40.5 us; the launch traced here: 40.3 us
  starting transfers between devices  24.2 us (60%)
  waiting for transfers between devices  8.66 us (21%)
  Pallas kernels  6.67 us (16%)
  between operations  0.75 us (2%)
    ppermute x2, starting transfers between devices, exchange(): db = lax.ppermute(db, ('ax', 'xs'), across)  11.3 us
    ppermute x2, starting transfers between devices, exchange(): b = lax.ppermute(b, 'ax', pair_b)  7.63 us
    pallas_call x7, Pallas kernels, call(): pl.pallas_call(kernel, name=name, out_shape=outs, in_specs=[pl.BlockSpec(...  6.67 us
    ppermute x2, waiting for transfers between devices, exchange(): db = lax.ppermute(db, ('ax', 'xs'), across)  6.25 us
    ppermute x2, starting transfers between devices, exchange(): y = lax.ppermute(y, 'xs', [(0, 1), (1, 0)])  4.94 us
    ppermute x2, waiting for transfers between devices, exchange(): ya = lax.ppermute(line, 'ax', pair_a)  2.4 us
  transfers between devices with their start and end apart: 10, of which 4 were waited for; matrix products, arithmetic and copies ran while one was open for 0% of the time, Pallas kernels for 3%

profile of v8, /device:TPU:128, one launch (start us, length us, event | category | flops | bytes accessed | tf_op | source)
XLA Modules:
  0.0 40.3 jit_solution(9704686664014066877)
XLA Ops:
  0.6 2.7 %restrict_and_first_step.1 = (f32[8,6912]{1,0:T(8,128)S(1)}, f32[8,13568]{1,0:T(8,128)S(1)}, f32[8,1280]{1,0:T(8,128)S(1)}, f32[8,13440]{1,0:T(8,128)S(1)}, f32[...) custom-call(s32[4]{0:T(128)} %mask_hbm.1, ...), custom_call_target="tpu_custom_call" | custom-call | tf_op jit(solution)/shard_map/restrict_and_first_step/pallas_call | solution.py:537
  3.4 3.1 %collective-permute-start = (f32[8,6912]{1,0:T(8,128)S(1)}, f32[8,6912]{1,0:T(8,128)S(1)}, u32[]{:S(2)}, u32[]{:S(2)}) collective-permute-start(f32[8,6912]{1,0:T(8,128)S(1)} %get-tuple-element.33), channel_id=1, source_target_pairs={{0,1},{1,0},{2,3},{3,2},{4,5},{5,4},{6,7},{7,6},{8,9},{9,8},{10,11... | collective-permute-start | bytes 663560 | tf_op jit(solution)/shard_map/ppermute | solution.py:565
  6.5 3.6 %collective-permute-start.1 = (f32[8,13568]{1,0:T(8,128)S(1)}, f32[8,13568]{1,0:T(8,128)S(1)}, u32[]{:S(2)}, u32[]{:S(2)}) collective-permute-start(f32[8,13568]{1,0:T(8,128)S(1)} %get-tuple-element.34), channel_id=1, source_target_pairs={{2,4},{4,2},{6,8},{8,6},{10,12},{12,10},{14,16},{16,14},{18,20},{2... | collective-permute-start | bytes 1302536 | tf_op jit(solution)/shard_map/ppermute | solution.py:566
  10.1 0.1 collective-permute-start.3
  10.2 5.2 %collective-permute-start.2 = (f32[8,1280]{1,0:T(8,128)S(1)}, f32[8,1280]{1,0:T(8,128)S(1)}, u32[]{:S(2)}, u32[]{:S(2)}) collective-permute-start(f32[8,1280]{1,0:T(8,128)S(1)} %get-tuple-element.35), channel_id=1, source_target_pairs={{2,5},{3,4},{4,3},{5,2},{6,9},{7,8},{8,7},{9,6},{10,13},{11,12},{1... | collective-permute-start | bytes 122888 | tf_op jit(solution)/shard_map/ppermute | solution.py:567
  15.4 0.0 collective-permute-done.y_ref.y
  15.4 0.1 collective-permute-start.4
  15.5 1.2 %collective-permute-done.4.ya = f32[8,1152]{1,0:T(8,128)S(1)} collective-permute-done((f32[8,1152]{1,0:T(8,128)S(1)}, f32[8,1152]{1,0:T(8,128)S(1)}, u32[]{:S(2)}, u32[]{:S(2)}) %collective-permute-start.4) | collective-permute-done | bytes 36896 | tf_op jit(solution)/shard_map/ppermute | solution.py:571
  16.7 0.0 collective-permute-done.3.a
  16.7 0.7 %early_two_steps.1 = (f32[7,8,1536]{2,1,0:T(8,128)S(1)}, f32[3,4,8,1536]{3,2,1,0:T(8,128)S(1)}, f32[3,4,8,1536]{3,2,1,0:T(8,128)S(1)}, f32[3,2,8,1536]{3,2,1,0:T(8,128)S(1)}, f32[3,8,1536]{2,1,0:T(8,128)S(1)}) custom-call(f32[8,6912]{1,0:T(8,128)S(1)} %collective-permute-done.y_ref.y, f32[8,13440]{1,0:T(8,128)S(1)} %collective-permute-done.3.a, ...), custom_call_target="tpu_custom_call" | custom-call | flops 1 | bytes 1024 | tf_op jit(solution)/shard_map/early_two_steps/pallas_call | solution.py:537
  17.5 3.5 %collective-permute-done.2.db = f32[8,1280]{1,0:T(8,128)S(1)} collective-permute-done((f32[8,1280]{1,0:T(8,128)S(1)}, f32[8,1280]{1,0:T(8,128)S(1)}, u32[]{:S(2)}, u32[]{:S(2)}) %collective-permute-start.2) | collective-permute-done | bytes 40992 | tf_op jit(solution)/shard_map/ppermute | solution.py:567
  21.0 0.0 collective-permute-done.1.b
  21.0 1.4 %late_two_steps.1 = (f32[8,5760]{1,0:T(8,128)S(1)}, f32[8,11648]{1,0:T(8,128)S(1)}, f32[8,1280]{1,0:T(8,128)S(1)}, f32[8,11520]{1,0:T(8,128)S(1)}, f32[3,8,1536]...) custom-call(f32[8,6912]{1,0:T(8,128)S(1)} %collective-permute-done.y, ...), custom_call_target="tpu_custom_call" | custom-call | tf_op jit(solution)/shard_map/late_two_steps/pallas_call | solution.py:537
  22.3 1.8 %collective-permute-start.5 = (f32[8,5760]{1,0:T(8,128)S(1)}, f32[8,5760]{1,0:T(8,128)S(1)}, u32[]{:S(2)}, u32[]{:S(2)}) collective-permute-start(f32[8,5760]{1,0:T(8,128)S(1)} %get-tuple-element.51), channel_id=1, source_target_pairs={{0,1},{1,0},{2,3},{3,2},{4,5},{5,4},{6,7},{7,6},{8,9},{9,8},{10,11... | collective-permute-start | bytes 552968 | tf_op jit(solution)/shard_map/ppermute | solution.py:565
  24.2 4.0 %collective-permute-start.6 = (f32[8,11648]{1,0:T(8,128)S(1)}, f32[8,11648]{1,0:T(8,128)S(1)}, u32[]{:S(2)}, u32[]{:S(2)}) collective-permute-start(f32[8,11648]{1,0:T(8,128)S(1)} %get-tuple-element.52), channel_id=1, source_target_pairs={{2,4},{4,2},{6,8},{8,6},{10,12},{12,10},{14,16},{16,14},{18,20},{2... | collective-permute-start | bytes 1118216 | tf_op jit(solution)/shard_map/ppermute | solution.py:566
  28.2 0.1 collective-permute-start.8
  28.3 6.1 %collective-permute-start.7 = (f32[8,1280]{1,0:T(8,128)S(1)}, f32[8,1280]{1,0:T(8,128)S(1)}, u32[]{:S(2)}, u32[]{:S(2)}) collective-permute-start(f32[8,1280]{1,0:T(8,128)S(1)} %get-tuple-element.53), channel_id=1, source_target_pairs={{2,5},{3,4},{4,3},{5,2},{6,9},{7,8},{8,7},{9,6},{10,13},{11,12},{1... | collective-permute-start | bytes 122888 | tf_op jit(solution)/shard_map/ppermute | solution.py:567
  34.4 0.1 collective-permute-start.9
  34.5 1.2 %collective-permute-done.9.ya = f32[8,1152]{1,0:T(8,128)S(1)} collective-permute-done((f32[8,1152]{1,0:T(8,128)S(1)}, f32[8,1152]{1,0:T(8,128)S(1)}, u32[]{:S(2)}, u32[]{:S(2)}) %collective-permute-start.9) | collective-permute-done | bytes 36896 | tf_op jit(solution)/shard_map/ppermute | solution.py:571
  35.7 0.0 collective-permute-done.8.a
  35.7 0.6 %early_last_steps.1 = (f32[3,4,8,1536]{3,2,1,0:T(8,128)S(1)}, f32[3,4,8,1536]{3,2,1,0:T(8,128)S(1)}, f32[3,2,8,1536]{3,2,1,0:T(8,128)S(1)}) custom-call(f32[8,5760]{1,0:T(8,128)S(1)} %collective-permute-done.5.y_ref.y, f32[8,11520]{1,0:T(8,128)S(1)} %collective-permute-done.8.a, f32[8,1152]{1,0:T(8,128)S(1)} %collective-permute-done.9.ya, ...), custom_call_target="tpu_custom_call" | custom-call | flops 1 | bytes 1024 | tf_op jit(solution)/shard_map/early_last_steps/pallas_call | solution.py:537
  36.3 2.7 %collective-permute-done.7.db = f32[8,1280]{1,0:T(8,128)S(1)} collective-permute-done((f32[8,1280]{1,0:T(8,128)S(1)}, f32[8,1280]{1,0:T(8,128)S(1)}, u32[]{:S(2)}, u32[]{:S(2)}) %collective-permute-start.7) | collective-permute-done | bytes 40992 | tf_op jit(solution)/shard_map/ppermute | solution.py:567
  39.0 0.0 collective-permute-done.6.b
  39.0 1.3 %late_last_steps.1 = (f32[3,4,8,1536]{3,2,1,0:T(8,128)}, f32[3,2,4,768]{3,2,1,0:T(4,128)}) custom-call(f32[8,5760]{1,0:T(8,128)S(1)} %collective-permute-done.5.y_ref.y, f32[8,11648]{1,0:T(8,128)S(1)} %collective-permute-done.6.b, f32[8,1280]{1,0:T(8,128)S(1)} %collective-permute-done.7.db, f32[8,11520]{1,0:T(8,128)S(1)} %collective-permute-done.8.a, ...), custom_call_target="tpu_custom_call" | custom-call | tf_op jit(solution)/shard_map/late_last_steps/pallas_call | solution.py:537
  (3 shorter events, 0.0 us)
Async XLA Ops:
  3.4 12.0 %collective-permute-start = (f32[8,6912]{1,0:T(8,128)S(1)}, f32[8,6912]{1,0:T(8,128)S(1)}, u32[]{:S(2)}, u32[]{:S(2)}) collective-permute-start(f32[8,6912]{1,0:T(8,128)S(1)} %get-tuple-element.33), channel_id=1, source_target_pairs={{0,1},{1,0},{2,3},{3,2},{4,5},{5,4},{6,7},{7,6},{8,9},{9,8},{10,11... | collective-permute-start | bytes 663560 | tf_op jit(solution)/shard_map/ppermute | solution.py:565
  6.5 14.5 %collective-permute-start.1 = (f32[8,13568]{1,0:T(8,128)S(1)}, f32[8,13568]{1,0:T(8,128)S(1)}, u32[]{:S(2)}, u32[]{:S(2)}) collective-permute-start(f32[8,13568]{1,0:T(8,128)S(1)} %get-tuple-element.34), channel_id=1, source_target_pairs={{2,4},{4,2},{6,8},{8,6},{10,12},{12,10},{14,16},{16,14},{18,20},{2... | collective-permute-start | bytes 1302536 | tf_op jit(solution)/shard_map/ppermute | solution.py:566
  10.1 6.6 %collective-permute-start.3 = (f32[8,13440]{1,0:T(8,128)S(1)}, f32[8,13440]{1,0:T(8,128)S(1)}, u32[]{:S(2)}, u32[]{:S(2)}) collective-permute-start(f32[8,13440]{1,0:T(8,128)S(1)} %get-tuple-element.36), channel_id=1, source_target_pairs={{0,2},{2,0},{4,6},{6,4},{8,10},{10,8},{12,14},{14,12},{16,18},{18,... | collective-permute-start | bytes 1290248 | tf_op jit(solution)/shard_map/ppermute | solution.py:568
  10.2 10.8 %collective-permute-start.2 = (f32[8,1280]{1,0:T(8,128)S(1)}, f32[8,1280]{1,0:T(8,128)S(1)}, u32[]{:S(2)}, u32[]{:S(2)}) collective-permute-start(f32[8,1280]{1,0:T(8,128)S(1)} %get-tuple-element.35), channel_id=1, source_target_pairs={{2,5},{3,4},{4,3},{5,2},{6,9},{7,8},{8,7},{9,6},{10,13},{11,12},{1... | collective-permute-start | bytes 122888 | tf_op jit(solution)/shard_map/ppermute | solution.py:567
  15.4 1.3 %collective-permute-start.4 = (f32[8,1152]{1,0:T(8,128)S(1)}, f32[8,1152]{1,0:T(8,128)S(1)}, u32[]{:S(2)}, u32[]{:S(2)}) collective-permute-start(f32[8,1152]{1,0:T(8,128)S(1)} %corner_lines.2), channel_id=1, source_target_pairs={{0,2},{2,0},{4,6},{6,4},{8,10},{10,8},{12,14},{14,12},{16,18},{18,... | collective-permute-start | bytes 110600 | tf_op jit(solution)/shard_map/ppermute | solution.py:571
  22.3 12.0 %collective-permute-start.5 = (f32[8,5760]{1,0:T(8,128)S(1)}, f32[8,5760]{1,0:T(8,128)S(1)}, u32[]{:S(2)}, u32[]{:S(2)}) collective-permute-start(f32[8,5760]{1,0:T(8,128)S(1)} %get-tuple-element.51), channel_id=1, source_target_pairs={{0,1},{1,0},{2,3},{3,2},{4,5},{5,4},{6,7},{7,6},{8,9},{9,8},{10,11... | collective-permute-start | bytes 552968 | tf_op jit(solution)/shard_map/ppermute | solution.py:565
  24.2 14.9 %collective-permute-start.6 = (f32[8,11648]{1,0:T(8,128)S(1)}, f32[8,11648]{1,0:T(8,128)S(1)}, u32[]{:S(2)}, u32[]{:S(2)}) collective-permute-start(f32[8,11648]{1,0:T(8,128)S(1)} %get-tuple-element.52), channel_id=1, source_target_pairs={{2,4},{4,2},{6,8},{8,6},{10,12},{12,10},{14,16},{16,14},{18,20},{2... | collective-permute-start | bytes 1118216 | tf_op jit(solution)/shard_map/ppermute | solution.py:566
  28.2 7.5 %collective-permute-start.8 = (f32[8,11520]{1,0:T(8,128)S(1)}, f32[8,11520]{1,0:T(8,128)S(1)}, u32[]{:S(2)}, u32[]{:S(2)}) collective-permute-start(f32[8,11520]{1,0:T(8,128)S(1)} %get-tuple-element.54), channel_id=1, source_target_pairs={{0,2},{2,0},{4,6},{6,4},{8,10},{10,8},{12,14},{14,12},{16,18},{18,... | collective-permute-start | bytes 1105928 | tf_op jit(solution)/shard_map/ppermute | solution.py:568
  28.3 10.8 %collective-permute-start.7 = (f32[8,1280]{1,0:T(8,128)S(1)}, f32[8,1280]{1,0:T(8,128)S(1)}, u32[]{:S(2)}, u32[]{:S(2)}) collective-permute-start(f32[8,1280]{1,0:T(8,128)S(1)} %get-tuple-element.53), channel_id=1, source_target_pairs={{2,5},{3,4},{4,3},{5,2},{6,9},{7,8},{8,7},{9,6},{10,13},{11,12},{1... | collective-permute-start | bytes 122888 | tf_op jit(solution)/shard_map/ppermute | solution.py:567
  34.4 1.3 %collective-permute-start.9 = (f32[8,1152]{1,0:T(8,128)S(1)}, f32[8,1152]{1,0:T(8,128)S(1)}, u32[]{:S(2)}, u32[]{:S(2)}) collective-permute-start(f32[8,1152]{1,0:T(8,128)S(1)} %corner_lines.3), channel_id=1, source_target_pairs={{0,2},{2,0},{4,6},{6,4},{8,10},{10,8},{12,14},{14,12},{16,18},{18,... | collective-permute-start | bytes 110600 | tf_op jit(solution)/shard_map/ppermute | solution.py:571
